TPU v7x, 32 devices: a whole 2x2x4 slice. The times are simulated.
32 devices in a mesh: dom: 8 (over z, core), mem: 4 (over y, x).
Axes of the slice: x: 2, y: 2, z: 4, core: 2. Of those that a mesh axis runs over, the one named last changes fastest.
Arguments:
- coarse_latents: bfloat16 [4, 4096, 512], P('mem', 'dom'), may hold values from -6 to 6
- send_rows: int32 [8, 8, 128], P('dom'), may hold values from 0 to 511
- up_index: int32 [3, 16384], P(None, 'dom'), may hold values from 0 to 1023
- up_weight: float32 [3, 16384], P(None, 'dom'), may hold values from 0.2 to 1
- neighbors: int32 [6, 16384], P(None, 'dom'), may hold values from 0 to 2303, as said below
- live_counts: int32 [8], P('dom'), may hold values from 1 to 2048, 12288 in all
- area: float32 [16384], P('dom'), may hold values from 0.25 to 4.5
- fine_skip: bfloat16 [16384, 512], P('dom'), may hold values from -6 to 6
- targets: bfloat16 [83, 16384], P(None, 'dom'), may hold values from -6 to 6
- kernel_width: float32 [83], replicated, may hold values from 0.5 to 2
- w_in: bfloat16 [1024, 512], replicated, may hold values from -0.1875 to 0.1875
- w_out: bfloat16 [512, 512], replicated, may hold values from -0.25 to 0.25
- ln_gain: float32 [512], replicated, may hold values from 0.1 to 1.9
- w_head: bfloat16 [512, 83], replicated, may hold values from -0.25 to 0.25
Outputs:
- grad_latent: bfloat16 [4, 16384, 512], P('mem', 'dom')
- grad_head: float32 [8, 512, 83], P('dom')
Inputs may be any that keep to these rules, and one draw needn't show every extreme that they name: neighbors[k, p] = 128 + (p % 2048) + e with -128 <= e <= 128.
All inputs are finite; a program needn't handle non-finite values. No bound on the sum of `live_counts` on one device may be relied on, other than what follows from the above.
Results may differ from a plain program's by a relative error of at most 0.015.
The roundings to bfloat16 on the way count: a program that leaves them out, or rounds other values in their place, can miss the bound.
Values may be sent and summed in bfloat16 or wider, within the bound.
No kernel may reach another device: no remote copies, remote signals or barrier semaphores. Data moves between devices by JAX's collectives and lax.ppermute only.
A program may use at most 128 MiB of HBM per device.

v0:
```python
import math

import jax
import jax.numpy as jnp
from jax import lax
from jax.sharding import PartitionSpec as P

K_NB = 6
RIM = 128


def extended_2(value, sides, width):
    for axis, dim in sides:
        count, length = (lax.axis_size(axis), value.shape[dim])
        up = [(i, (i + 1) % count) for i in range(count - 1)]
        down = [(j, i) for i, j in up]
        last = lax.slice_in_dim(value, length - width, length, axis=dim)
        first = lax.slice_in_dim(value, 0, width, axis=dim)
        before = lax.ppermute(last, axis, up)
        after = lax.ppermute(first, axis, down)
        value = jnp.concatenate([before, value, after], axis=dim)
    return value


def slope(diff, inv_sq):
    return -(diff * inv_sq) * jnp.exp(-0.5 * diff * diff * inv_sq)


def shards(
    coarse_latents,
    send_rows,
    up_index,
    up_weight,
    neighbors,
    live_counts,
    area,
    fine_skip,
    targets,
    kernel_width,
    w_in,
    w_out,
    ln_gain,
    w_head,
):
    dom_count = lax.axis_size("dom")
    mem_count = lax.axis_size("mem")
    fine_rows = fine_skip.shape[0]
    width = fine_skip.shape[1]
    outgoing = coarse_latents[0][send_rows[0]]
    incoming = lax.all_to_all(outgoing, "dom", split_axis=0, concat_axis=0, tiled=True)
    table = incoming.reshape(dom_count * incoming.shape[1], width)
    unpooled = jnp.zeros((fine_rows, width), jnp.float32)
    for k in range(up_index.shape[0]):
        unpooled = unpooled + up_weight[k][:, None] * table[up_index[k]].astype(jnp.float32)
    latent = (fine_skip.astype(jnp.float32) + unpooled).astype(jnp.bfloat16)
    extended = extended_2(latent, (("dom", 0),), RIM)
    total = jnp.zeros((fine_rows, width), jnp.float32)
    for k in range(neighbors.shape[0]):
        total = total + extended[neighbors[k]].astype(jnp.float32)
    agg = (total / K_NB).astype(jnp.bfloat16)
    pre = jnp.dot(latent, w_in[:width], preferred_element_type=jnp.float32) + jnp.dot(
        agg, w_in[width:], preferred_element_type=jnp.float32
    )
    act = jax.nn.silu(pre).astype(jnp.bfloat16)
    upd = jnp.dot(act, w_out, preferred_element_type=jnp.float32)
    mean_upd = jnp.mean(upd, axis=1, keepdims=True)
    centred = upd - mean_upd
    var_upd = jnp.mean(centred * centred, axis=1, keepdims=True)
    hidden = (
        latent.astype(jnp.float32) + centred * lax.rsqrt(var_upd + 1e-05) * ln_gain[None, :]
    ).astype(jnp.bfloat16)
    pred = lax.dot_general(
        w_head, hidden, (((0,), (1,)), ((), ())), preferred_element_type=jnp.float32
    ).astype(jnp.bfloat16)
    num_vars = pred.shape[0]
    inv_sq = (1.0 / (kernel_width * kernel_width))[:, None]
    local = jnp.arange(fine_rows, dtype=jnp.int32)
    weight = (area * (local < live_counts[0]).astype(jnp.float32))[None, :]
    pred_f = pred.astype(jnp.float32)
    piece = lax.all_gather(pred[None], "mem", axis=0, tiled=True)

    def add_member(j, inner):
        other = lax.dynamic_index_in_dim(piece, j, 0, keepdims=False).astype(jnp.float32)
        return inner + slope(pred_f - other, inv_sq)

    acc = lax.fori_loop(
        0, piece.shape[0], add_member, jnp.zeros((num_vars, fine_rows), jnp.float32)
    )
    gscore = (
        weight * (acc / mem_count - slope(pred_f - targets.astype(jnp.float32), inv_sq))
    ).astype(jnp.bfloat16)
    grad_latent = lax.dot_general(
        gscore, w_head, (((0,), (1,)), ((), ())), preferred_element_type=jnp.float32
    ).astype(jnp.bfloat16)
    head_term = lax.dot_general(
        hidden, gscore, (((0,), (1,)), ((), ())), preferred_element_type=jnp.float32
    )
    head_total = lax.psum(head_term.astype(jnp.bfloat16), "mem").astype(jnp.float32)
    scale = 1.0 / math.sqrt(mem_count * fine_rows)
    return (grad_latent[None], (head_total * scale)[None])


def solution(mesh):
    return jax.shard_map(
        shards,
        mesh=mesh,
        in_specs=(
            P("mem", "dom", None),
            P("dom", None, None),
            P(None, "dom"),
            P(None, "dom"),
            P(None, "dom"),
            P("dom"),
            P("dom"),
            P("dom", None),
            P(None, "dom"),
            P(),
            P(),
            P(),
            P(),
            P(),
        ),
        out_specs=(P("mem", "dom", None), P("dom", None, None)),
        check_vma=False,
    )
```

profile of v0, /device:TPU:24, one launch (start us, length us, event | category | flops | bytes accessed | tf_op | source)
XLA Modules:
  0.0 267.6 jit_solution(14298033616810194048)
XLA Ops:
  7.2 0.0 copy-start
  7.2 0.7 fusion.19
  7.9 6.2 %gather_fusion = bf16[1024,512]{1,0:T(8,128)(2,1)} fusion(bf16[512,512]{1,0:T(8,128)(2,1)} %bitcast.72, s32[1024]{0:T(1024)S(1)} %fusion.19), kind=kCustom, calls=%fused_computation | custom fusion | bytes 2101248 | tf_op jit(solution)/shard_map/gather | solution.py:49
  14.2 5.2 %all-to-all-start = ((bf16[8,128,512]{2,1,0:T(8,128)(2,1)}), bf16[8,128,512]{2,1,0:T(8,128)(2,1)S(1)}, u32[]{:S(2)}, u32[]{:S(2)}) async-start(bf16[8,128,512]{2,1,0:T(8,128)(2,1)} %bitcast.5), calls=%async_computation | async-start | bytes 2097152 | tf_op jit(solution)/shard_map/all_to_all | solution.py:50
  19.5 0.1 compare_select_fusion.5
  19.6 0.0 copy-start.11
  19.6 4.0 %copy.38 = bf16[2048,512]{0,1:T(8,128)(2,1)} copy(bf16[2048,512]{1,0:T(8,128)(2,1)} %param.23) | data formatting | bytes 4194304 | tf_op args[7]
  23.6 19.8 %all-to-all-done = bf16[8,128,512]{2,1,0:T(8,128)(2,1)S(1)} async-done(((bf16[8,128,512]{2,1,0:T(8,128)(2,1)}), bf16[8,128,512]{2,1,0:T(8,128)(2,1)S(1)}, u32[]{:S(2)}, u32[]{:S(2)}) %all-to-all-start) | async-done | bytes 1048608 | tf_op jit(solution)/shard_map/all_to_all | solution.py:50
  43.4 9.2 %gather_fusion.1 = bf16[2048,512]{1,0:T(8,128)(2,1)} fusion(bf16[1024,512]{1,0:T(8,128)(2,1)S(1)} %bitcast.69, s32[2048]{0:T(1024)S(1)} %broadcast_clamp_fusion.8), kind=kCustom, calls=%fused_computation.1 | custom fusion | bytes 4202496 | tf_op jit(solution)/shard_map/gather | solution.py:54
  52.6 4.0 %copy.39 = bf16[2048,512]{0,1:T(8,128)(2,1)} copy(bf16[2048,512]{1,0:T(8,128)(2,1)} %gather_fusion.1) | data formatting | bytes 4194304 | tf_op jit(solution)/shard_map/gather | solution.py:54
  56.6 9.2 %gather_fusion.2 = bf16[2048,512]{1,0:T(8,128)(2,1)} fusion(bf16[1024,512]{1,0:T(8,128)(2,1)S(1)} %bitcast.70, s32[2048]{0:T(1024)S(1)} %broadcast_clamp_fusion.7), kind=kCustom, calls=%fused_computation.2 | custom fusion | bytes 4202496 | tf_op jit(solution)/shard_map/gather | solution.py:54
  65.8 4.0 %copy.40 = bf16[2048,512]{0,1:T(8,128)(2,1)} copy(bf16[2048,512]{1,0:T(8,128)(2,1)} %gather_fusion.2) | data formatting | bytes 4194304 | tf_op jit(solution)/shard_map/gather | solution.py:54
  69.7 9.2 %gather_fusion.3 = bf16[2048,512]{1,0:T(8,128)(2,1)} fusion(bf16[1024,512]{1,0:T(8,128)(2,1)S(1)} %bitcast.71, s32[2048]{0:T(1024)S(1)} %broadcast_clamp_fusion.6), kind=kCustom, calls=%fused_computation.3 | custom fusion | bytes 4202496 | tf_op jit(solution)/shard_map/gather | solution.py:54
  78.9 4.1 %copy.41 = bf16[2048,512]{0,1:T(8,128)(2,1)} copy(bf16[2048,512]{1,0:T(8,128)(2,1)} %gather_fusion.3) | data formatting | bytes 4194304 | tf_op jit(solution)/shard_map/gather | solution.py:54
  83.1 4.8 %add_convert_fusion.1 = bf16[2048,512]{0,1:T(8,128)(2,1)S(1)} fusion(bf16[2048,512]{0,1:T(8,128)(2,1)} %copy.41, bf16[2048,512]{0,1:T(8,128)(2,1)} %copy.40, bf16[2048,512]{0,1:T(8,128)(2,1)} %copy.39, bf16[2048,512]{0,1:T(8,128)(2,1)S(1)} %copy-done.4, f32[2048]{0:T(1024)S(1)} %bitcast.84, f32[2048]{0:T(1024)S(1)} %bitcast.85, f32[2048]{0:T(1024)S(1)} %bitcast.83), kind=kLoop, calls=%fused_computation.20 | loop fusion | flops 11534336 | bytes 10510336 | tf_op jit(solution)/shard_map/convert_element_type | solution.py:55
  87.9 0.0 copy-start.1
  88.0 2.0 collective-permute-start
  90.0 3.8 %collective-permute-start.1 = (bf16[128,512]{0,1:T(8,128)(2,1)S(1)}, bf16[128,512]{0,1:T(8,128)(2,1)S(1)}, u32[]{:S(2)}, u32[]{:S(2)}) collective-permute-start(bf16[128,512]{0,1:T(8,128)(2,1)S(1)} %get-tuple-element.132), channel_id=1, source_target_pairs={{4,0},{8,4},{12,8},{16,12},{20,16},{24,20},{28,24},{5,1},{9,5},{13... | collective-permute-start | bytes 393224 | tf_op jit(solution)/shard_map/ppermute | solution.py:20
  93.7 3.2 %fusion.15 = f32[2048,512]{1,0:T(8,128)} fusion(bf16[2048,512]{0,1:T(8,128)(2,1)S(1)} %add_convert_fusion.1, bf16[1024,512]{1,0:T(8,128)(2,1)S(1)} %copy-done.8), kind=kOutput, calls=%fused_computation.36 | convolution fusion | flops 1073741824 | bytes 6815744 | tf_op jit(solution)/shard_map/dot_general | solution.py:61
  97.0 1.7 pad_maximum_fusion
  98.7 2.8 %copy.42 = bf16[2304,512]{1,0:T(8,128)(2,1)S(1)} copy(bf16[2304,512]{0,1:T(8,128)(2,1)} %pad_maximum_fusion) | data formatting | bytes 4718592 | tf_op jit(solution)/shard_map/concatenate | solution.py:21
  101.5 9.2 %gather_fusion.4 = bf16[2048,512]{1,0:T(8,128)(2,1)} fusion(bf16[2304,512]{1,0:T(8,128)(2,1)S(1)} %copy.42, s32[2048]{0:T(1024)S(1)} %broadcast_clamp_fusion.5), kind=kCustom, calls=%fused_computation.4 | custom fusion | bytes 4202496 | tf_op jit(solution)/shard_map/gather | solution.py:59
  110.7 9.2 %gather_fusion.5 = bf16[2048,512]{1,0:T(8,128)(2,1)} fusion(bf16[2304,512]{1,0:T(8,128)(2,1)S(1)} %copy.42, s32[2048]{0:T(1024)S(1)} %broadcast_clamp_fusion.4), kind=kCustom, calls=%fused_computation.5 | custom fusion | bytes 4202496 | tf_op jit(solution)/shard_map/gather | solution.py:59
  119.8 9.2 %gather_fusion.6 = bf16[2048,512]{1,0:T(8,128)(2,1)} fusion(bf16[2304,512]{1,0:T(8,128)(2,1)S(1)} %copy.42, s32[2048]{0:T(1024)S(1)} %broadcast_clamp_fusion.3), kind=kCustom, calls=%fused_computation.6 | custom fusion | bytes 4202496 | tf_op jit(solution)/shard_map/gather | solution.py:59
  129.0 9.2 %gather_fusion.7 = bf16[2048,512]{1,0:T(8,128)(2,1)} fusion(bf16[2304,512]{1,0:T(8,128)(2,1)S(1)} %copy.42, s32[2048]{0:T(1024)S(1)} %broadcast_clamp_fusion.2), kind=kCustom, calls=%fused_computation.7 | custom fusion | bytes 4202496 | tf_op jit(solution)/shard_map/gather | solution.py:59
  138.2 9.2 %gather_fusion.8 = bf16[2048,512]{1,0:T(8,128)(2,1)} fusion(bf16[2304,512]{1,0:T(8,128)(2,1)S(1)} %copy.42, s32[2048]{0:T(1024)S(1)} %broadcast_clamp_fusion.1), kind=kCustom, calls=%fused_computation.8 | custom fusion | bytes 4202496 | tf_op jit(solution)/shard_map/gather | solution.py:59
  147.3 9.2 %gather_fusion.9 = bf16[2048,512]{1,0:T(8,128)(2,1)} fusion(bf16[2304,512]{1,0:T(8,128)(2,1)S(1)} %copy.42, s32[2048]{0:T(1024)S(1)} %broadcast_clamp_fusion), kind=kCustom, calls=%fused_computation.9 | custom fusion | bytes 4202496 | tf_op jit(solution)/shard_map/gather | solution.py:59
  156.5 11.6 %fusion.25 = (f32[2048]{0:T(1024)S(1)}, f32[2048,512]{0,1:T(8,128)}) fusion(bf16[512,512]{1,0:T(8,128)(2,1)S(1)} %copy-done, f32[2048,512]{1,0:T(8,128)} %fusion.15, bf16[2048,512]{1,0:T(8,128)(2,1)} %gather_fusion.9, bf16[2048,512]{1,0:T(8,128)(2,1)} %gather_fusion.8, bf16[2048,512]{1,0:T(8,128)(2,1)} %gather_fusion.7, ...), kind=kOutput, calls=%fused_computation.70 | convolution fusion | flops 2168453120 | bytes 22028288 | tf_op jit(solution)/shard_map/dot_general | solution.py:65
  168.1 2.8 %multiply_reduce_fusion = f32[2048]{0:T(1024)S(1)} fusion(f32[2048,512]{0,1:T(8,128)} %get-tuple-element.146, f32[2048]{0:T(1024)S(1)} %broadcast_multiply_fusion), kind=kLoop, calls=%fused_computation.17 | loop fusion | flops 3143680 | bytes 4210688 | tf_op jit(solution)/shard_map/reduce_sum | solution.py:68
  170.9 0.0 copy-done.2
  171.0 3.3 %add_convert_fusion = bf16[2048,512]{0,1:T(8,128)(2,1)S(1)} fusion(bf16[2048,512]{0,1:T(8,128)(2,1)S(1)} %copy-done.2, f32[2048,512]{0,1:T(8,128)} %get-tuple-element.146, f32[512]{0:T(512)S(1)} %copy-done.13, f32[2048]{0:T(1024)S(1)} %add_rsqrt_fusion, f32[2048]{0:T(1024)S(1)} %broadcast_multiply_fusion), kind=kLoop, calls=%fused_computation.16 | loop fusion | flops 6291456 | bytes 8407040 | tf_op jit(solution)/shard_map/convert_element_type | solution.py:71
  174.3 1.3 copy-done.3
  175.6 1.2 bitcast_convert_fusion
  176.8 0.0 all-gather.4.cloned.1.call-update
  176.8 0.0 all-reduce.2.cloned.1.call-start
  177.6 30.3 %all-gather.4.cloned.1.call-done = bf16[4,83,2048]{2,1,0:T(8,128)(2,1)} async-done(((bf16[1,83,2048]{2,1,0:T(8,128)(2,1)}), bf16[4,83,2048]{2,1,0:T(8,128)(2,1)}) %all-gather.4.cloned.1.call-update) | async-done | bytes 1359888 | tf_op jit(solution)/shard_map/all_gather | solution.py:80
  207.9 5.8 %while.14 = (s32[]{:T(128)}, f32[83,2048]{1,0:T(8,128)S(1)}, bf16[4,83,2048]{2,1,0:T(8,128)(2,1)}, f32[83,2048]{1,0:T(8,128)S(1)}, f32[83,1]{0,1:T(1,128)S(1)}, /*index=5*/s32[]{:T(128)}, s32[]{:T(128)}) while((s32[]{:T(128)}, f32[83,2048]{1,0:T(8,128)S(1)}, bf16[4,83,2048]{2,1,0:T(8,128)(2,1)}, f32[83,2048]{1,0:T(8,128)S(1)}, ...), condition=%wide.region_3.4_spmd.clone, body=%wide.region_2.3_spmd.clone.sunk | while | flops 1699843 | bytes 2380199 | solution.py:86
  207.9 1.5 fusion.38
  209.4 1.4 fusion.38
  210.8 1.4 fusion.38
  212.3 1.4 fusion.38
  213.7 0.4 fusion.12
  214.1 3.0 %convolution_convert_fusion.2 = bf16[512,83]{0,1:T(8,128)(2,1)} fusion(bf16[2048,512]{0,1:T(8,128)(2,1)} %copy-done.3, bf16[83,2048]{1,0:T(8,128)(2,1)S(1)} %fusion.12), kind=kOutput, calls=%fused_computation.27 | convolution fusion | flops 174106112 | bytes 2522112 | tf_op jit(solution)/shard_map/dot_general | solution.py:95
  217.1 0.0 all-reduce.2.cloned.1.call-update
  217.1 2.1 fusion.4
  219.2 39.8 %all-reduce.2.cloned.1.call-done = bf16[512,83]{0,1:T(8,128)(2,1)} async-done(((bf16[512,83]{0,1:T(8,128)(2,1)}), bf16[512,83]{0,1:T(8,128)(2,1)}) %all-reduce.2.cloned.1.call-update) | async-done | bytes 85008 | tf_op jit(solution)/shard_map/psum | solution.py:98
  259.0 0.9 multiply_bitcast_fusion
  259.9 0.8 copy.48
  (46 shorter events, 0.2 us)
Async XLA Ops:
  7.2 149.3 %copy-start = (bf16[512,512]{1,0:T(8,128)(2,1)S(1)}, bf16[512,512]{1,0:T(8,128)(2,1)}, u32[]{:S(2)}) copy-start(bf16[512,512]{1,0:T(8,128)(2,1)} %param.27) | copy-start | bytes 1572868
  14.2 5.2 %copy-start.10 = (s32[3,2048]{1,0:T(4,128)S(1)}, s32[3,2048]{1,0:T(4,128)}, u32[]{:S(2)}) copy-start(s32[3,2048]{1,0:T(4,128)} %param.18) | copy-start | bytes 73732
  14.2 5.3 %copy-start.9 = (s32[6,2048]{1,0:T(8,128)S(1)}, s32[6,2048]{1,0:T(8,128)}, u32[]{:S(2)}) copy-start(s32[6,2048]{1,0:T(8,128)} %param.20) | copy-start | bytes 147460
  14.2 29.3 %all-to-all-start = ((bf16[8,128,512]{2,1,0:T(8,128)(2,1)}), bf16[8,128,512]{2,1,0:T(8,128)(2,1)S(1)}, u32[]{:S(2)}, u32[]{:S(2)}) async-start(bf16[8,128,512]{2,1,0:T(8,128)(2,1)} %bitcast.5), calls=%async_computation | async-start | bytes 2097152 | tf_op jit(solution)/shard_map/all_to_all | solution.py:50
  19.4 188.5 %all-gather.4.cloned.1.call-start = ((), (), s32[]{:S(2)}) async-start(), calls=%async_computation.2 | async-start | bytes 1802240 | tf_op jit(solution)/shard_map/all_gather | solution.py:80
  19.6 4.0 %copy-start.11 = (f32[3,2048]{1,0:T(4,128)S(1)}, f32[3,2048]{1,0:T(4,128)}, u32[]{:S(2)}) copy-start(f32[3,2048]{1,0:T(4,128)} %param.19) | copy-start | bytes 73732
  78.9 4.1 %copy-start.4 = (bf16[2048,512]{0,1:T(8,128)(2,1)S(1)}, bf16[2048,512]{0,1:T(8,128)(2,1)}, u32[]{:S(2)}) copy-start(bf16[2048,512]{0,1:T(8,128)(2,1)} %copy.38) | copy-start | bytes 6291460
  83.1 10.7 %copy-start.8 = (bf16[1024,512]{1,0:T(8,128)(2,1)S(1)}, bf16[1024,512]{1,0:T(8,128)(2,1)}, u32[]{:S(2)}) copy-start(bf16[1024,512]{1,0:T(8,128)(2,1)} %param.26) | copy-start | bytes 3145732
  87.9 9.1 %copy-start.1 = (bf16[2048,512]{0,1:T(8,128)(2,1)}, bf16[2048,512]{0,1:T(8,128)(2,1)S(1)}, u32[]{:S(2)}) copy-start(bf16[2048,512]{0,1:T(8,128)(2,1)S(1)} %add_convert_fusion.1) | copy-start | bytes 6291460
  88.0 9.0 %collective-permute-start = (bf16[128,512]{0,1:T(8,128)(2,1)S(1)}, bf16[128,512]{0,1:T(8,128)(2,1)S(1)}, u32[]{:S(2)}, u32[]{:S(2)}) collective-permute-start(bf16[128,512]{0,1:T(8,128)(2,1)S(1)} %get-tuple-element.131), channel_id=1, source_target_pairs={{0,4},{4,8},{8,12},{12,16},{16,20},{20,24},{24,28},{1,5},{5,9},{9,... | collective-permute-start | bytes 393224 | tf_op jit(solution)/shard_map/ppermute | solution.py:19
  90.0 7.0 %collective-permute-start.1 = (bf16[128,512]{0,1:T(8,128)(2,1)S(1)}, bf16[128,512]{0,1:T(8,128)(2,1)S(1)}, u32[]{:S(2)}, u32[]{:S(2)}) collective-permute-start(bf16[128,512]{0,1:T(8,128)(2,1)S(1)} %get-tuple-element.132), channel_id=1, source_target_pairs={{4,0},{8,4},{12,8},{16,12},{20,16},{24,20},{28,24},{5,1},{9,5},{13... | collective-permute-start | bytes 393224 | tf_op jit(solution)/shard_map/ppermute | solution.py:20
  168.1 2.9 %copy-start.2 = (bf16[2048,512]{0,1:T(8,128)(2,1)S(1)}, bf16[2048,512]{0,1:T(8,128)(2,1)}, u32[]{:S(2)}) copy-start(bf16[2048,512]{0,1:T(8,128)(2,1)} %copy-done.1) | copy-start | bytes 6291460
  168.1 2.9 %copy-start.13 = (f32[512]{0:T(512)S(1)}, f32[512]{0:T(512)}, u32[]{:S(2)}) copy-start(f32[512]{0:T(512)} %param.28) | copy-start | bytes 6148
  170.9 4.7 %copy-start.6 = (bf16[512,83]{0,1:T(8,128)(2,1)S(1)}, bf16[512,83]{0,1:T(8,128)(2,1)}, u32[]{:S(2)}) copy-start(bf16[512,83]{0,1:T(8,128)(2,1)} %param.29) | copy-start | bytes 254980
  174.3 1.3 copy-start.3
  175.6 2.0 copy-start.14
  175.6 2.0 copy-start.12
  176.8 82.1 %all-reduce.2.cloned.1.call-start = ((), (), s32[]{:S(2)}) async-start(), calls=%async_computation.1 | async-start | bytes 180224 | tf_op jit(solution)/shard_map/psum | solution.py:98
  207.9 5.8 %copy-start.5 = (bf16[2048,83]{0,1:T(8,128)(2,1)S(1)}, bf16[2048,83]{0,1:T(8,128)(2,1)}, u32[]{:S(2)}) copy-start(bf16[2048,83]{0,1:T(8,128)(2,1)} %get-tuple-element.148) | copy-start | bytes 1019908
  207.9 5.8 %copy-start.7 = (bf16[83,2048]{1,0:T(8,128)(2,1)S(1)}, bf16[83,2048]{1,0:T(8,128)(2,1)}, u32[]{:S(2)}) copy-start(bf16[83,2048]{1,0:T(8,128)(2,1)} %param.24) | copy-start | bytes 1019908
Sparse Core Ops, SparseCore 0:
  177.0 30.8 all-gather.3
  217.2 41.7 all-reduce.1
where the time goes:
time: 270 us; the launch traced here: 268 us
  local copies, waits for them, and re-layouts  110 us (41%)
  waiting for transfers between devices  89.9 us (33%)
  matrix products  21.1 us (8%)
  other arithmetic  20.5 us (8%)
  between operations  15 us (6%)
  starting transfers between devices  11 us (4%)
    gather x6, local copies, waits for them, and re-layouts, shards(): total = total + extended[neighbors[k]].astype(jnp.float32)  55 us
    psum x1, waiting for transfers between devices, shards(): lax.psum(head_term.astype(jnp.bfloat16), 'mem').astype(jnp.float32)  39.8 us
    gather x6, local copies, waits for them, and re-layouts, shards(): table[up_index[k]].astype(jnp.float32)  39.6 us
    all_gather x1, waiting for transfers between devices, shards(): piece = lax.all_gather(pred[None], 'mem', axis=0, tiled=True)  30.3 us
    all_to_all x1, waiting for transfers between devices, shards(): lax.all_to_all(outgoing, 'dom', split_axis=0, concat_axis=0, tiled=True)  19.8 us
    dot_general x1, matrix products, shards(): upd = jnp.dot(act, w_out, preferred_element_type=jnp.float32)  11.6 us
    gather x1, local copies, waits for them, and re-layouts, shards(): outgoing = coarse_latents[0][send_rows[0]]  6.22 us
    unnamed x32, local copies, waits for them, and re-layouts  6.21 us
  transfers between devices with their start and end apart: 5, of which 3 were waited for; matrix products, arithmetic and copies ran while one was open for 4% of the time, Pallas kernels for 0%

commit v1 on v0

v1 whole, which is shorter than its diff:
```python
import functools
import math

import jax
import jax.numpy as jnp
from jax import lax
from jax.experimental import pallas as pl
from jax.experimental.pallas import tpu as pltpu
from jax.sharding import PartitionSpec as P

RIM = 128
MIB = 1024 * 1024
F32 = jnp.float32
BF16 = jnp.bfloat16
VMEM = pltpu.VMEM


def dot(a, b):
    return jnp.dot(a, b, preferred_element_type=F32)


def dot_of(a, b, da, db):
    return lax.dot_general(a, b, (((da,), (db,)), ((), ())), preferred_element_type=F32)


def params(mib):
    return pltpu.CompilerParams(vmem_limit_bytes=mib * MIB)


def cost(flops, nbytes, trans=0):
    return pl.CostEstimate(flops=flops, bytes_accessed=nbytes, transcendentals=trans)


def columns(rows):
    pad = -rows.shape[0] % 8
    if pad:
        rows = jnp.concatenate([rows, jnp.zeros((pad, rows.shape[1]), rows.dtype)], axis=0)
    return rows.T


def slope(diff, inv_sq):
    return -(diff * inv_sq) * jnp.exp(-0.5 * diff * diff * inv_sq)


def xor_permute(value, axis, step):
    count = lax.axis_size(axis)
    return lax.ppermute(value, axis, [(i, i ^ step) for i in range(count)])


def pick_kernel(send_ref, coarse_ref, *outs):
    me = lax.axis_index("dom")
    rows = jnp.concatenate([send_ref[0, pl.ds(me ^ s, 1), :] for s in range(len(outs))], axis=0)
    cols = columns(rows.astype(F32))
    table = coarse_ref[0]
    spots = lax.broadcasted_iota(jnp.int32, (rows.shape[1], table.shape[0]), 1).astype(F32)
    for s, out in enumerate(outs):
        hot = (cols[:, s : s + 1] == spots).astype(F32).astype(BF16)
        out[...] = dot(hot, table).astype(BF16)


def pick(send_rows, coarse):
    _, count, slots = send_rows.shape
    width = coarse.shape[2]
    return pl.pallas_call(
        pick_kernel,
        out_shape=[jax.ShapeDtypeStruct((slots, width), BF16)] * count,
        in_specs=[pl.BlockSpec(memory_space=VMEM)] * 2,
        out_specs=[pl.BlockSpec(memory_space=VMEM)] * count,
        compiler_params=params(16),
        cost_estimate=cost(2 * count * slots * coarse.shape[1] * width, 2 * MIB),
        name="pick",
    )(send_rows, coarse)


def spread_kernel(tile, index_ref, weight_ref, nb_ref, high_ref, low_ref, count_ref):
    me = lax.axis_index("dom")
    t = pl.program_id(0)
    slots = high_ref.shape[1]
    index = (index_ref[...] ^ (me * 128)).astype(F32)
    cols = columns(jnp.concatenate([index, weight_ref[...]], axis=0))
    k_up = index.shape[0]
    spots = lax.broadcasted_iota(jnp.int32, (tile, slots), 1).astype(F32)
    total = jnp.zeros((tile, slots), F32)
    for k in range(k_up):
        total = total + jnp.where(cols[:, k : k + 1] == spots, cols[:, k_up + k : k_up + k + 1], 0.0)
    high = total.astype(BF16)
    high_ref[...] = high
    low_ref[...] = (total - high.astype(F32)).astype(BF16)
    near = columns((nb_ref[...] - t * tile).astype(F32))
    span = count_ref.shape[2]
    places = lax.broadcasted_iota(jnp.int32, (tile, span), 1).astype(F32)
    counts = jnp.zeros((tile, span), F32)
    for k in range(nb_ref.shape[0]):
        counts = counts + jnp.where(near[:, k : k + 1] == places, 1.0, 0.0)
    count_ref[0] = counts.astype(BF16)


def spread(up_index, up_weight, neighbors, slots, tile):
    k_up, rows = up_index.shape
    k_nb = neighbors.shape[0]
    steps = rows // tile
    span = tile + 2 * RIM
    return pl.pallas_call(
        functools.partial(spread_kernel, tile),
        grid=(steps,),
        out_shape=[
            jax.ShapeDtypeStruct((rows, slots), BF16),
            jax.ShapeDtypeStruct((rows, slots), BF16),
            jax.ShapeDtypeStruct((steps, tile, span), BF16),
        ],
        in_specs=[
            pl.BlockSpec((k_up, tile), lambda t: (0, t)),
            pl.BlockSpec((k_up, tile), lambda t: (0, t)),
            pl.BlockSpec((k_nb, tile), lambda t: (0, t)),
        ],
        out_specs=[
            pl.BlockSpec((tile, slots), lambda t: (t, 0)),
            pl.BlockSpec((tile, slots), lambda t: (t, 0)),
            pl.BlockSpec((1, tile, span), lambda t: (t, 0, 0)),
        ],
        compiler_params=params(24),
        cost_estimate=cost(40 * rows * slots, 4 * rows * slots),
        name="spread",
    )(up_index, up_weight, neighbors)


def unpool_kernel(parts, high_ref, low_ref, skip_ref, *refs):
    tables, (x_ref, first_ref, last_ref) = refs[:parts], refs[parts:]
    t = pl.program_id(0)
    table = jnp.concatenate([r[...] for r in tables], axis=0)
    total = dot(high_ref[...], table) + dot(low_ref[...], table)
    x = (skip_ref[...].astype(F32) + total).astype(BF16)
    x_ref[...] = x

    @pl.when(t == 0)
    def _():
        first_ref[...] = x[:RIM]

    @pl.when(t == pl.num_programs(0) - 1)
    def _():
        last_ref[...] = x[x.shape[0] - RIM :]


def unpool(high, low, skip, tables, tile):
    rows, width = skip.shape
    slots = high.shape[1]
    count = len(tables)
    edge = jax.ShapeDtypeStruct((RIM, width), BF16)
    return pl.pallas_call(
        functools.partial(unpool_kernel, count),
        grid=(rows // tile,),
        out_shape=[jax.ShapeDtypeStruct((rows, width), BF16), edge, edge],
        in_specs=[
            pl.BlockSpec((tile, slots), lambda t: (t, 0)),
            pl.BlockSpec((tile, slots), lambda t: (t, 0)),
            pl.BlockSpec((tile, width), lambda t: (t, 0)),
        ]
        + [pl.BlockSpec(r.shape, lambda t: (0, 0)) for r in tables],
        out_specs=[
            pl.BlockSpec((tile, width), lambda t: (t, 0)),
            pl.BlockSpec((RIM, width), lambda t: (0, 0)),
            pl.BlockSpec((RIM, width), lambda t: (0, 0)),
        ],
        compiler_params=params(24),
        cost_estimate=cost(4 * rows * slots * width, 16 * MIB),
        name="unpool",
    )(high, low, skip, *tables)


def update_kernel(chunk, members, rimmed, x_ref, count_ref, w_in_ref, w_out_ref, gain_ref, head_ref, *refs):
    if rimmed:
        before_ref, after_ref, *refs = refs
    h_ref, preds = refs[0], refs[1:]
    me = lax.axis_index("mem")
    tiles, tile, _ = count_ref.shape
    rows, width = x_ref.shape
    gain = gain_ref[...]
    for s in range(members):
        t = lax.rem(1 + chunk * members + (me ^ s), tiles)
        start = pl.multiple_of(t * tile, tile)
        above = pl.multiple_of(jnp.maximum(start - RIM, 0), RIM)
        below = pl.multiple_of(jnp.minimum(start + tile, rows - RIM), RIM)
        x = x_ref[pl.ds(start, tile), :]
        top = x_ref[pl.ds(above, RIM), :]
        bottom = x_ref[pl.ds(below, RIM), :]
        if rimmed:
            top = jnp.where(t == 0, before_ref[...], top)
            bottom = jnp.where(t == tiles - 1, after_ref[...], bottom)
        window = jnp.concatenate([top, x, bottom], axis=0)
        agg = (dot(count_ref[t], window) * (1.0 / 6.0)).astype(BF16)
        pre = dot(x, w_in_ref[:width, :]) + dot(agg, w_in_ref[width:, :])
        act = (0.5 * pre * (1.0 + jnp.tanh(0.5 * pre))).astype(BF16)
        upd = dot(act, w_out_ref[...])
        mean = jnp.mean(upd, axis=1, keepdims=True)
        centred = upd - mean
        var = jnp.mean(centred * centred, axis=1, keepdims=True)
        h = (x.astype(F32) + centred * lax.rsqrt(var + 1e-05) * gain).astype(BF16)
        h_ref[pl.ds(s * tile, tile), :] = h
        preds[s][...] = dot_of(head_ref[...], h, 1, 1).astype(BF16)


def update(chunk, members, x, counts, w_in, w_out, gain, head, rims):
    tiles, tile, _ = counts.shape
    width = x.shape[1]
    points = members * tile
    operands = (x, counts, w_in, w_out, gain, head) + rims
    return pl.pallas_call(
        functools.partial(update_kernel, chunk, members, bool(rims)),
        out_shape=[jax.ShapeDtypeStruct((points, width), BF16)]
        + [jax.ShapeDtypeStruct((head.shape[0], tile), BF16)] * members,
        in_specs=[pl.BlockSpec(memory_space=VMEM)] * len(operands),
        out_specs=[pl.BlockSpec(memory_space=VMEM)] * (1 + members),
        compiler_params=params(32),
        cost_estimate=cost(points * width * width * 10, 8 * MIB, points * width),
        name="update",
    )(*operands)


def score_kernel(members, chunk, tiles, inv_ref, weight_ref, target_ref, *refs):
    preds, outs = refs[:members], refs[members:]
    t = lax.rem(1 + chunk * members + lax.axis_index("mem"), tiles)
    inv_sq = inv_ref[...]
    weight = weight_ref[pl.ds(t, 1), :]
    target = target_ref[t].astype(F32)
    values = [r[...].astype(F32) for r in preds]
    sums = [jnp.zeros(v.shape, F32) for v in values]
    for i in range(members):
        for j in range(i + 1, members):
            phi = slope(values[i] - values[j], inv_sq)
            sums[i] = sums[i] + phi
            sums[j] = sums[j] - phi
    for i in range(members):
        outs[i][...] = (weight * (sums[i] * (1.0 / members) - slope(values[i] - target, inv_sq))).astype(BF16)


def score(chunk, inv_sq, weight, target, preds):
    members = len(preds)
    tiles = target.shape[0]
    return pl.pallas_call(
        functools.partial(score_kernel, members, chunk, tiles),
        out_shape=[jax.ShapeDtypeStruct(preds[0].shape, BF16)] * members,
        in_specs=[pl.BlockSpec(memory_space=VMEM)] * (3 + members),
        out_specs=[pl.BlockSpec(memory_space=VMEM)] * members,
        compiler_params=params(16),
        cost_estimate=cost(10 * preds[0].size * members * members, MIB, preds[0].size * members * members),
        name="score",
    )(inv_sq, weight, target, *preds)


def head_kernel(chunks, members, *refs):
    hidden, scores, out = refs[:chunks], refs[chunks:-1], refs[-1]
    tile = scores[0].shape[1]
    total = jnp.zeros(out.shape, F32)
    for c in range(chunks):
        for s in range(members):
            total = total + dot(scores[c * members + s][...], hidden[c][s * tile : (s + 1) * tile, :])
    out[...] = total.astype(BF16)


def head_terms(members, hidden, scores):
    width = hidden[0].shape[1]
    return pl.pallas_call(
        functools.partial(head_kernel, len(hidden), members),
        out_shape=jax.ShapeDtypeStruct((scores[0].shape[0], width), BF16),
        in_specs=[pl.BlockSpec(memory_space=VMEM)] * (len(hidden) + len(scores)),
        out_specs=pl.BlockSpec(memory_space=VMEM),
        compiler_params=params(16),
        cost_estimate=cost(2 * scores[0].size * len(scores) * width, 3 * MIB),
        name="head_terms",
    )(*hidden, *scores)


def latent_kernel(chunks, members, head_ref, *refs):
    scores, out = refs[:-1], refs[-1]
    me = lax.axis_index("mem")
    tile = scores[0].shape[1]
    tiles = chunks * members
    for c in range(chunks):
        for s in range(members):
            t = lax.rem(1 + c * members + (me ^ s), tiles)
            rows = pl.ds(pl.multiple_of(t * tile, tile), tile)
            out[0, rows, :] = dot_of(scores[c * members + s][...], head_ref[...], 0, 0).astype(BF16)


def latent_grad(chunks, members, head, scores):
    rows, width = scores[0].shape[1] * len(scores), head.shape[1]
    return pl.pallas_call(
        functools.partial(latent_kernel, chunks, members),
        out_shape=jax.ShapeDtypeStruct((1, rows, width), BF16),
        in_specs=[pl.BlockSpec(memory_space=VMEM)] * (1 + len(scores)),
        out_specs=pl.BlockSpec(memory_space=VMEM),
        compiler_params=params(16),
        cost_estimate=cost(2 * scores[0].size * len(scores) * width, 3 * MIB),
        name="latent_grad",
    )(head, *scores)


def total_kernel(scale, *refs):
    terms, out = refs[:-1], refs[-1]
    total = terms[0][...].astype(F32)
    for term in terms[1:]:
        total = total + term[...].astype(F32)
    out[0] = (total * scale).T[:, : out.shape[2]]


def head_total(terms, num_vars, scale):
    return pl.pallas_call(
        functools.partial(total_kernel, scale),
        out_shape=jax.ShapeDtypeStruct((1, terms[0].shape[1], num_vars), F32),
        in_specs=[pl.BlockSpec(memory_space=VMEM)] * len(terms),
        out_specs=pl.BlockSpec(memory_space=VMEM),
        compiler_params=params(16),
        cost_estimate=cost(terms[0].size * len(terms), MIB),
        name="head_total",
    )(*terms)


def shards(
    coarse_latents,
    send_rows,
    up_index,
    up_weight,
    neighbors,
    live_counts,
    area,
    fine_skip,
    targets,
    kernel_width,
    w_in,
    w_out,
    ln_gain,
    w_head,
):
    dom_count = lax.axis_size("dom")
    members = lax.axis_size("mem")
    rows, width = fine_skip.shape
    num_vars = w_head.shape[1]
    padded = num_vars + -num_vars % 16
    tile = min(256, rows // members)
    tiles = rows // tile
    chunks = tiles // members

    outgoing = pick(send_rows, coarse_latents)
    tables = [outgoing[0]] + [None] * (dom_count - 1)
    for s in range(dom_count - 1, 0, -1):
        tables[s] = xor_permute(outgoing[s], "dom", s)

    high, low, counts = spread(up_index, up_weight, neighbors, dom_count * send_rows.shape[2], tile)
    pad = padded - num_vars
    head = jnp.pad(w_head.T, ((0, pad), (0, 0)))
    inv_sq = jnp.pad(1.0 / (kernel_width * kernel_width), (0, pad))[:, None]
    target = jnp.pad(targets, ((0, pad), (0, 0))).reshape(padded, tiles, tile).transpose(1, 0, 2)
    local = jnp.arange(rows, dtype=jnp.int32)
    weight = (area * (local < live_counts[0]).astype(F32)).reshape(tiles, tile)
    gain = ln_gain[None, :]

    x, first, last = unpool(high, low, fine_skip, tables, tile)
    up = [(i, i + 1) for i in range(dom_count - 1)]
    before = lax.ppermute(last, "dom", up)
    after = lax.ppermute(first, "dom", [(j, i) for i, j in up])

    hidden, scores = [], []
    for c in range(chunks):
        rims = (before, after) if c == chunks - 1 else ()
        h, *preds = update(c, members, x, counts, w_in, w_out, gain, head, rims)
        hidden.append(h)
        preds = [preds[0]] + [xor_permute(preds[s], "mem", s) for s in range(1, members)]
        got = score(c, inv_sq, weight, target, preds)
        scores += [got[0]] + [xor_permute(got[s], "mem", s) for s in range(1, members)]
    term = head_terms(members, hidden, scores)
    terms = [term] + [xor_permute(term, "mem", s) for s in range(1, members)]
    grad_latent = latent_grad(chunks, members, head, scores)
    scale = 1.0 / math.sqrt(members * rows)
    return (grad_latent, head_total(terms, num_vars, scale))


def solution(mesh):
    return jax.shard_map(
        shards,
        mesh=mesh,
        in_specs=(
            P("mem", "dom", None),
            P("dom", None, None),
            P(None, "dom"),
            P(None, "dom"),
            P(None, "dom"),
            P("dom"),
            P("dom"),
            P("dom", None),
            P(None, "dom"),
            P(),
            P(),
            P(),
            P(),
            P(),
        ),
        out_specs=(P("mem", "dom", None), P("dom", None, None)),
        check_vma=False,
    )
```

time: 270 us -> 84.1 us (0.31)
  the two profiles are of different devices: /device:TPU:24 before, /device:TPU:16 now
where the time goes in v1:
time: 84.1 us; the launch traced here: 83.7 us
  starting transfers between devices  29.8 us (35%)
  Pallas kernels  29.6 us (35%)
  waiting for transfers between devices  15.8 us (19%)
  local copies, waits for them, and re-layouts  6.42 us (8%)
  between operations  1.5 us (2%)
    ppermute x22, starting transfers between devices, xor_permute(): return lax.ppermute(value, axis, [(i, i ^ step) for i in range(count)])  24.1 us
    ppermute x22, waiting for transfers between devices, xor_permute(): return lax.ppermute(value, axis, [(i, i ^ step) for i in range(count)])  15.7 us
    pallas_call x2, Pallas kernels, update(): pl.pallas_call(functools.partial(update_kernel, chunk, members, bool(rims...  9.33 us
    pallas_call x1, Pallas kernels, spread(): pl.pallas_call(functools.partial(spread_kernel, tile), grid=(steps,), out...  8.29 us
    pallas_call x1, Pallas kernels, unpool(): pl.pallas_call(functools.partial(unpool_kernel, count), grid=(rows // til...  6.99 us
    unnamed x25, local copies, waits for them, and re-layouts  4.37 us
    ppermute x1, starting transfers between devices, shards(): after = lax.ppermute(first, 'dom', [(j, i) for i, j in up])  3.37 us
    ppermute x1, starting transfers between devices, shards(): before = lax.ppermute(last, 'dom', up)  2.38 us
  transfers between devices with their start and end apart: 24, of which 8 were waited for; matrix products, arithmetic and copies ran while one was open for 3% of the time, Pallas kernels for 25%

profile of v1, /device:TPU:16, one launch (start us, length us, event | category | flops | bytes accessed | tf_op | source)
XLA Modules:
  0.0 83.7 jit_solution(12673835821937989913)
XLA Ops:
  0.7 1.2 %copy-done.2 = bf16[1,512,512]{2,1,0:T(8,128)(2,1)S(1)} copy-done((bf16[1,512,512]{2,1,0:T(8,128)(2,1)S(1)}, bf16[1,512,512]{2,1,0:T(8,128)(2,1)}, u32[]{:S(2)}) %copy-start.2) | copy-done | bytes 524312
  1.8 0.7 copy-done.7
  2.5 1.4 %pick.1 = (bf16[128,512]{1,0:T(8,128)(2,1)S(1)}, bf16[128,512]{1,0:T(8,128)(2,1)}, bf16[128,512]{1,0:T(8,128)(2,1)}, bf16[128,512]{1,0:T(8,128)(2,1)}, bf16[128,...) custom-call(s32[1,8,128]{2,1,0:T(8,128)S(1)} %copy-done.7, ...), custom_call_target="tpu_custom_call" | custom-call | flops 536870912 | bytes 2097152 | tf_op jit(solution)/shard_map/pick/pallas_call | solution.py:64
  4.0 1.6 %collective-permute-start.1 = (bf16[128,512]{1,0:T(8,128)(2,1)}, bf16[128,512]{1,0:T(8,128)(2,1)S(1)}, u32[]{:S(2)}, u32[]{:S(2)}) collective-permute-start(bf16[128,512]{1,0:T(8,128)(2,1)} %get-tuple-element.38), channel_id=1, source_target_pairs={{0,8},{4,12},{8,0},{12,4},{16,24},{20,28},{24,16},{28,20},{1,9},{5... | collective-permute-start | bytes 393224 | tf_op jit(solution)/shard_map/ppermute | solution.py:47
  5.6 0.3 collective-permute-start.2
  5.8 0.2 collective-permute-start.3
  6.0 2.3 %collective-permute-start.4 = (bf16[128,512]{1,0:T(8,128)(2,1)}, bf16[128,512]{1,0:T(8,128)(2,1)}, u32[]{:S(2)}, u32[]{:S(2)}) collective-permute-start(bf16[128,512]{1,0:T(8,128)(2,1)} %get-tuple-element.41), channel_id=1, source_target_pairs={{0,20},{4,16},{8,28},{12,24},{16,4},{20,0},{24,12},{28,8},{1,21},{... | collective-permute-start | bytes 393224 | tf_op jit(solution)/shard_map/ppermute | solution.py:47
  8.4 0.7 multiply_divide_fusion
  9.0 0.9 %pad.12.head_ref = bf16[96,512]{1,0:T(8,128)(2,1)S(1)} pad(bf16[83,512]{1,0:T(8,128)(2,1)} %bitcast.18, bf16[]{:T(256)} %constant.5.clone.1), padding=0_13x0_0 | pad | bytes 183298 | tf_op jit(solution)/shard_map/jit(_pad)/pad | solution.py:350
  9.9 1.0 %pad.14 = bf16[96,2048]{1,0:T(8,128)(2,1)S(1)} pad(bf16[83,2048]{1,0:T(8,128)(2,1)} %param.22, bf16[]{:T(256)} %constant.5.clone.1), padding=0_13x0_0 | pad | bytes 733186 | tf_op jit(solution)/shard_map/jit(_pad)/pad | solution.py:352
  11.8 0.6 collective-permute-start.5
  12.4 1.3 %collective-permute-start.6 = (bf16[128,512]{1,0:T(8,128)(2,1)S(1)}, bf16[128,512]{1,0:T(8,128)(2,1)}, u32[]{:S(2)}, u32[]{:S(2)}) collective-permute-start(bf16[128,512]{1,0:T(8,128)(2,1)S(1)} %get-tuple-element.43), channel_id=1, source_target_pairs={{0,28},{4,24},{8,20},{12,16},{16,12},{20,8},{24,4},{28,0},{1,29},{... | collective-permute-start | bytes 393224 | tf_op jit(solution)/shard_map/ppermute | solution.py:47
  13.7 0.7 copy-done.6
  14.5 8.3 %spread.1 = (bf16[2048,1024]{1,0:T(8,128)(2,1)S(1)}, bf16[2048,1024]{1,0:T(8,128)(2,1)S(1)}, bf16[8,256,512]{2,1,0:T(8,128)(2,1)S(1)}) custom-call(s32[3,2048]{1,0:T(4,128)S(1)} %copy-done.5, f32[3,2048]{1,0:T(4,128)S(1)} %copy-done.6, s32[6,2048]{1,0:T(8,128)S(1)} %copy-done.4), custom_call_target="tpu_custom_call" | custom-call | flops 83886080 | bytes 8388608 | tf_op jit(solution)/shard_map/spread/pallas_call | solution.py:103
  22.8 0.9 %collective-permute-done.4.refs_5_ = bf16[128,512]{1,0:T(8,128)(2,1)} collective-permute-done((bf16[128,512]{1,0:T(8,128)(2,1)}, bf16[128,512]{1,0:T(8,128)(2,1)}, u32[]{:S(2)}, u32[]{:S(2)}) %collective-permute-start.4) | collective-permute-done | bytes 131104 | tf_op jit(solution)/shard_map/ppermute | solution.py:47
  23.8 6.6 %collective-permute-done.5.refs_6_ = bf16[128,512]{1,0:T(8,128)(2,1)} collective-permute-done((bf16[128,512]{1,0:T(8,128)(2,1)S(1)}, bf16[128,512]{1,0:T(8,128)(2,1)}, u32[]{:S(2)}, u32[]{:S(2)}) %collective-permute-start.5) | collective-permute-done | bytes 131104 | tf_op jit(solution)/shard_map/ppermute | solution.py:47
  30.4 1.5 %collective-permute-done.6.refs_7_ = bf16[128,512]{1,0:T(8,128)(2,1)} collective-permute-done((bf16[128,512]{1,0:T(8,128)(2,1)S(1)}, bf16[128,512]{1,0:T(8,128)(2,1)}, u32[]{:S(2)}, u32[]{:S(2)}) %collective-permute-start.6) | collective-permute-done | bytes 131104 | tf_op jit(solution)/shard_map/ppermute | solution.py:47
  31.9 0.9 %copy-done.10 = bf16[128,512]{1,0:T(8,128)(2,1)S(1)} copy-done((bf16[128,512]{1,0:T(8,128)(2,1)S(1)}, bf16[128,512]{1,0:T(8,128)(2,1)}, u32[]{:S(2)}) %copy-start.10) | copy-done | bytes 131096
  32.8 7.0 %unpool.1 = (bf16[2048,512]{1,0:T(8,128)(2,1)S(1)}, bf16[128,512]{1,0:T(8,128)(2,1)S(1)}, bf16[128,512]{1,0:T(8,128)(2,1)S(1)}) custom-call(bf16[2048,1024]{1,0:T(8,128)(2,1)S(1)} %get-tuple-element.34.high_ref, bf16[2048,1024]{1,0:T(8,128)(2,1)S(1)} %get-tuple-element.35.low_ref, bf16[2048,512]{1,0:T(8,128)(2,1)S(1)} %copy-done, ...), custom_call_target="tpu_custom_call" | custom-call | flops 4294967296 | bytes 16777216 | tf_op jit(solution)/shard_map/unpool/pallas_call | solution.py:149
  39.8 2.4 %collective-permute-start.13 = (bf16[128,512]{1,0:T(8,128)(2,1)S(1)}, bf16[128,512]{1,0:T(8,128)(2,1)S(1)}, u32[]{:S(2)}, u32[]{:S(2)}) collective-permute-start(bf16[128,512]{1,0:T(8,128)(2,1)S(1)} %get-tuple-element.54), channel_id=1, source_target_pairs={{0,4},{4,8},{8,12},{12,16},{16,20},{20,24},{24,28},{1,5},{5,9},{9,... | collective-permute-start | bytes 393224 | tf_op jit(solution)/shard_map/ppermute | solution.py:359
  42.2 3.4 %collective-permute-start.14 = (bf16[128,512]{1,0:T(8,128)(2,1)S(1)}, bf16[128,512]{1,0:T(8,128)(2,1)S(1)}, u32[]{:S(2)}, u32[]{:S(2)}) collective-permute-start(bf16[128,512]{1,0:T(8,128)(2,1)S(1)} %get-tuple-element.55), channel_id=1, source_target_pairs={{4,0},{8,4},{12,8},{16,12},{20,16},{24,20},{28,24},{5,1},{9,5},{13... | collective-permute-start | bytes 393224 | tf_op jit(solution)/shard_map/ppermute | solution.py:360
  45.6 4.7 %update.2 = (bf16[1024,512]{1,0:T(8,128)(2,1)S(1)}, bf16[96,256]{1,0:T(8,128)(2,1)S(1)}, bf16[96,256]{1,0:T(8,128)(2,1)S(1)}, bf16[96,256]{1,0:T(8,128)(2,1)S(1)}, bf16[96,256]{1,0:T(8,128)(2,1)S(1)}) custom-call(bf16[2048,512]{1,0:T(8,128)(2,1)S(1)} %get-tuple-element.44.x_ref, bf16[8,256,512]{2,1,0:T(8,128)(2,1)S(1)} %get-tuple-element.45.count_ref, ...), custom_call_target="tpu_custom_call" | custom-call | flops 2684354560 | bytes 8388608 | tf_op jit(solution)/shard_map/update/pallas_call | solution.py:207
  50.3 1.6 %collective-permute-start.7 = (bf16[96,256]{1,0:T(8,128)(2,1)S(1)}, bf16[96,256]{1,0:T(8,128)(2,1)S(1)}, u32[]{:S(2)}, u32[]{:S(2)}) collective-permute-start(bf16[96,256]{1,0:T(8,128)(2,1)S(1)} %get-tuple-element.47), channel_id=1, source_target_pairs={{0,1},{1,0},{2,3},{3,2},{4,5},{5,4},{6,7},{7,6},{8,9},{9,8},{10,11... | collective-permute-start | bytes 147464 | tf_op jit(solution)/shard_map/ppermute | solution.py:47
  51.9 1.5 %collective-permute-start.8 = (bf16[96,256]{1,0:T(8,128)(2,1)S(1)}, bf16[96,256]{1,0:T(8,128)(2,1)S(1)}, u32[]{:S(2)}, u32[]{:S(2)}) collective-permute-start(bf16[96,256]{1,0:T(8,128)(2,1)S(1)} %get-tuple-element.48), channel_id=1, source_target_pairs={{0,2},{1,3},{2,0},{3,1},{4,6},{5,7},{6,4},{7,5},{8,10},{9,11},{10,... | collective-permute-start | bytes 147464 | tf_op jit(solution)/shard_map/ppermute | solution.py:47
  53.4 0.5 collective-permute-start.9
  53.9 4.6 %update.3 = (bf16[1024,512]{1,0:T(8,128)(2,1)S(1)}, bf16[96,256]{1,0:T(8,128)(2,1)S(1)}, bf16[96,256]{1,0:T(8,128)(2,1)S(1)}, bf16[96,256]{1,0:T(8,128)(2,1)S(1)}, bf16[96,256]{1,0:T(8,128)(2,1)S(1)}) custom-call(bf16[2048,512]{1,0:T(8,128)(2,1)S(1)} %get-tuple-element.44.x_ref, bf16[8,256,512]{2,1,0:T(8,128)(2,1)S(1)} %get-tuple-element.45.count_ref, ...), custom_call_target="tpu_custom_call" | custom-call | flops 2684354560 | bytes 8388608 | tf_op jit(solution)/shard_map/update/pallas_call | solution.py:207
  58.5 1.6 %collective-permute-start.15 = (bf16[96,256]{1,0:T(8,128)(2,1)S(1)}, bf16[96,256]{1,0:T(8,128)(2,1)S(1)}, u32[]{:S(2)}, u32[]{:S(2)}) collective-permute-start(bf16[96,256]{1,0:T(8,128)(2,1)S(1)} %get-tuple-element.57), channel_id=1, source_target_pairs={{0,1},{1,0},{2,3},{3,2},{4,5},{5,4},{6,7},{7,6},{8,9},{9,8},{10,11... | collective-permute-start | bytes 147464 | tf_op jit(solution)/shard_map/ppermute | solution.py:47
  60.1 1.5 %collective-permute-start.16 = (bf16[96,256]{1,0:T(8,128)(2,1)S(1)}, bf16[96,256]{1,0:T(8,128)(2,1)S(1)}, u32[]{:S(2)}, u32[]{:S(2)}) collective-permute-start(bf16[96,256]{1,0:T(8,128)(2,1)S(1)} %get-tuple-element.58), channel_id=1, source_target_pairs={{0,2},{1,3},{2,0},{3,1},{4,6},{5,7},{6,4},{7,5},{8,10},{9,11},{10,... | collective-permute-start | bytes 147464 | tf_op jit(solution)/shard_map/ppermute | solution.py:47
  61.6 0.5 collective-permute-start.17
  62.1 0.4 score.2
  62.5 1.6 %collective-permute-start.10 = (bf16[96,256]{1,0:T(8,128)(2,1)S(1)}, bf16[96,256]{1,0:T(8,128)(2,1)S(1)}, u32[]{:S(2)}, u32[]{:S(2)}) collective-permute-start(bf16[96,256]{1,0:T(8,128)(2,1)S(1)} %get-tuple-element.51), channel_id=1, source_target_pairs={{0,1},{1,0},{2,3},{3,2},{4,5},{5,4},{6,7},{7,6},{8,9},{9,8},{10,11... | collective-permute-start | bytes 147464 | tf_op jit(solution)/shard_map/ppermute | solution.py:47
  64.1 1.5 %collective-permute-start.11 = (bf16[96,256]{1,0:T(8,128)(2,1)S(1)}, bf16[96,256]{1,0:T(8,128)(2,1)S(1)}, u32[]{:S(2)}, u32[]{:S(2)}) collective-permute-start(bf16[96,256]{1,0:T(8,128)(2,1)S(1)} %get-tuple-element.52), channel_id=1, source_target_pairs={{0,2},{1,3},{2,0},{3,1},{4,6},{5,7},{6,4},{7,5},{8,10},{9,11},{10,... | collective-permute-start | bytes 147464 | tf_op jit(solution)/shard_map/ppermute | solution.py:47
  65.6 0.5 collective-permute-start.12
  66.1 1.0 %collective-permute-done.17.refs_3_ = bf16[96,256]{1,0:T(8,128)(2,1)S(1)} collective-permute-done((bf16[96,256]{1,0:T(8,128)(2,1)S(1)}, bf16[96,256]{1,0:T(8,128)(2,1)S(1)}, u32[]{:S(2)}, u32[]{:S(2)}) %collective-permute-start.17) | collective-permute-done | bytes 49184 | tf_op jit(solution)/shard_map/ppermute | solution.py:47
  67.1 0.4 score.3
  67.5 0.6 collective-permute-start.18
  68.1 1.5 %collective-permute-start.19 = (bf16[96,256]{1,0:T(8,128)(2,1)S(1)}, bf16[96,256]{1,0:T(8,128)(2,1)S(1)}, u32[]{:S(2)}, u32[]{:S(2)}) collective-permute-start(bf16[96,256]{1,0:T(8,128)(2,1)S(1)} %get-tuple-element.62), channel_id=1, source_target_pairs={{0,2},{1,3},{2,0},{3,1},{4,6},{5,7},{6,4},{7,5},{8,10},{9,11},{10,... | collective-permute-start | bytes 147464 | tf_op jit(solution)/shard_map/ppermute | solution.py:47
  69.6 1.5 %collective-permute-start.20 = (bf16[96,256]{1,0:T(8,128)(2,1)S(1)}, bf16[96,256]{1,0:T(8,128)(2,1)S(1)}, u32[]{:S(2)}, u32[]{:S(2)}) collective-permute-start(bf16[96,256]{1,0:T(8,128)(2,1)S(1)} %get-tuple-element.63), channel_id=1, source_target_pairs={{0,3},{1,2},{2,1},{3,0},{4,7},{5,6},{6,5},{7,4},{8,11},{9,10},{10,... | collective-permute-start | bytes 147464 | tf_op jit(solution)/shard_map/ppermute | solution.py:47
  71.1 0.6 collective-permute-done.18.refs_5_.refs_7_
  71.7 0.5 collective-permute-done.19.refs_6_.refs_8_
  72.2 2.5 %collective-permute-done.20.refs_7_.refs_9_ = bf16[96,256]{1,0:T(8,128)(2,1)S(1)} collective-permute-done((bf16[96,256]{1,0:T(8,128)(2,1)S(1)}, bf16[96,256]{1,0:T(8,128)(2,1)S(1)}, u32[]{:S(2)}, u32[]{:S(2)}) %collective-permute-start.20) | collective-permute-done | bytes 49184 | tf_op jit(solution)/shard_map/ppermute | solution.py:47
  74.7 0.5 head_terms.1.refs_0_
  75.2 0.8 collective-permute-start.21
  76.0 1.3 %collective-permute-start.22 = (bf16[96,512]{1,0:T(8,128)(2,1)S(1)}, bf16[96,512]{1,0:T(8,128)(2,1)S(1)}, u32[]{:S(2)}, u32[]{:S(2)}) collective-permute-start(bf16[96,512]{1,0:T(8,128)(2,1)S(1)} %head_terms.1.refs_0_), channel_id=1, source_target_pairs={{0,2},{1,3},{2,0},{3,1},{4,6},{5,7},{6,4},{7,5},{8,10},{9,11},{10,... | collective-permute-start | bytes 294920 | tf_op jit(solution)/shard_map/ppermute | solution.py:47
  77.3 1.5 %collective-permute-start.23 = (bf16[96,512]{1,0:T(8,128)(2,1)S(1)}, bf16[96,512]{1,0:T(8,128)(2,1)S(1)}, u32[]{:S(2)}, u32[]{:S(2)}) collective-permute-start(bf16[96,512]{1,0:T(8,128)(2,1)S(1)} %head_terms.1.refs_0_), channel_id=1, source_target_pairs={{0,3},{1,2},{2,1},{3,0},{4,7},{5,6},{6,5},{7,4},{8,11},{9,10},{10,... | collective-permute-start | bytes 294920 | tf_op jit(solution)/shard_map/ppermute | solution.py:47
  78.8 2.0 %latent_grad.1 = bf16[1,2048,512]{2,1,0:T(8,128)(2,1)} custom-call(bf16[96,512]{1,0:T(8,128)(2,1)S(1)} %pad.12.head_ref, bf16[96,256]{1,0:T(8,128)(2,1)S(1)} %get-tuple-element.50.refs_0_.refs_2_, bf16[96,256]{1,0:T(8,128)(2,1)S(1)} %collective-permute-done.10.refs_1_.refs_3_, bf16[96,256]{1,0:T(8,128)(2,1)S(1)} %collective-permute-done.11.refs_2_.refs_4_, ...), custom_call_target="tpu_custom_call" | custom-call | flops 201326592 | bytes 3145728 | tf_op jit(solution)/shard_map/latent_grad/pallas_call | solution.py:287
  80.8 2.0 %collective-permute-done.23.refs_3_ = bf16[96,512]{1,0:T(8,128)(2,1)S(1)} collective-permute-done((bf16[96,512]{1,0:T(8,128)(2,1)S(1)}, bf16[96,512]{1,0:T(8,128)(2,1)S(1)}, u32[]{:S(2)}, u32[]{:S(2)}) %collective-permute-start.23) | collective-permute-done | bytes 98336 | tf_op jit(solution)/shard_map/ppermute | solution.py:47
  82.9 0.8 copy.22
  (43 shorter events, 0.4 us)
Async XLA Ops:
  0.6 31.3 %copy-start = (bf16[2048,512]{1,0:T(8,128)(2,1)S(1)}, bf16[2048,512]{1,0:T(8,128)(2,1)}, u32[]{:S(2)}) copy-start(bf16[2048,512]{1,0:T(8,128)(2,1)} %skip_ref.1) | copy-start | bytes 6291460
  0.6 1.2 %copy-start.2 = (bf16[1,512,512]{2,1,0:T(8,128)(2,1)S(1)}, bf16[1,512,512]{2,1,0:T(8,128)(2,1)}, u32[]{:S(2)}) copy-start(bf16[1,512,512]{2,1,0:T(8,128)(2,1)} %coarse_ref.1) | copy-start | bytes 1572868
  1.8 0.7 copy-start.7
  2.5 11.2 %copy-start.11 = (f32[2048]{0:T(1024)S(1)}, f32[2048]{0:T(1024)}, u32[]{:S(2)}) copy-start(f32[2048]{0:T(1024)} %param.20) | copy-start | bytes 24580
  2.5 11.2 %copy-start.4 = (s32[6,2048]{1,0:T(8,128)S(1)}, s32[6,2048]{1,0:T(8,128)}, u32[]{:S(2)}) copy-start(s32[6,2048]{1,0:T(8,128)} %nb_ref.1) | copy-start | bytes 147460
  2.5 11.2 %copy-start.5 = (s32[3,2048]{1,0:T(4,128)S(1)}, s32[3,2048]{1,0:T(4,128)}, u32[]{:S(2)}) copy-start(s32[3,2048]{1,0:T(4,128)} %index_ref.1) | copy-start | bytes 73732
  4.0 7.0 %copy-start.9 = (bf16[128,512]{1,0:T(8,128)(2,1)}, bf16[128,512]{1,0:T(8,128)(2,1)S(1)}, u32[]{:S(2)}) copy-start(bf16[128,512]{1,0:T(8,128)(2,1)S(1)} %get-tuple-element.36.refs_0_) | copy-start | bytes 393220
  4.0 7.8 %collective-permute-start = (bf16[128,512]{1,0:T(8,128)(2,1)}, bf16[128,512]{1,0:T(8,128)(2,1)S(1)}, u32[]{:S(2)}, u32[]{:S(2)}) collective-permute-start(bf16[128,512]{1,0:T(8,128)(2,1)} %get-tuple-element.37), channel_id=1, source_target_pairs={{0,4},{4,0},{8,12},{12,8},{16,20},{20,16},{24,28},{28,24},{1,5},{5... | collective-permute-start | bytes 393224 | tf_op jit(solution)/shard_map/ppermute | solution.py:47
  4.0 8.4 %collective-permute-start.1 = (bf16[128,512]{1,0:T(8,128)(2,1)}, bf16[128,512]{1,0:T(8,128)(2,1)S(1)}, u32[]{:S(2)}, u32[]{:S(2)}) collective-permute-start(bf16[128,512]{1,0:T(8,128)(2,1)} %get-tuple-element.38), channel_id=1, source_target_pairs={{0,8},{4,12},{8,0},{12,4},{16,24},{20,28},{24,16},{28,20},{1,9},{5... | collective-permute-start | bytes 393224 | tf_op jit(solution)/shard_map/ppermute | solution.py:47
  5.6 17.2 %collective-permute-start.2 = (bf16[128,512]{1,0:T(8,128)(2,1)}, bf16[128,512]{1,0:T(8,128)(2,1)S(1)}, u32[]{:S(2)}, u32[]{:S(2)}) collective-permute-start(bf16[128,512]{1,0:T(8,128)(2,1)} %get-tuple-element.39), channel_id=1, source_target_pairs={{0,12},{4,8},{8,4},{12,0},{16,28},{20,24},{24,20},{28,16},{1,13},{... | collective-permute-start | bytes 393224 | tf_op jit(solution)/shard_map/ppermute | solution.py:47
  5.8 17.0 %collective-permute-start.3 = (bf16[128,512]{1,0:T(8,128)(2,1)}, bf16[128,512]{1,0:T(8,128)(2,1)S(1)}, u32[]{:S(2)}, u32[]{:S(2)}) collective-permute-start(bf16[128,512]{1,0:T(8,128)(2,1)} %get-tuple-element.40), channel_id=1, source_target_pairs={{0,16},{4,20},{8,24},{12,28},{16,0},{20,4},{24,8},{28,12},{1,17},{... | collective-permute-start | bytes 393224 | tf_op jit(solution)/shard_map/ppermute | solution.py:47
  6.0 17.7 %collective-permute-start.4 = (bf16[128,512]{1,0:T(8,128)(2,1)}, bf16[128,512]{1,0:T(8,128)(2,1)}, u32[]{:S(2)}, u32[]{:S(2)}) collective-permute-start(bf16[128,512]{1,0:T(8,128)(2,1)} %get-tuple-element.41), channel_id=1, source_target_pairs={{0,20},{4,16},{8,28},{12,24},{16,4},{20,0},{24,12},{28,8},{1,21},{... | collective-permute-start | bytes 393224 | tf_op jit(solution)/shard_map/ppermute | solution.py:47
  11.8 18.6 %collective-permute-start.5 = (bf16[128,512]{1,0:T(8,128)(2,1)S(1)}, bf16[128,512]{1,0:T(8,128)(2,1)}, u32[]{:S(2)}, u32[]{:S(2)}) collective-permute-start(bf16[128,512]{1,0:T(8,128)(2,1)S(1)} %get-tuple-element.42), channel_id=1, source_target_pairs={{0,24},{4,28},{8,16},{12,20},{16,8},{20,12},{24,0},{28,4},{1,25},{... | collective-permute-start | bytes 393224 | tf_op jit(solution)/shard_map/ppermute | solution.py:47
  12.4 19.6 %collective-permute-start.6 = (bf16[128,512]{1,0:T(8,128)(2,1)S(1)}, bf16[128,512]{1,0:T(8,128)(2,1)}, u32[]{:S(2)}, u32[]{:S(2)}) collective-permute-start(bf16[128,512]{1,0:T(8,128)(2,1)S(1)} %get-tuple-element.43), channel_id=1, source_target_pairs={{0,28},{4,24},{8,20},{12,16},{16,12},{20,8},{24,4},{28,0},{1,29},{... | collective-permute-start | bytes 393224 | tf_op jit(solution)/shard_map/ppermute | solution.py:47
  13.7 0.8 copy-start.6
  31.9 0.9 %copy-start.10 = (bf16[128,512]{1,0:T(8,128)(2,1)S(1)}, bf16[128,512]{1,0:T(8,128)(2,1)}, u32[]{:S(2)}) copy-start(bf16[128,512]{1,0:T(8,128)(2,1)} %copy-done.9) | copy-start | bytes 393220
  32.8 12.8 %copy-start.1 = (bf16[1024,512]{1,0:T(8,128)(2,1)S(1)}, bf16[1024,512]{1,0:T(8,128)(2,1)}, u32[]{:S(2)}) copy-start(bf16[1024,512]{1,0:T(8,128)(2,1)} %w_in_ref.3) | copy-start | bytes 3145732
  32.8 12.8 %copy-start.3 = (bf16[512,512]{1,0:T(8,128)(2,1)S(1)}, bf16[512,512]{1,0:T(8,128)(2,1)}, u32[]{:S(2)}) copy-start(bf16[512,512]{1,0:T(8,128)(2,1)} %w_out_ref.3) | copy-start | bytes 1572868
  32.8 12.8 %copy-start.8 = (f32[512]{0:T(512)S(1)}, f32[512]{0:T(512)}, u32[]{:S(2)}) copy-start(f32[512]{0:T(512)} %param.26) | copy-start | bytes 6148
  39.8 14.0 %collective-permute-start.13 = (bf16[128,512]{1,0:T(8,128)(2,1)S(1)}, bf16[128,512]{1,0:T(8,128)(2,1)S(1)}, u32[]{:S(2)}, u32[]{:S(2)}) collective-permute-start(bf16[128,512]{1,0:T(8,128)(2,1)S(1)} %get-tuple-element.54), channel_id=1, source_target_pairs={{0,4},{4,8},{8,12},{12,16},{16,20},{20,24},{24,28},{1,5},{5,9},{9,... | collective-permute-start | bytes 393224 | tf_op jit(solution)/shard_map/ppermute | solution.py:359
  42.2 11.7 %collective-permute-start.14 = (bf16[128,512]{1,0:T(8,128)(2,1)S(1)}, bf16[128,512]{1,0:T(8,128)(2,1)S(1)}, u32[]{:S(2)}, u32[]{:S(2)}) collective-permute-start(bf16[128,512]{1,0:T(8,128)(2,1)S(1)} %get-tuple-element.55), channel_id=1, source_target_pairs={{4,0},{8,4},{12,8},{16,12},{20,16},{24,20},{28,24},{5,1},{9,5},{13... | collective-permute-start | bytes 393224 | tf_op jit(solution)/shard_map/ppermute | solution.py:360
  50.3 11.3 %collective-permute-start.7 = (bf16[96,256]{1,0:T(8,128)(2,1)S(1)}, bf16[96,256]{1,0:T(8,128)(2,1)S(1)}, u32[]{:S(2)}, u32[]{:S(2)}) collective-permute-start(bf16[96,256]{1,0:T(8,128)(2,1)S(1)} %get-tuple-element.47), channel_id=1, source_target_pairs={{0,1},{1,0},{2,3},{3,2},{4,5},{5,4},{6,7},{7,6},{8,9},{9,8},{10,11... | collective-permute-start | bytes 147464 | tf_op jit(solution)/shard_map/ppermute | solution.py:47
  51.9 10.2 %collective-permute-start.8 = (bf16[96,256]{1,0:T(8,128)(2,1)S(1)}, bf16[96,256]{1,0:T(8,128)(2,1)S(1)}, u32[]{:S(2)}, u32[]{:S(2)}) collective-permute-start(bf16[96,256]{1,0:T(8,128)(2,1)S(1)} %get-tuple-element.48), channel_id=1, source_target_pairs={{0,2},{1,3},{2,0},{3,1},{4,6},{5,7},{6,4},{7,5},{8,10},{9,11},{10,... | collective-permute-start | bytes 147464 | tf_op jit(solution)/shard_map/ppermute | solution.py:47
  53.4 8.7 %collective-permute-start.9 = (bf16[96,256]{1,0:T(8,128)(2,1)S(1)}, bf16[96,256]{1,0:T(8,128)(2,1)S(1)}, u32[]{:S(2)}, u32[]{:S(2)}) collective-permute-start(bf16[96,256]{1,0:T(8,128)(2,1)S(1)} %get-tuple-element.49), channel_id=1, source_target_pairs={{0,3},{1,2},{2,1},{3,0},{4,7},{5,6},{6,5},{7,4},{8,11},{9,10},{10,... | collective-permute-start | bytes 147464 | tf_op jit(solution)/shard_map/ppermute | solution.py:47
  58.5 7.1 %collective-permute-start.15 = (bf16[96,256]{1,0:T(8,128)(2,1)S(1)}, bf16[96,256]{1,0:T(8,128)(2,1)S(1)}, u32[]{:S(2)}, u32[]{:S(2)}) collective-permute-start(bf16[96,256]{1,0:T(8,128)(2,1)S(1)} %get-tuple-element.57), channel_id=1, source_target_pairs={{0,1},{1,0},{2,3},{3,2},{4,5},{5,4},{6,7},{7,6},{8,9},{9,8},{10,11... | collective-permute-start | bytes 147464 | tf_op jit(solution)/shard_map/ppermute | solution.py:47
  60.1 6.0 %collective-permute-start.16 = (bf16[96,256]{1,0:T(8,128)(2,1)S(1)}, bf16[96,256]{1,0:T(8,128)(2,1)S(1)}, u32[]{:S(2)}, u32[]{:S(2)}) collective-permute-start(bf16[96,256]{1,0:T(8,128)(2,1)S(1)} %get-tuple-element.58), channel_id=1, source_target_pairs={{0,2},{1,3},{2,0},{3,1},{4,6},{5,7},{6,4},{7,5},{8,10},{9,11},{10,... | collective-permute-start | bytes 147464 | tf_op jit(solution)/shard_map/ppermute | solution.py:47
  61.6 5.5 %collective-permute-start.17 = (bf16[96,256]{1,0:T(8,128)(2,1)S(1)}, bf16[96,256]{1,0:T(8,128)(2,1)S(1)}, u32[]{:S(2)}, u32[]{:S(2)}) collective-permute-start(bf16[96,256]{1,0:T(8,128)(2,1)S(1)} %get-tuple-element.59), channel_id=1, source_target_pairs={{0,3},{1,2},{2,1},{3,0},{4,7},{5,6},{6,5},{7,4},{8,11},{9,10},{10,... | collective-permute-start | bytes 147464 | tf_op jit(solution)/shard_map/ppermute | solution.py:47
  62.5 7.1 %collective-permute-start.10 = (bf16[96,256]{1,0:T(8,128)(2,1)S(1)}, bf16[96,256]{1,0:T(8,128)(2,1)S(1)}, u32[]{:S(2)}, u32[]{:S(2)}) collective-permute-start(bf16[96,256]{1,0:T(8,128)(2,1)S(1)} %get-tuple-element.51), channel_id=1, source_target_pairs={{0,1},{1,0},{2,3},{3,2},{4,5},{5,4},{6,7},{7,6},{8,9},{9,8},{10,11... | collective-permute-start | bytes 147464 | tf_op jit(solution)/shard_map/ppermute | solution.py:47
  64.1 7.0 %collective-permute-start.11 = (bf16[96,256]{1,0:T(8,128)(2,1)S(1)}, bf16[96,256]{1,0:T(8,128)(2,1)S(1)}, u32[]{:S(2)}, u32[]{:S(2)}) collective-permute-start(bf16[96,256]{1,0:T(8,128)(2,1)S(1)} %get-tuple-element.52), channel_id=1, source_target_pairs={{0,2},{1,3},{2,0},{3,1},{4,6},{5,7},{6,4},{7,5},{8,10},{9,11},{10,... | collective-permute-start | bytes 147464 | tf_op jit(solution)/shard_map/ppermute | solution.py:47
  65.6 5.5 %collective-permute-start.12 = (bf16[96,256]{1,0:T(8,128)(2,1)S(1)}, bf16[96,256]{1,0:T(8,128)(2,1)S(1)}, u32[]{:S(2)}, u32[]{:S(2)}) collective-permute-start(bf16[96,256]{1,0:T(8,128)(2,1)S(1)} %get-tuple-element.53), channel_id=1, source_target_pairs={{0,3},{1,2},{2,1},{3,0},{4,7},{5,6},{6,5},{7,4},{8,11},{9,10},{10,... | collective-permute-start | bytes 147464 | tf_op jit(solution)/shard_map/ppermute | solution.py:47
  67.5 4.2 %collective-permute-start.18 = (bf16[96,256]{1,0:T(8,128)(2,1)S(1)}, bf16[96,256]{1,0:T(8,128)(2,1)S(1)}, u32[]{:S(2)}, u32[]{:S(2)}) collective-permute-start(bf16[96,256]{1,0:T(8,128)(2,1)S(1)} %get-tuple-element.61), channel_id=1, source_target_pairs={{0,1},{1,0},{2,3},{3,2},{4,5},{5,4},{6,7},{7,6},{8,9},{9,8},{10,11... | collective-permute-start | bytes 147464 | tf_op jit(solution)/shard_map/ppermute | solution.py:47
  68.1 4.1 %collective-permute-start.19 = (bf16[96,256]{1,0:T(8,128)(2,1)S(1)}, bf16[96,256]{1,0:T(8,128)(2,1)S(1)}, u32[]{:S(2)}, u32[]{:S(2)}) collective-permute-start(bf16[96,256]{1,0:T(8,128)(2,1)S(1)} %get-tuple-element.62), channel_id=1, source_target_pairs={{0,2},{1,3},{2,0},{3,1},{4,6},{5,7},{6,4},{7,5},{8,10},{9,11},{10,... | collective-permute-start | bytes 147464 | tf_op jit(solution)/shard_map/ppermute | solution.py:47
  69.6 5.1 %collective-permute-start.20 = (bf16[96,256]{1,0:T(8,128)(2,1)S(1)}, bf16[96,256]{1,0:T(8,128)(2,1)S(1)}, u32[]{:S(2)}, u32[]{:S(2)}) collective-permute-start(bf16[96,256]{1,0:T(8,128)(2,1)S(1)} %get-tuple-element.63), channel_id=1, source_target_pairs={{0,3},{1,2},{2,1},{3,0},{4,7},{5,6},{6,5},{7,4},{8,11},{9,10},{10,... | collective-permute-start | bytes 147464 | tf_op jit(solution)/shard_map/ppermute | solution.py:47
  75.2 5.6 %collective-permute-start.21 = (bf16[96,512]{1,0:T(8,128)(2,1)S(1)}, bf16[96,512]{1,0:T(8,128)(2,1)S(1)}, u32[]{:S(2)}, u32[]{:S(2)}) collective-permute-start(bf16[96,512]{1,0:T(8,128)(2,1)S(1)} %head_terms.1.refs_0_), channel_id=1, source_target_pairs={{0,1},{1,0},{2,3},{3,2},{4,5},{5,4},{6,7},{7,6},{8,9},{9,8},{10,11... | collective-permute-start | bytes 294920 | tf_op jit(solution)/shard_map/ppermute | solution.py:47
  76.0 4.8 %collective-permute-start.22 = (bf16[96,512]{1,0:T(8,128)(2,1)S(1)}, bf16[96,512]{1,0:T(8,128)(2,1)S(1)}, u32[]{:S(2)}, u32[]{:S(2)}) collective-permute-start(bf16[96,512]{1,0:T(8,128)(2,1)S(1)} %head_terms.1.refs_0_), channel_id=1, source_target_pairs={{0,2},{1,3},{2,0},{3,1},{4,6},{5,7},{6,4},{7,5},{8,10},{9,11},{10,... | collective-permute-start | bytes 294920 | tf_op jit(solution)/shard_map/ppermute | solution.py:47
  77.3 5.5 %collective-permute-start.23 = (bf16[96,512]{1,0:T(8,128)(2,1)S(1)}, bf16[96,512]{1,0:T(8,128)(2,1)S(1)}, u32[]{:S(2)}, u32[]{:S(2)}) collective-permute-start(bf16[96,512]{1,0:T(8,128)(2,1)S(1)} %head_terms.1.refs_0_), channel_id=1, source_target_pairs={{0,3},{1,2},{2,1},{3,0},{4,7},{5,6},{6,5},{7,4},{8,11},{9,10},{10,... | collective-permute-start | bytes 294920 | tf_op jit(solution)/shard_map/ppermute | solution.py:47

commit v2 on v0

v2 whole, which is shorter than its diff:
```python
import functools
import math

import jax
import jax.numpy as jnp
from jax import lax
from jax.experimental import pallas as pl
from jax.experimental.pallas import tpu as pltpu
from jax.sharding import PartitionSpec as P

RIM = 128
MIB = 1024 * 1024
F32 = jnp.float32
BF16 = jnp.bfloat16
VMEM = pltpu.VMEM


def dot(a, b):
    return jnp.dot(a, b, preferred_element_type=F32)


def dot_of(a, b, da, db):
    return lax.dot_general(a, b, (((da,), (db,)), ((), ())), preferred_element_type=F32)


def params(mib):
    return pltpu.CompilerParams(vmem_limit_bytes=mib * MIB)


def cost(flops, nbytes, trans=0):
    return pl.CostEstimate(flops=flops, bytes_accessed=nbytes, transcendentals=trans)


def columns(rows):
    pad = -rows.shape[0] % 8
    if pad:
        rows = jnp.concatenate([rows, jnp.zeros((pad, rows.shape[1]), rows.dtype)], axis=0)
    return rows.T


def slope(diff, inv_sq):
    return -(diff * inv_sq) * jnp.exp(-0.5 * diff * diff * inv_sq)


def xor_permute(value, axis, step):
    count = lax.axis_size(axis)
    return lax.ppermute(value, axis, [(i, i ^ step) for i in range(count)])


def pick_kernel(send_ref, coarse_ref, *refs):
    outs, (rows_ref, table_ref, sems) = refs[:-3], refs[-3:]
    copies = [
        pltpu.make_async_copy(send_ref, rows_ref, sems.at[0]),
        pltpu.make_async_copy(coarse_ref, table_ref, sems.at[1]),
    ]
    for copy in copies:
        copy.start()
    me = lax.axis_index("dom")
    copies[0].wait()
    rows = jnp.concatenate([rows_ref[0, pl.ds(me ^ s, 1), :] for s in range(len(outs))], axis=0)
    cols = columns(rows.astype(F32))
    spots = lax.broadcasted_iota(jnp.int32, (rows.shape[1], table_ref.shape[1]), 1).astype(F32)
    copies[1].wait()
    table = table_ref[0]
    for s in reversed(range(len(outs))):
        hot = (cols[:, s : s + 1] == spots).astype(F32).astype(BF16)
        outs[s][...] = dot(hot, table).astype(BF16)


def pick(send_rows, coarse):
    _, count, slots = send_rows.shape
    width = coarse.shape[2]
    return pl.pallas_call(
        pick_kernel,
        out_shape=[jax.ShapeDtypeStruct((slots, width), BF16)] * count,
        in_specs=[pl.BlockSpec(memory_space=pl.ANY)] * 2,
        out_specs=[pl.BlockSpec(memory_space=VMEM)] * count,
        scratch_shapes=[
            VMEM(send_rows.shape, jnp.int32),
            VMEM(coarse.shape, BF16),
            pltpu.SemaphoreType.DMA((2,)),
        ],
        compiler_params=params(16),
        cost_estimate=cost(2 * count * slots * coarse.shape[1] * width, 2 * MIB),
        name="pick",
    )(send_rows, coarse)


def spread_kernel(tile, index_ref, weight_ref, nb_ref, head_in_ref, spread_ref, count_ref, head_ref):
    me = lax.axis_index("dom")
    rows, slots = spread_ref.shape
    span = count_ref.shape[2]
    part = 32
    head_ref[...] = jnp.zeros(head_ref.shape, BF16)
    head_ref[: head_in_ref.shape[0], :] = head_in_ref[...]
    zero, one = jnp.zeros((), BF16), jnp.ones((), BF16)
    spots = lax.broadcasted_iota(jnp.int16, (part, slots), 1)
    places = lax.broadcasted_iota(jnp.int16, (part, span), 1)

    def narrow(value):
        return columns(value.astype(F32)).astype(jnp.int32).astype(jnp.int16)

    def step(t, carry):
        start = pl.multiple_of(t * tile, tile)
        lanes = pl.ds(start, tile)
        index = narrow(index_ref[:, lanes] ^ (me * 128))
        weight = columns(weight_ref[:, lanes]).astype(BF16)
        near = narrow(nb_ref[:, lanes] - start)
        for r in range(0, tile, part):
            total = jnp.zeros((part, slots), BF16)
            for k in range(index_ref.shape[0]):
                total = total + jnp.where(index[r : r + part, k : k + 1] == spots, weight[r : r + part, k : k + 1], zero)
            spread_ref[pl.ds(pl.multiple_of(start + r, part), part), :] = total
            counts = jnp.zeros((part, span), BF16)
            for k in range(nb_ref.shape[0]):
                counts = counts + jnp.where(near[r : r + part, k : k + 1] == places, one, zero)
            count_ref[t, r : r + part, :] = counts
        return carry

    lax.fori_loop(0, rows // tile, step, 0)


def spread(up_index, up_weight, neighbors, head, slots, tile, padded):
    rows = up_index.shape[1]
    steps = rows // tile
    span = tile + 2 * RIM
    return pl.pallas_call(
        functools.partial(spread_kernel, tile),
        out_shape=[
            jax.ShapeDtypeStruct((rows, slots), BF16),
            jax.ShapeDtypeStruct((steps, tile, span), BF16),
            jax.ShapeDtypeStruct((padded, head.shape[1]), BF16),
        ],
        in_specs=[pl.BlockSpec(memory_space=VMEM)] * 4,
        out_specs=[pl.BlockSpec(memory_space=VMEM)] * 3,
        compiler_params=params(16),
        cost_estimate=cost(40 * rows * slots, 4 * rows * slots),
        name="spread",
    )(up_index, up_weight, neighbors, head)


def early_kernel(begin, end, tile, spread_ref, skip_ref, *refs):
    tables, out = refs[:-1], refs[-1]
    table = jnp.concatenate([r[...] for r in tables], axis=0)

    def step(t, carry):
        rows = pl.ds(pl.multiple_of(t * tile, tile), tile)
        out[rows, :] = skip_ref[rows, :].astype(F32) + dot(spread_ref[rows, begin:end], table)
        return carry

    lax.fori_loop(0, out.shape[0] // tile, step, 0)


def early(spread_rows, skip, begin, end, tables, tile):
    rows, width = skip.shape
    operands = (spread_rows, skip, *tables)
    return pl.pallas_call(
        functools.partial(early_kernel, begin, end, tile),
        out_shape=jax.ShapeDtypeStruct((rows, width), F32),
        in_specs=[pl.BlockSpec(memory_space=VMEM)] * len(operands),
        out_specs=pl.BlockSpec(memory_space=VMEM),
        compiler_params=params(16),
        cost_estimate=cost(2 * rows * (end - begin) * width, 8 * MIB),
        name="early",
    )(*operands)


def late_kernel(begin, end, tile, sum_ref, spread_ref, *refs):
    tables, (x_ref, inner_ref, outer_ref) = refs[:-3], refs[-3:]
    table = jnp.concatenate([r[...] for r in tables], axis=0)
    count = x_ref.shape[0]

    def step(t, carry):
        rows = pl.ds(pl.multiple_of(t * tile, tile), tile)
        x_ref[rows, :] = (sum_ref[rows, :] + dot(spread_ref[rows, begin:end], table)).astype(BF16)
        return carry

    lax.fori_loop(0, count // tile, step, 0)
    odd = lax.rem(lax.axis_index("dom"), 2) == 1
    first, last = x_ref[:RIM, :], x_ref[count - RIM :, :]
    inner_ref[...] = jnp.where(odd, first, last)
    outer_ref[...] = jnp.where(odd, last, first)


def late(sums, spread_rows, begin, end, tables, tile):
    rows, width = sums.shape
    operands = (sums, spread_rows, *tables)
    edge = jax.ShapeDtypeStruct((RIM, width), BF16)
    return pl.pallas_call(
        functools.partial(late_kernel, begin, end, tile),
        out_shape=[jax.ShapeDtypeStruct((rows, width), BF16), edge, edge],
        in_specs=[pl.BlockSpec(memory_space=VMEM)] * len(operands),
        out_specs=[pl.BlockSpec(memory_space=VMEM)] * 3,
        compiler_params=params(16),
        cost_estimate=cost(2 * rows * (end - begin) * width, 8 * MIB),
        name="late",
    )(*operands)


def tile_update(x, window, counts, w_in_ref, w_out_ref, gain_ref, head_ref):
    width = x.shape[1]
    agg = (dot(counts, window) * (1.0 / 6.0)).astype(BF16)
    pre = dot(x, w_in_ref[:width, :]) + dot(agg, w_in_ref[width:, :])
    act = (0.5 * pre * (1.0 + jnp.tanh(0.5 * pre))).astype(BF16)
    upd = dot(act, w_out_ref[...])
    mean = jnp.mean(upd, axis=1, keepdims=True)
    centred = upd - mean
    var = jnp.mean(centred * centred, axis=1, keepdims=True)
    h = (x.astype(F32) + centred * lax.rsqrt(var + 1e-05) * gain_ref[...]).astype(BF16)
    return h, dot_of(head_ref[...], h, 1, 1).astype(BF16)


def inner_kernel(x_ref, count_ref, w_in_ref, w_out_ref, gain_ref, head_ref, h_ref, pred_ref):
    tiles, tile, _ = count_ref.shape
    for t in range(1, tiles - 1):
        x = x_ref[t * tile : (t + 1) * tile, :]
        window = x_ref[t * tile - RIM : (t + 1) * tile + RIM, :]
        h, pred = tile_update(x, window, count_ref[t], w_in_ref, w_out_ref, gain_ref, head_ref)
        h_ref[(t - 1) * tile : t * tile, :] = h
        pred_ref[t - 1] = pred


def outer_kernel(members, x_ref, count_ref, w_in_ref, w_out_ref, gain_ref, head_ref, inner_ref, outer_ref, done_ref, h_ref, *refs):
    outs, all_ref = refs[:-1], refs[-1]
    tiles, tile, _ = count_ref.shape
    odd = lax.rem(lax.axis_index("dom"), 2) == 1
    inner, outer = inner_ref[...], outer_ref[...]
    before, after = jnp.where(odd, inner, outer), jnp.where(odd, outer, inner)
    rows = tiles * tile
    for place, t in enumerate((0, tiles - 1)):
        x = x_ref[t * tile : (t + 1) * tile, :]
        if t == 0:
            window = jnp.concatenate([before, x_ref[: tile + RIM, :]], axis=0)
        else:
            window = jnp.concatenate([x_ref[rows - tile - RIM :, :], after], axis=0)
        h, pred = tile_update(x, window, count_ref[t], w_in_ref, w_out_ref, gain_ref, head_ref)
        h_ref[place * tile : (place + 1) * tile, :] = h
        all_ref[t] = pred
    all_ref[1 : tiles - 1] = done_ref[...]
    me = lax.axis_index("mem")
    per = tiles // members
    for s, out in enumerate(outs):
        for k in range(per):
            out[:, k * tile : (k + 1) * tile] = all_ref[(me ^ s) * per + k]


def update_call(kernel, operands, out_shape, scratch, flops, name):
    return pl.pallas_call(
        kernel,
        out_shape=out_shape,
        in_specs=[pl.BlockSpec(memory_space=VMEM)] * len(operands),
        out_specs=[pl.BlockSpec(memory_space=VMEM)] * len(out_shape),
        scratch_shapes=scratch,
        compiler_params=params(24),
        cost_estimate=cost(flops, 8 * MIB),
        name=name,
    )(*operands)


def update(members, x, counts, w_in, w_out, gain, head, inner, outer):
    tiles, tile, _ = counts.shape
    width = x.shape[1]
    padded = head.shape[0]
    shared = (x, counts, w_in, w_out, gain, head)
    h_mid, pred_mid = update_call(
        inner_kernel,
        shared,
        [
            jax.ShapeDtypeStruct(((tiles - 2) * tile, width), BF16),
            jax.ShapeDtypeStruct((tiles - 2, padded, tile), BF16),
        ],
        [],
        (tiles - 2) * tile * width * width * 10,
        "inner",
    )
    h_end, *preds = update_call(
        functools.partial(outer_kernel, members),
        shared + (inner, outer, pred_mid),
        [jax.ShapeDtypeStruct((2 * tile, width), BF16)]
        + [jax.ShapeDtypeStruct((padded, tiles // members * tile), BF16)] * members,
        [VMEM((tiles, padded, tile), BF16)],
        2 * tile * width * width * 10,
        "outer",
    )
    return h_mid, h_end, preds


def score_kernel(members, live_ref, kw_ref, area_ref, target_ref, *refs):
    preds, outs, (kw_rows, target) = refs[:members], refs[members:-2], refs[-2:]
    num_vars = target_ref.shape[0]
    padded, piece = target.shape
    start = pl.multiple_of(lax.axis_index("mem") * piece, piece)
    lanes = pl.ds(start, piece)
    kw_rows[...] = jnp.ones(kw_rows.shape, F32)
    kw_rows[0:1, :num_vars] = kw_ref[...]
    width = kw_rows[...].T[:padded, 0:1]
    inv_sq = 1.0 / (width * width)
    target[...] = jnp.zeros(target.shape, F32)
    target[:num_vars, :] = target_ref[:, lanes].astype(F32)
    place = start + lax.broadcasted_iota(jnp.int32, (1, piece), 1)
    weight = jnp.where(place < live_ref[0], area_ref[:, lanes], 0.0)
    values = [r[...].astype(F32) for r in preds]
    sums = [jnp.zeros(v.shape, F32) for v in values]
    for i in range(members):
        for j in range(i + 1, members):
            phi = slope(values[i] - values[j], inv_sq)
            sums[i] = sums[i] + phi
            sums[j] = sums[j] - phi
    for i in range(members):
        total = sums[i] * (1.0 / members) - slope(values[i] - target[...], inv_sq)
        outs[i][...] = (weight * total).astype(BF16)


def score(live_counts, kernel_width, area, targets, preds):
    members = len(preds)
    shape = preds[0].shape
    return pl.pallas_call(
        functools.partial(score_kernel, members),
        out_shape=[jax.ShapeDtypeStruct(shape, BF16)] * members,
        in_specs=[pl.BlockSpec(memory_space=pltpu.SMEM)] + [pl.BlockSpec(memory_space=VMEM)] * (3 + members),
        out_specs=[pl.BlockSpec(memory_space=VMEM)] * members,
        scratch_shapes=[VMEM((8, 128), F32), VMEM(shape, F32)],
        compiler_params=params(16),
        cost_estimate=cost(10 * preds[0].size * members * members, MIB, preds[0].size * members * members),
        name="score",
    )(live_counts, kernel_width, area, targets, *preds)


def head_kernel(members, mid_ref, end_ref, *refs):
    scores, (out, all_ref) = refs[:-2], refs[-2:]
    tiles, _, tile = all_ref.shape
    me = lax.axis_index("mem")
    per = tiles // members
    for s in range(members):
        for k in range(per):
            all_ref[(me ^ s) * per + k] = scores[s][:, k * tile : (k + 1) * tile]
    total = dot(all_ref[0], end_ref[:tile, :]) + dot(all_ref[tiles - 1], end_ref[tile:, :])
    for t in range(1, tiles - 1):
        total = total + dot(all_ref[t], mid_ref[(t - 1) * tile : t * tile, :])
    out[...] = total.astype(BF16)


def head_terms(members, mid, end, scores):
    width = end.shape[1]
    tile = end.shape[0] // 2
    tiles = members * scores[0].shape[1] // tile
    padded = scores[0].shape[0]
    return pl.pallas_call(
        functools.partial(head_kernel, members),
        out_shape=[
            jax.ShapeDtypeStruct((padded, width), BF16),
            jax.ShapeDtypeStruct((tiles, padded, tile), BF16),
        ],
        in_specs=[pl.BlockSpec(memory_space=VMEM)] * (2 + members),
        out_specs=[pl.BlockSpec(memory_space=VMEM)] * 2,
        compiler_params=params(16),
        cost_estimate=cost(2 * padded * tiles * tile * width, 3 * MIB),
        name="head_terms",
    )(mid, end, *scores)


def latent_kernel(head_ref, score_ref, out):
    tile = score_ref.shape[2]
    for t in range(score_ref.shape[0]):
        out[0, t * tile : (t + 1) * tile, :] = dot_of(score_ref[t], head_ref[...], 0, 0).astype(BF16)


def latent_grad(head, scores):
    tiles, padded, tile = scores.shape
    width = head.shape[1]
    return pl.pallas_call(
        latent_kernel,
        out_shape=jax.ShapeDtypeStruct((1, tiles * tile, width), BF16),
        in_specs=[pl.BlockSpec(memory_space=VMEM)] * 2,
        out_specs=pl.BlockSpec(memory_space=VMEM),
        compiler_params=params(16),
        cost_estimate=cost(2 * scores.size * width, 3 * MIB),
        name="latent_grad",
    )(head, scores)


def total_kernel(scale, *refs):
    terms, out = refs[:-1], refs[-1]
    total = terms[0][...].astype(F32)
    for term in terms[1:]:
        total = total + term[...].astype(F32)
    out[0] = (total * scale)[: out.shape[1], :]


def head_total(terms, num_vars, scale):
    return pl.pallas_call(
        functools.partial(total_kernel, scale),
        out_shape=jax.ShapeDtypeStruct((1, num_vars, terms[0].shape[1]), F32),
        in_specs=[pl.BlockSpec(memory_space=VMEM)] * len(terms),
        out_specs=pl.BlockSpec(memory_space=VMEM),
        compiler_params=params(16),
        cost_estimate=cost(terms[0].size * len(terms), MIB),
        name="head_total",
    )(*terms)


def shards(
    coarse_latents,
    send_rows,
    up_index,
    up_weight,
    neighbors,
    live_counts,
    area,
    fine_skip,
    targets,
    kernel_width,
    w_in,
    w_out,
    ln_gain,
    w_head,
):
    dom_count = lax.axis_size("dom")
    members = lax.axis_size("mem")
    slots = send_rows.shape[2]
    rows, width = fine_skip.shape
    num_vars = w_head.shape[1]
    padded = num_vars + -num_vars % 16
    tile = min(256, rows // members)

    outgoing = pick(send_rows, coarse_latents)
    tables = [outgoing[0]] + [None] * (dom_count - 1)
    for s in range(1, dom_count):
        tables[s] = xor_permute(outgoing[s], "dom", s)

    spread_rows, counts, head = spread(
        up_index, up_weight, neighbors, w_head.T, dom_count * slots, tile, padded
    )
    split = dom_count - 2
    sums = early(spread_rows, fine_skip, 0, split * slots, tables[:split], tile)
    x, inner, outer = late(sums, spread_rows, split * slots, dom_count * slots, tables[split:], tile)
    inner = xor_permute(inner, "dom", 1)
    pairs = [(i, i + 1) for i in range(1, dom_count - 1, 2)]
    outer = lax.ppermute(outer, "dom", pairs + [(j, i) for i, j in pairs])

    mid, end, preds = update(members, x, counts, w_in, w_out, ln_gain[None, :], head, inner, outer)
    preds = [preds[0]] + [xor_permute(preds[s], "mem", s) for s in range(1, members)]
    scores = score(live_counts, kernel_width[None, :], area[None, :], targets, preds)
    scores = [scores[0]] + [xor_permute(scores[s], "mem", s) for s in range(1, members)]
    term, by_tile = head_terms(members, mid, end, scores)
    terms = [term] + [xor_permute(term, "mem", s) for s in range(1, members)]
    grad_latent = latent_grad(head, by_tile)
    scale = 1.0 / math.sqrt(members * rows)
    return (grad_latent, head_total(terms, num_vars, scale).transpose(0, 2, 1))


def solution(mesh):
    return jax.shard_map(
        shards,
        mesh=mesh,
        in_specs=(
            P("mem", "dom", None),
            P("dom", None, None),
            P(None, "dom"),
            P(None, "dom"),
            P(None, "dom"),
            P("dom"),
            P("dom"),
            P("dom", None),
            P(None, "dom"),
            P(),
            P(),
            P(),
            P(),
            P(),
        ),
        out_specs=(P("mem", "dom", None), P("dom", None, None)),
        check_vma=False,
    )
```

time: 270 us -> 72.6 us (0.27)
  local copies, waits for them, and re-layouts: 110 us -> 6 us
  waiting for transfers between devices: 89.9 us -> 14.7 us
  Pallas kernels: 0 us -> 23.7 us
  matrix products: 21.1 us -> 0 us
  other arithmetic: 20.5 us -> 0 us
  starting transfers between devices: 11 us -> 26.4 us
  between operations: 15 us -> 1.49 us
    gather x13 -> x0, local copies, waits for them, and re-layouts: 101 us -> none  [the longest x6 55 us: shards(): total = total + extended[neighbors[k]].astype(jnp.float32)]
    psum x1 -> x0, waiting for transfers between devices: 39.8 us -> none  [shards(): lax.psum(head_term.astype(jnp.bfloat16), 'mem').astype(jnp.float32)]
    all_gather x1 -> x0, waiting for transfers between devices: 30.3 us -> none  [shards(): piece = lax.all_gather(pred[None], 'mem', axis=0, tiled=True)]
    pallas_call x0 -> x10, Pallas kernels: none -> 23.7 us  [the longest x2 9.34 us: update_call(): pl.pallas_call(kernel, out_shape=out_shape, in_specs=[pl.BlockSpec(memory...]
    dot_general x5 -> x0, matrix products: 21.1 us -> none  [the longest x1 11.6 us: shards(): upd = jnp.dot(act, w_out, preferred_element_type=jnp.float32)]
    ppermute x2 -> x18, starting transfers between devices: 5.74 us -> 26.4 us  [the longest x17 22.3 us: xor_permute(): return lax.ppermute(value, axis, [(i, i ^ step) for i in range(count)])]
    all_to_all x1 -> x0, waiting for transfers between devices: 19.8 us -> none  [shards(): lax.all_to_all(outgoing, 'dom', split_axis=0, concat_axis=0, tiled=True)]
    ppermute x2 -> x18, waiting for transfers between devices: 0.01 us -> 14.7 us  [the longest x17 14.7 us: xor_permute(): return lax.ppermute(value, axis, [(i, i ^ step) for i in range(count)])]
  transfers between devices with their start and end apart: 5 -> 18, of which waited for: 3 -> 9; matrix products, arithmetic and copies ran while one was open for 4% -> 0% of each run, Pallas kernels for 0% -> 23%
where the time goes in v2:
time: 72.6 us; the launch traced here: 72.2 us
  starting transfers between devices  26.4 us (36%)
  Pallas kernels  23.7 us (33%)
  waiting for transfers between devices  14.7 us (20%)
  local copies, waits for them, and re-layouts  6 us (8%)
  between operations  1.49 us (2%)
    ppermute x17, starting transfers between devices, xor_permute(): return lax.ppermute(value, axis, [(i, i ^ step) for i in range(count)])  22.3 us
    ppermute x17, waiting for transfers between devices, xor_permute(): return lax.ppermute(value, axis, [(i, i ^ step) for i in range(count)])  14.7 us
    pallas_call x2, Pallas kernels, update_call(): pl.pallas_call(kernel, out_shape=out_shape, in_specs=[pl.BlockSpec(memory...  9.34 us
    unnamed x27, local copies, waits for them, and re-layouts  6 us
    pallas_call x1, Pallas kernels, spread(): pl.pallas_call(functools.partial(spread_kernel, tile), out_shape=[jax.Sha...  4.81 us
    ppermute x1, starting transfers between devices, shards(): outer = lax.ppermute(outer, 'dom', pairs + [(j, i) for i, j in pairs])  4.12 us
    pallas_call x1, Pallas kernels, early(): pl.pallas_call(functools.partial(early_kernel, begin, end, tile), out_sha...  3.01 us
    pallas_call x1, Pallas kernels, latent_grad(): pl.pallas_call(latent_kernel, out_shape=jax.ShapeDtypeStruct((1, tiles *...  2.04 us
  transfers between devices with their start and end apart: 18, of which 9 were waited for; matrix products, arithmetic and copies ran while one was open for 0% of the time, Pallas kernels for 23%

profile of v2, /device:TPU:24, one launch (start us, length us, event | category | flops | bytes accessed | tf_op | source)
XLA Modules:
  0.0 72.2 jit_solution(14973939785178856358)
XLA Ops:
  0.6 1.2 %copy-done.4 = bf16[1,512,512]{2,1,0:T(8,128)(2,1)S(1)} copy-done((bf16[1,512,512]{2,1,0:T(8,128)(2,1)S(1)}, bf16[1,512,512]{2,1,0:T(8,128)(2,1)}, u32[]{:S(2)}) %copy-start.4) | copy-done | bytes 524312
  1.8 0.7 copy-done.11
  2.5 0.9 %pick.1 = (bf16[128,512]{1,0:T(8,128)(2,1)S(1)}, bf16[128,512]{1,0:T(8,128)(2,1)S(1)}, bf16[128,512]{1,0:T(8,128)(2,1)S(1)}, bf16[128,512]{1,0:T(8,128)(2,1)S(1)...) custom-call(s32[1,8,128]{2,1,0:T(8,128)S(1)} %copy-done.11, ...), custom_call_target="tpu_custom_call" | custom-call | flops 536870912 | bytes 2097152 | tf_op jit(solution)/shard_map/pick/pallas_call | solution.py:73
  3.5 0.1 collective-permute-start
  3.5 0.5 collective-permute-start.1
  4.1 1.4 %collective-permute-start.2 = (bf16[128,512]{1,0:T(8,128)(2,1)S(1)}, bf16[128,512]{1,0:T(8,128)(2,1)S(1)}, u32[]{:S(2)}, u32[]{:S(2)}) collective-permute-start(bf16[128,512]{1,0:T(8,128)(2,1)S(1)} %get-tuple-element.34), channel_id=1, source_target_pairs={{0,12},{4,8},{8,4},{12,0},{16,28},{20,24},{24,20},{28,16},{1,13},{... | collective-permute-start | bytes 393224 | tf_op jit(solution)/shard_map/ppermute | solution.py:47
  5.4 0.3 collective-permute-start.3
  5.7 2.3 %collective-permute-start.4 = (bf16[128,512]{1,0:T(8,128)(2,1)S(1)}, bf16[128,512]{1,0:T(8,128)(2,1)S(1)}, u32[]{:S(2)}, u32[]{:S(2)}) collective-permute-start(bf16[128,512]{1,0:T(8,128)(2,1)S(1)} %get-tuple-element.36), channel_id=1, source_target_pairs={{0,20},{4,16},{8,28},{12,24},{16,4},{20,0},{24,12},{28,8},{1,21},{... | collective-permute-start | bytes 393224 | tf_op jit(solution)/shard_map/ppermute | solution.py:47
  8.0 0.9 %copy-done.6 = bf16[512,83]{0,1:T(8,128)(2,1)S(1)} copy-done((bf16[512,83]{0,1:T(8,128)(2,1)S(1)}, bf16[512,83]{0,1:T(8,128)(2,1)}, u32[]{:S(2)}) %copy-start.6) | copy-done | bytes 85016
  8.9 0.8 %copy-done.7 = s32[6,2048]{1,0:T(8,128)S(1)} copy-done((s32[6,2048]{1,0:T(8,128)S(1)}, s32[6,2048]{1,0:T(8,128)}, u32[]{:S(2)}) %copy-start.7) | copy-done | bytes 49176
  9.7 0.8 %copy-done.8 = s32[3,2048]{1,0:T(4,128)S(1)} copy-done((s32[3,2048]{1,0:T(4,128)S(1)}, s32[3,2048]{1,0:T(4,128)}, u32[]{:S(2)}) %copy-start.8) | copy-done | bytes 24600
  10.5 0.8 %copy-done.9 = f32[3,2048]{1,0:T(4,128)S(1)} copy-done((f32[3,2048]{1,0:T(4,128)S(1)}, f32[3,2048]{1,0:T(4,128)}, u32[]{:S(2)}) %copy-start.9) | copy-done | bytes 24600
  11.2 4.8 %spread.1 = (bf16[2048,1024]{1,0:T(8,128)(2,1)S(1)}, bf16[8,256,512]{2,1,0:T(8,128)(2,1)S(1)}, bf16[96,512]{1,0:T(8,128)(2,1)S(1)}) custom-call(s32[3,2048]{1,0:T(4,128)S(1)} %copy-done.8, f32[3,2048]{1,0:T(4,128)S(1)} %copy-done.9, s32[6,2048]{1,0:T(8,128)S(1)} %copy-done.7, bf16[83,512]{1,0:T(8,128)(2,1)S(1)} %bitcast.8), custom_call_target="tpu_custom_call" | custom-call | flops 83886080 | bytes 8388608 | tf_op jit(solution)/shard_map/spread/pallas_call | solution.py:127
  16.1 0.3 collective-permute-start.5
  16.4 3.4 %collective-permute-start.6 = (bf16[128,512]{1,0:T(8,128)(2,1)S(1)}, bf16[128,512]{1,0:T(8,128)(2,1)S(1)}, u32[]{:S(2)}, u32[]{:S(2)}) collective-permute-start(bf16[128,512]{1,0:T(8,128)(2,1)S(1)} %get-tuple-element.38), channel_id=1, source_target_pairs={{0,28},{4,24},{8,20},{12,16},{16,12},{20,8},{24,4},{28,0},{1,29},{... | collective-permute-start | bytes 393224 | tf_op jit(solution)/shard_map/ppermute | solution.py:47
  19.7 0.2 collective-permute-done.4.refs_5_
  20.0 3.0 %early.1.sum_ref = f32[2048,512]{1,0:T(8,128)S(1)} custom-call(bf16[2048,1024]{1,0:T(8,128)(2,1)S(1)} %get-tuple-element.30.spread_ref, bf16[2048,512]{1,0:T(8,128)(2,1)S(1)} %copy-done, bf16[128,512]{1,0:T(8,128)(2,1)S(1)} %get-tuple-element.31.refs_0_, bf16[128,512]{1,0:T(8,128)(2,1)S(1)} %collective-permute-done.refs_1_, ...), custom_call_target="tpu_custom_call" | custom-call | flops 1610612736 | bytes 8388608 | tf_op jit(solution)/shard_map/early/pallas_call | solution.py:157
  23.0 0.0 copy-start.1
  23.0 0.0 copy-start.2
  23.0 0.0 copy-start.3
  23.0 1.3 %collective-permute-done.5.refs_0_ = bf16[128,512]{1,0:T(8,128)(2,1)S(1)} collective-permute-done((bf16[128,512]{1,0:T(8,128)(2,1)S(1)}, bf16[128,512]{1,0:T(8,128)(2,1)S(1)}, u32[]{:S(2)}, u32[]{:S(2)}) %collective-permute-start.5) | collective-permute-done | bytes 131104 | tf_op jit(solution)/shard_map/ppermute | solution.py:47
  24.3 1.9 %collective-permute-done.6.refs_1_ = bf16[128,512]{1,0:T(8,128)(2,1)S(1)} collective-permute-done((bf16[128,512]{1,0:T(8,128)(2,1)S(1)}, bf16[128,512]{1,0:T(8,128)(2,1)S(1)}, u32[]{:S(2)}, u32[]{:S(2)}) %collective-permute-start.6) | collective-permute-done | bytes 131104 | tf_op jit(solution)/shard_map/ppermute | solution.py:47
  26.2 1.9 %late.1 = (bf16[2048,512]{1,0:T(8,128)(2,1)S(1)}, bf16[128,512]{1,0:T(8,128)(2,1)S(1)}, bf16[128,512]{1,0:T(8,128)(2,1)S(1)}) custom-call(f32[2048,512]{1,0:T(8,128)S(1)} %early.1.sum_ref, bf16[2048,1024]{1,0:T(8,128)(2,1)S(1)} %get-tuple-element.30.spread_ref, bf16[128,512]{1,0:T(8,128)(2,1)S(1)} %collective-permute-done.5.refs_0_, ...), custom_call_target="tpu_custom_call" | custom-call | flops 536870912 | bytes 8388608 | tf_op jit(solution)/shard_map/late/pallas_call | solution.py:189
  28.2 3.4 %collective-permute-start.7 = (bf16[128,512]{1,0:T(8,128)(2,1)S(1)}, bf16[128,512]{1,0:T(8,128)(2,1)S(1)}, u32[]{:S(2)}, u32[]{:S(2)}) collective-permute-start(bf16[128,512]{1,0:T(8,128)(2,1)S(1)} %get-tuple-element.42), channel_id=1, source_target_pairs={{0,4},{4,0},{8,12},{12,8},{16,20},{20,16},{24,28},{28,24},{1,5},{5... | collective-permute-start | bytes 393224 | tf_op jit(solution)/shard_map/ppermute | solution.py:47
  31.6 4.1 %collective-permute-start.8 = (bf16[128,512]{1,0:T(8,128)(2,1)S(1)}, bf16[128,512]{1,0:T(8,128)(2,1)S(1)}, u32[]{:S(2)}, u32[]{:S(2)}) collective-permute-start(bf16[128,512]{1,0:T(8,128)(2,1)S(1)} %get-tuple-element.43), channel_id=1, source_target_pairs={{4,8},{12,16},{20,24},{8,4},{16,12},{24,20},{5,9},{13,17},{21,25},... | collective-permute-start | bytes 393224 | tf_op jit(solution)/shard_map/ppermute | solution.py:439
  35.8 6.8 %inner.1 = (bf16[1536,512]{1,0:T(8,128)(2,1)S(1)}, bf16[6,96,256]{2,1,0:T(8,128)(2,1)S(1)}) custom-call(bf16[2048,512]{1,0:T(8,128)(2,1)S(1)} %get-tuple-element.39.x_ref, bf16[8,256,512]{2,1,0:T(8,128)(2,1)S(1)} %get-tuple-element.40.count_ref, bf16[1024,512]{1,0:T(8,128)(2,1)S(1)} %copy-done.1, bf16[512,512]{1,0:T(8,128)(2,1)S(1)} %copy-done.2, ...), custom_call_target="tpu_custom_call" | custom-call | flops 4026531840 | bytes 8388608 | tf_op jit(solution)/shard_map/inner/pallas_call | solution.py:248
  42.6 0.0 copy-start.5
  42.7 2.5 %outer.1 = (bf16[512,512]{1,0:T(8,128)(2,1)S(1)}, bf16[96,512]{1,0:T(8,128)(2,1)S(1)}, bf16[96,512]{1,0:T(8,128)(2,1)S(1)}, bf16[96,512]{1,0:T(8,128)(2,1)S(1)}, bf16[96,512]{1,0:T(8,128)(2,1)S(1)}) custom-call(bf16[2048,512]{1,0:T(8,128)(2,1)S(1)} %get-tuple-element.39.x_ref, bf16[8,256,512]{2,1,0:T(8,128)(2,1)S(1)} %get-tuple-element.40.count_ref, ...), custom_call_target="tpu_custom_call" | custom-call | flops 1342177280 | bytes 8388608 | tf_op jit(solution)/shard_map/outer/pallas_call | solution.py:248
  45.2 1.6 %collective-permute-start.10 = (bf16[96,512]{1,0:T(8,128)(2,1)S(1)}, bf16[96,512]{1,0:T(8,128)(2,1)S(1)}, u32[]{:S(2)}, u32[]{:S(2)}) collective-permute-start(bf16[96,512]{1,0:T(8,128)(2,1)S(1)} %get-tuple-element.48), channel_id=1, source_target_pairs={{0,2},{1,3},{2,0},{3,1},{4,6},{5,7},{6,4},{7,5},{8,10},{9,11},{10,... | collective-permute-start | bytes 294920 | tf_op jit(solution)/shard_map/ppermute | solution.py:47
  46.8 1.4 %collective-permute-start.11 = (bf16[96,512]{1,0:T(8,128)(2,1)S(1)}, bf16[96,512]{1,0:T(8,128)(2,1)S(1)}, u32[]{:S(2)}, u32[]{:S(2)}) collective-permute-start(bf16[96,512]{1,0:T(8,128)(2,1)S(1)} %get-tuple-element.49), channel_id=1, source_target_pairs={{0,3},{1,2},{2,1},{3,0},{4,7},{5,6},{6,5},{7,4},{8,11},{9,10},{10,... | collective-permute-start | bytes 294920 | tf_op jit(solution)/shard_map/ppermute | solution.py:47
  48.2 0.5 collective-permute-start.9
  49.4 0.5 collective-permute-done.10.refs_2_
  49.9 2.5 %collective-permute-done.11.refs_3_ = bf16[96,512]{1,0:T(8,128)(2,1)S(1)} collective-permute-done((bf16[96,512]{1,0:T(8,128)(2,1)S(1)}, bf16[96,512]{1,0:T(8,128)(2,1)S(1)}, u32[]{:S(2)}, u32[]{:S(2)}) %collective-permute-start.11) | collective-permute-done | bytes 98336 | tf_op jit(solution)/shard_map/ppermute | solution.py:47
  52.3 1.2 %collective-permute-done.9.refs_1_ = bf16[96,512]{1,0:T(8,128)(2,1)S(1)} collective-permute-done((bf16[96,512]{1,0:T(8,128)(2,1)S(1)}, bf16[96,512]{1,0:T(8,128)(2,1)S(1)}, u32[]{:S(2)}, u32[]{:S(2)}) %collective-permute-start.9) | collective-permute-done | bytes 98336 | tf_op jit(solution)/shard_map/ppermute | solution.py:47
  53.5 1.1 %score.1 = (bf16[96,512]{1,0:T(8,128)(2,1)S(1)}, bf16[96,512]{1,0:T(8,128)(2,1)S(1)}, bf16[96,512]{1,0:T(8,128)(2,1)S(1)}, bf16[96,512]{1,0:T(8,128)(2,1)S(1)}) custom-call(s32[1]{0:T(128)S(6)} %copy.17.live_ref, f32[1,83]{1,0:T(1,128)S(1)} %bitcast.10, f32[1,2048]{1,0:T(1,128)S(1)} %bitcast.9, bf16[83,2048]{1,0:T(8,128)(2,1)S(1)} %copy-done.5, ...), custom_call_target="tpu_custom_call" | custom-call | flops 7864320 | bytes 1048576 | tf_op jit(solution)/shard_map/score/pallas_call | solution.py:317
  54.6 1.6 %collective-permute-start.12 = (bf16[96,512]{1,0:T(8,128)(2,1)S(1)}, bf16[96,512]{1,0:T(8,128)(2,1)S(1)}, u32[]{:S(2)}, u32[]{:S(2)}) collective-permute-start(bf16[96,512]{1,0:T(8,128)(2,1)S(1)} %get-tuple-element.51), channel_id=1, source_target_pairs={{0,1},{1,0},{2,3},{3,2},{4,5},{5,4},{6,7},{7,6},{8,9},{9,8},{10,11... | collective-permute-start | bytes 294920 | tf_op jit(solution)/shard_map/ppermute | solution.py:47
  56.2 1.5 %collective-permute-start.13 = (bf16[96,512]{1,0:T(8,128)(2,1)S(1)}, bf16[96,512]{1,0:T(8,128)(2,1)S(1)}, u32[]{:S(2)}, u32[]{:S(2)}) collective-permute-start(bf16[96,512]{1,0:T(8,128)(2,1)S(1)} %get-tuple-element.52), channel_id=1, source_target_pairs={{0,2},{1,3},{2,0},{3,1},{4,6},{5,7},{6,4},{7,5},{8,10},{9,11},{10,... | collective-permute-start | bytes 294920 | tf_op jit(solution)/shard_map/ppermute | solution.py:47
  57.7 0.4 collective-permute-start.14
  58.1 1.9 %collective-permute-done.12.refs_1_ = bf16[96,512]{1,0:T(8,128)(2,1)S(1)} collective-permute-done((bf16[96,512]{1,0:T(8,128)(2,1)S(1)}, bf16[96,512]{1,0:T(8,128)(2,1)S(1)}, u32[]{:S(2)}, u32[]{:S(2)}) %collective-permute-start.12) | collective-permute-done | bytes 98336 | tf_op jit(solution)/shard_map/ppermute | solution.py:47
  60.0 3.9 %collective-permute-done.13.refs_2_ = bf16[96,512]{1,0:T(8,128)(2,1)S(1)} collective-permute-done((bf16[96,512]{1,0:T(8,128)(2,1)S(1)}, bf16[96,512]{1,0:T(8,128)(2,1)S(1)}, u32[]{:S(2)}, u32[]{:S(2)}) %collective-permute-start.13) | collective-permute-done | bytes 98336 | tf_op jit(solution)/shard_map/ppermute | solution.py:47
  63.8 0.5 head_terms.1
  64.3 0.5 collective-permute-start.15
  64.8 1.0 %collective-permute-start.16 = (bf16[96,512]{1,0:T(8,128)(2,1)S(1)}, bf16[96,512]{1,0:T(8,128)(2,1)S(1)}, u32[]{:S(2)}, u32[]{:S(2)}) collective-permute-start(bf16[96,512]{1,0:T(8,128)(2,1)S(1)} %get-tuple-element.55.refs_0_), channel_id=1, source_target_pairs={{0,2},{1,3},{2,0},{3,1},{4,6},{5,7},{6,4},{7,5},{8,10},{9,11},{10,... | collective-permute-start | bytes 294920 | tf_op jit(solution)/shard_map/ppermute | solution.py:47
  65.8 2.1 %collective-permute-start.17 = (bf16[96,512]{1,0:T(8,128)(2,1)S(1)}, bf16[96,512]{1,0:T(8,128)(2,1)S(1)}, u32[]{:S(2)}, u32[]{:S(2)}) collective-permute-start(bf16[96,512]{1,0:T(8,128)(2,1)S(1)} %get-tuple-element.55.refs_0_), channel_id=1, source_target_pairs={{0,3},{1,2},{2,1},{3,0},{4,7},{5,6},{6,5},{7,4},{8,11},{9,10},{10,... | collective-permute-start | bytes 294920 | tf_op jit(solution)/shard_map/ppermute | solution.py:47
  67.9 2.0 %latent_grad.1 = bf16[1,2048,512]{2,1,0:T(8,128)(2,1)} custom-call(bf16[96,512]{1,0:T(8,128)(2,1)S(1)} %get-tuple-element.29.head_ref, bf16[8,96,256]{2,1,0:T(8,128)(2,1)S(1)} %get-tuple-element.54.score_ref), custom_call_target="tpu_custom_call" | custom-call | flops 201326592 | bytes 3145728 | tf_op jit(solution)/shard_map/latent_grad/pallas_call | solution.py:371
  69.9 1.4 %collective-permute-done.17.refs_3_ = bf16[96,512]{1,0:T(8,128)(2,1)S(1)} collective-permute-done((bf16[96,512]{1,0:T(8,128)(2,1)S(1)}, bf16[96,512]{1,0:T(8,128)(2,1)S(1)}, u32[]{:S(2)}, u32[]{:S(2)}) %collective-permute-start.17) | collective-permute-done | bytes 98336 | tf_op jit(solution)/shard_map/ppermute | solution.py:47
  71.3 0.1 head_total.1
  71.4 0.8 %copy.16 = f32[1,512,83]{1,0,2:T(1,128)} copy(f32[1,512,83]{1,2,0:T(8,128)S(1)} %bitcast.5) | data formatting | bytes 339968
  (25 shorter events, 0.1 us)
Async XLA Ops:
  0.6 19.3 %copy-start = (bf16[2048,512]{1,0:T(8,128)(2,1)S(1)}, bf16[2048,512]{1,0:T(8,128)(2,1)}, u32[]{:S(2)}) copy-start(bf16[2048,512]{1,0:T(8,128)(2,1)} %skip_ref.1) | copy-start | bytes 6291460
  0.6 1.2 %copy-start.4 = (bf16[1,512,512]{2,1,0:T(8,128)(2,1)S(1)}, bf16[1,512,512]{2,1,0:T(8,128)(2,1)}, u32[]{:S(2)}) copy-start(bf16[1,512,512]{2,1,0:T(8,128)(2,1)} %coarse_ref.1) | copy-start | bytes 1572868
  1.8 0.7 copy-start.11
  3.5 12.6 %collective-permute-start = (bf16[128,512]{1,0:T(8,128)(2,1)S(1)}, bf16[128,512]{1,0:T(8,128)(2,1)S(1)}, u32[]{:S(2)}, u32[]{:S(2)}) collective-permute-start(bf16[128,512]{1,0:T(8,128)(2,1)S(1)} %get-tuple-element.32), channel_id=1, source_target_pairs={{0,4},{4,0},{8,12},{12,8},{16,20},{20,16},{24,28},{28,24},{1,5},{5... | collective-permute-start | bytes 393224 | tf_op jit(solution)/shard_map/ppermute | solution.py:47
  3.5 12.8 %collective-permute-start.1 = (bf16[128,512]{1,0:T(8,128)(2,1)S(1)}, bf16[128,512]{1,0:T(8,128)(2,1)S(1)}, u32[]{:S(2)}, u32[]{:S(2)}) collective-permute-start(bf16[128,512]{1,0:T(8,128)(2,1)S(1)} %get-tuple-element.33), channel_id=1, source_target_pairs={{0,8},{4,12},{8,0},{12,4},{16,24},{20,28},{24,16},{28,20},{1,9},{5... | collective-permute-start | bytes 393224 | tf_op jit(solution)/shard_map/ppermute | solution.py:47
  4.1 15.7 %collective-permute-start.2 = (bf16[128,512]{1,0:T(8,128)(2,1)S(1)}, bf16[128,512]{1,0:T(8,128)(2,1)S(1)}, u32[]{:S(2)}, u32[]{:S(2)}) collective-permute-start(bf16[128,512]{1,0:T(8,128)(2,1)S(1)} %get-tuple-element.34), channel_id=1, source_target_pairs={{0,12},{4,8},{8,4},{12,0},{16,28},{20,24},{24,20},{28,16},{1,13},{... | collective-permute-start | bytes 393224 | tf_op jit(solution)/shard_map/ppermute | solution.py:47
  5.4 14.3 %collective-permute-start.3 = (bf16[128,512]{1,0:T(8,128)(2,1)S(1)}, bf16[128,512]{1,0:T(8,128)(2,1)S(1)}, u32[]{:S(2)}, u32[]{:S(2)}) collective-permute-start(bf16[128,512]{1,0:T(8,128)(2,1)S(1)} %get-tuple-element.35), channel_id=1, source_target_pairs={{0,16},{4,20},{8,24},{12,28},{16,0},{20,4},{24,8},{28,12},{1,17},{... | collective-permute-start | bytes 393224 | tf_op jit(solution)/shard_map/ppermute | solution.py:47
  5.7 14.2 %collective-permute-start.4 = (bf16[128,512]{1,0:T(8,128)(2,1)S(1)}, bf16[128,512]{1,0:T(8,128)(2,1)S(1)}, u32[]{:S(2)}, u32[]{:S(2)}) collective-permute-start(bf16[128,512]{1,0:T(8,128)(2,1)S(1)} %get-tuple-element.36), channel_id=1, source_target_pairs={{0,20},{4,16},{8,28},{12,24},{16,4},{20,0},{24,12},{28,8},{1,21},{... | collective-permute-start | bytes 393224 | tf_op jit(solution)/shard_map/ppermute | solution.py:47
  8.0 0.9 %copy-start.6 = (bf16[512,83]{0,1:T(8,128)(2,1)S(1)}, bf16[512,83]{0,1:T(8,128)(2,1)}, u32[]{:S(2)}) copy-start(bf16[512,83]{0,1:T(8,128)(2,1)} %param.27) | copy-start | bytes 254980
  8.9 0.8 %copy-start.7 = (s32[6,2048]{1,0:T(8,128)S(1)}, s32[6,2048]{1,0:T(8,128)}, u32[]{:S(2)}) copy-start(s32[6,2048]{1,0:T(8,128)} %nb_ref.1) | copy-start | bytes 147460
  9.7 0.8 %copy-start.8 = (s32[3,2048]{1,0:T(4,128)S(1)}, s32[3,2048]{1,0:T(4,128)}, u32[]{:S(2)}) copy-start(s32[3,2048]{1,0:T(4,128)} %index_ref.1) | copy-start | bytes 73732
  10.5 0.8 %copy-start.9 = (f32[3,2048]{1,0:T(4,128)S(1)}, f32[3,2048]{1,0:T(4,128)}, u32[]{:S(2)}) copy-start(f32[3,2048]{1,0:T(4,128)} %weight_ref.1) | copy-start | bytes 73732
  16.1 8.3 %collective-permute-start.5 = (bf16[128,512]{1,0:T(8,128)(2,1)S(1)}, bf16[128,512]{1,0:T(8,128)(2,1)S(1)}, u32[]{:S(2)}, u32[]{:S(2)}) collective-permute-start(bf16[128,512]{1,0:T(8,128)(2,1)S(1)} %get-tuple-element.37), channel_id=1, source_target_pairs={{0,24},{4,28},{8,16},{12,20},{16,8},{20,12},{24,0},{28,4},{1,25},{... | collective-permute-start | bytes 393224 | tf_op jit(solution)/shard_map/ppermute | solution.py:47
  16.4 9.9 %collective-permute-start.6 = (bf16[128,512]{1,0:T(8,128)(2,1)S(1)}, bf16[128,512]{1,0:T(8,128)(2,1)S(1)}, u32[]{:S(2)}, u32[]{:S(2)}) collective-permute-start(bf16[128,512]{1,0:T(8,128)(2,1)S(1)} %get-tuple-element.38), channel_id=1, source_target_pairs={{0,28},{4,24},{8,20},{12,16},{16,12},{20,8},{24,4},{28,0},{1,29},{... | collective-permute-start | bytes 393224 | tf_op jit(solution)/shard_map/ppermute | solution.py:47
  23.0 12.8 %copy-start.1 = (bf16[1024,512]{1,0:T(8,128)(2,1)S(1)}, bf16[1024,512]{1,0:T(8,128)(2,1)}, u32[]{:S(2)}) copy-start(bf16[1024,512]{1,0:T(8,128)(2,1)} %w_in_ref.3) | copy-start | bytes 3145732
  23.0 12.8 %copy-start.2 = (bf16[512,512]{1,0:T(8,128)(2,1)S(1)}, bf16[512,512]{1,0:T(8,128)(2,1)}, u32[]{:S(2)}) copy-start(bf16[512,512]{1,0:T(8,128)(2,1)} %w_out_ref.3) | copy-start | bytes 1572868
  23.0 12.8 %copy-start.3 = (f32[512]{0:T(512)S(1)}, f32[512]{0:T(512)}, u32[]{:S(2)}) copy-start(f32[512]{0:T(512)} %param.26) | copy-start | bytes 6148
  28.2 14.4 %collective-permute-start.7 = (bf16[128,512]{1,0:T(8,128)(2,1)S(1)}, bf16[128,512]{1,0:T(8,128)(2,1)S(1)}, u32[]{:S(2)}, u32[]{:S(2)}) collective-permute-start(bf16[128,512]{1,0:T(8,128)(2,1)S(1)} %get-tuple-element.42), channel_id=1, source_target_pairs={{0,4},{4,0},{8,12},{12,8},{16,20},{20,16},{24,28},{28,24},{1,5},{5... | collective-permute-start | bytes 393224 | tf_op jit(solution)/shard_map/ppermute | solution.py:47
  31.6 11.0 %collective-permute-start.8 = (bf16[128,512]{1,0:T(8,128)(2,1)S(1)}, bf16[128,512]{1,0:T(8,128)(2,1)S(1)}, u32[]{:S(2)}, u32[]{:S(2)}) collective-permute-start(bf16[128,512]{1,0:T(8,128)(2,1)S(1)} %get-tuple-element.43), channel_id=1, source_target_pairs={{4,8},{12,16},{20,24},{8,4},{16,12},{24,20},{5,9},{13,17},{21,25},... | collective-permute-start | bytes 393224 | tf_op jit(solution)/shard_map/ppermute | solution.py:439
  42.6 10.8 %copy-start.5 = (bf16[83,2048]{1,0:T(8,128)(2,1)S(1)}, bf16[83,2048]{1,0:T(8,128)(2,1)}, u32[]{:S(2)}) copy-start(bf16[83,2048]{1,0:T(8,128)(2,1)} %target_ref.1) | copy-start | bytes 1019908
  42.6 10.8 %copy-start.10 = (f32[2048]{0:T(1024)S(1)}, f32[2048]{0:T(1024)}, u32[]{:S(2)}) copy-start(f32[2048]{0:T(1024)} %param.20) | copy-start | bytes 24580
  42.7 10.8 %copy-start.12 = (f32[83]{0:T(128)S(1)}, f32[83]{0:T(128)}, u32[]{:S(2)}) copy-start(f32[83]{0:T(128)} %param.23) | copy-start | bytes 1000
  45.2 4.7 %collective-permute-start.10 = (bf16[96,512]{1,0:T(8,128)(2,1)S(1)}, bf16[96,512]{1,0:T(8,128)(2,1)S(1)}, u32[]{:S(2)}, u32[]{:S(2)}) collective-permute-start(bf16[96,512]{1,0:T(8,128)(2,1)S(1)} %get-tuple-element.48), channel_id=1, source_target_pairs={{0,2},{1,3},{2,0},{3,1},{4,6},{5,7},{6,4},{7,5},{8,10},{9,11},{10,... | collective-permute-start | bytes 294920 | tf_op jit(solution)/shard_map/ppermute | solution.py:47
  46.8 5.5 %collective-permute-start.11 = (bf16[96,512]{1,0:T(8,128)(2,1)S(1)}, bf16[96,512]{1,0:T(8,128)(2,1)S(1)}, u32[]{:S(2)}, u32[]{:S(2)}) collective-permute-start(bf16[96,512]{1,0:T(8,128)(2,1)S(1)} %get-tuple-element.49), channel_id=1, source_target_pairs={{0,3},{1,2},{2,1},{3,0},{4,7},{5,6},{6,5},{7,4},{8,11},{9,10},{10,... | collective-permute-start | bytes 294920 | tf_op jit(solution)/shard_map/ppermute | solution.py:47
  48.2 5.3 %collective-permute-start.9 = (bf16[96,512]{1,0:T(8,128)(2,1)S(1)}, bf16[96,512]{1,0:T(8,128)(2,1)S(1)}, u32[]{:S(2)}, u32[]{:S(2)}) collective-permute-start(bf16[96,512]{1,0:T(8,128)(2,1)S(1)} %get-tuple-element.47), channel_id=1, source_target_pairs={{0,1},{1,0},{2,3},{3,2},{4,5},{5,4},{6,7},{7,6},{8,9},{9,8},{10,11... | collective-permute-start | bytes 294920 | tf_op jit(solution)/shard_map/ppermute | solution.py:47
  54.6 5.4 %collective-permute-start.12 = (bf16[96,512]{1,0:T(8,128)(2,1)S(1)}, bf16[96,512]{1,0:T(8,128)(2,1)S(1)}, u32[]{:S(2)}, u32[]{:S(2)}) collective-permute-start(bf16[96,512]{1,0:T(8,128)(2,1)S(1)} %get-tuple-element.51), channel_id=1, source_target_pairs={{0,1},{1,0},{2,3},{3,2},{4,5},{5,4},{6,7},{7,6},{8,9},{9,8},{10,11... | collective-permute-start | bytes 294920 | tf_op jit(solution)/shard_map/ppermute | solution.py:47
  56.2 7.6 %collective-permute-start.13 = (bf16[96,512]{1,0:T(8,128)(2,1)S(1)}, bf16[96,512]{1,0:T(8,128)(2,1)S(1)}, u32[]{:S(2)}, u32[]{:S(2)}) collective-permute-start(bf16[96,512]{1,0:T(8,128)(2,1)S(1)} %get-tuple-element.52), channel_id=1, source_target_pairs={{0,2},{1,3},{2,0},{3,1},{4,6},{5,7},{6,4},{7,5},{8,10},{9,11},{10,... | collective-permute-start | bytes 294920 | tf_op jit(solution)/shard_map/ppermute | solution.py:47
  57.7 6.1 %collective-permute-start.14 = (bf16[96,512]{1,0:T(8,128)(2,1)S(1)}, bf16[96,512]{1,0:T(8,128)(2,1)S(1)}, u32[]{:S(2)}, u32[]{:S(2)}) collective-permute-start(bf16[96,512]{1,0:T(8,128)(2,1)S(1)} %get-tuple-element.53), channel_id=1, source_target_pairs={{0,3},{1,2},{2,1},{3,0},{4,7},{5,6},{6,5},{7,4},{8,11},{9,10},{10,... | collective-permute-start | bytes 294920 | tf_op jit(solution)/shard_map/ppermute | solution.py:47
  64.3 5.6 %collective-permute-start.15 = (bf16[96,512]{1,0:T(8,128)(2,1)S(1)}, bf16[96,512]{1,0:T(8,128)(2,1)S(1)}, u32[]{:S(2)}, u32[]{:S(2)}) collective-permute-start(bf16[96,512]{1,0:T(8,128)(2,1)S(1)} %get-tuple-element.55.refs_0_), channel_id=1, source_target_pairs={{0,1},{1,0},{2,3},{3,2},{4,5},{5,4},{6,7},{7,6},{8,9},{9,8},{10,11... | collective-permute-start | bytes 294920 | tf_op jit(solution)/shard_map/ppermute | solution.py:47
  64.8 5.1 %collective-permute-start.16 = (bf16[96,512]{1,0:T(8,128)(2,1)S(1)}, bf16[96,512]{1,0:T(8,128)(2,1)S(1)}, u32[]{:S(2)}, u32[]{:S(2)}) collective-permute-start(bf16[96,512]{1,0:T(8,128)(2,1)S(1)} %get-tuple-element.55.refs_0_), channel_id=1, source_target_pairs={{0,2},{1,3},{2,0},{3,1},{4,6},{5,7},{6,4},{7,5},{8,10},{9,11},{10,... | collective-permute-start | bytes 294920 | tf_op jit(solution)/shard_map/ppermute | solution.py:47
  65.8 5.5 %collective-permute-start.17 = (bf16[96,512]{1,0:T(8,128)(2,1)S(1)}, bf16[96,512]{1,0:T(8,128)(2,1)S(1)}, u32[]{:S(2)}, u32[]{:S(2)}) collective-permute-start(bf16[96,512]{1,0:T(8,128)(2,1)S(1)} %get-tuple-element.55.refs_0_), channel_id=1, source_target_pairs={{0,3},{1,2},{2,1},{3,0},{4,7},{5,6},{6,5},{7,4},{8,11},{9,10},{10,... | collective-permute-start | bytes 294920 | tf_op jit(solution)/shard_map/ppermute | solution.py:47

commit v3 on v2

--- a/solution.py
+++ b/solution.py
@@ -38,6 +38,18 @@
     return rows.T
 
 
+def in_hbm(*values):
+    return [pltpu.with_memory_space_constraint(v, pltpu.HBM) for v in values]
+
+
+def fetch(pairs, sems):
+    copies = [pltpu.make_async_copy(src, dst, sems.at[i]) for i, (src, dst) in enumerate(pairs)]
+    for copy in copies:
+        copy.start()
+    for copy in copies:
+        copy.wait()
+
+
 def slope(diff, inv_sq):
     return -(diff * inv_sq) * jnp.exp(-0.5 * diff * diff * inv_sq)
 
@@ -47,34 +59,37 @@
     return lax.ppermute(value, axis, [(i, i ^ step) for i in range(count)])
 
 
-def pick_kernel(send_ref, coarse_ref, *refs):
+def picked(rows, table, outs):
+    cols = columns(rows.astype(F32))
+    spots = lax.broadcasted_iota(jnp.int32, (rows.shape[1], table.shape[0]), 1).astype(F32)
+    hot = [(cols[:, k : k + 1] == spots).astype(F32).astype(BF16) for k in range(rows.shape[0])]
+    found = dot(jnp.concatenate(hot, axis=0), table).astype(BF16)
+    start = 0
+    for out in outs:
+        out[...] = found[start : start + out.shape[0], :]
+        start += out.shape[0]
+
+
+def send_rows_of(ref, steps):
+    me = lax.axis_index("dom")
+    return jnp.concatenate([ref[0, pl.ds(me ^ s, 1), :] for s in steps], axis=0)
+
+
+def pick_kernel(steps, send_ref, coarse_ref, *refs):
     outs, (rows_ref, table_ref, sems) = refs[:-3], refs[-3:]
-    copies = [
-        pltpu.make_async_copy(send_ref, rows_ref, sems.at[0]),
-        pltpu.make_async_copy(coarse_ref, table_ref, sems.at[1]),
-    ]
-    for copy in copies:
-        copy.start()
-    me = lax.axis_index("dom")
-    copies[0].wait()
-    rows = jnp.concatenate([rows_ref[0, pl.ds(me ^ s, 1), :] for s in range(len(outs))], axis=0)
-    cols = columns(rows.astype(F32))
-    spots = lax.broadcasted_iota(jnp.int32, (rows.shape[1], table_ref.shape[1]), 1).astype(F32)
-    copies[1].wait()
-    table = table_ref[0]
-    for s in reversed(range(len(outs))):
-        hot = (cols[:, s : s + 1] == spots).astype(F32).astype(BF16)
-        outs[s][...] = dot(hot, table).astype(BF16)
-
-
-def pick(send_rows, coarse):
+    fetch([(send_ref, rows_ref), (coarse_ref, table_ref)], sems)
+    picked(send_rows_of(rows_ref, steps), table_ref[0], outs)
+
+
+def pick(send_rows, coarse, groups):
     _, count, slots = send_rows.shape
+    steps = [s for group in groups for s in group]
     width = coarse.shape[2]
     return pl.pallas_call(
-        pick_kernel,
-        out_shape=[jax.ShapeDtypeStruct((slots, width), BF16)] * count,
-        in_specs=[pl.BlockSpec(memory_space=pl.ANY)] * 2,
-        out_specs=[pl.BlockSpec(memory_space=VMEM)] * count,
+        functools.partial(pick_kernel, steps),
+        out_shape=[jax.ShapeDtypeStruct((len(group) * slots, width), BF16) for group in groups],
+        in_specs=[pl.BlockSpec(memory_space=pltpu.HBM)] * 2,
+        out_specs=[pl.BlockSpec(memory_space=VMEM)] * len(groups),
         scratch_shapes=[
             VMEM(send_rows.shape, jnp.int32),
             VMEM(coarse.shape, BF16),
@@ -83,12 +98,29 @@
         compiler_params=params(16),
         cost_estimate=cost(2 * count * slots * coarse.shape[1] * width, 2 * MIB),
         name="pick",
-    )(send_rows, coarse)
-
-
-def spread_kernel(tile, index_ref, weight_ref, nb_ref, head_in_ref, spread_ref, count_ref, head_ref):
+    )(*in_hbm(send_rows, coarse))
+
+
+def best_scale(weight):
+    best = scale = jnp.ones((1, weight.shape[1]), F32)
+    for c in range(16):
+        factor = 1.0 + 0.0017 * c
+        part = weight * (1.0 / factor)
+        miss = part - part.astype(BF16).astype(F32)
+        miss = miss * miss
+        miss = miss[0:1] + miss[1:2] + miss[2:3]
+        scale = jnp.where(miss < best, factor, scale)
+        best = jnp.minimum(miss, best)
+    return scale
+
+
+def spread_kernel(tile, steps, *refs):
+    sources, (first_ref, last_ref, scale_ref, count_ref, head_ref), held, sems = refs[:4], refs[5:10], refs[10:-1], refs[-1]
+    fetch(list(zip(sources, held)), sems)
+    index_ref, weight_ref, nb_ref, head_in_ref = held
     me = lax.axis_index("dom")
-    rows, slots = spread_ref.shape
+    rows, cut = first_ref.shape
+    slots = cut + last_ref.shape[1]
     span = count_ref.shape[2]
     part = 32
     head_ref[...] = jnp.zeros(head_ref.shape, BF16)
@@ -103,139 +135,203 @@
     def step(t, carry):
         start = pl.multiple_of(t * tile, tile)
         lanes = pl.ds(start, tile)
-        index = narrow(index_ref[:, lanes] ^ (me * 128))
-        weight = columns(weight_ref[:, lanes]).astype(BF16)
+        wanted = index_ref[:, lanes]
+        step_of = lax.shift_right_logical(wanted, 7) ^ me
+        place = jnp.zeros(wanted.shape, jnp.int32)
+        for i, s in enumerate(steps):
+            place = jnp.where(step_of == s, i * 128, place)
+        found = place + (wanted & 127)
+        i0, i1, i2 = found[0:1], found[1:2], found[2:3]
+        w = weight_ref[:, lanes]
+        w0, w1, w2 = w[0:1], w[1:2], w[2:3]
+        same01, same02, same12 = i0 == i1, i0 == i2, (i1 == i2) & (i0 != i1)
+        w0 = w0 + jnp.where(same01, w1, 0.0) + jnp.where(same02, w2, 0.0)
+        w1 = jnp.where(same01, 0.0, w1 + jnp.where(same12, w2, 0.0))
+        w2 = jnp.where(same02 | same12, 0.0, w2)
+        i1 = jnp.where(same01, -1, i1)
+        i2 = jnp.where(same02 | same12, -1, i2)
+        index = narrow(jnp.concatenate([i0, i1, i2], axis=0))
+        w = jnp.concatenate([w0, w1, w2], axis=0)
+        scale = best_scale(w)
+        scale_ref[:, lanes] = scale
+        weight = columns(w / scale).astype(BF16)
         near = narrow(nb_ref[:, lanes] - start)
         for r in range(0, tile, part):
+            here = slice(r, r + part)
+            rows_here = pl.ds(pl.multiple_of(start + r, part), part)
             total = jnp.zeros((part, slots), BF16)
-            for k in range(index_ref.shape[0]):
-                total = total + jnp.where(index[r : r + part, k : k + 1] == spots, weight[r : r + part, k : k + 1], zero)
-            spread_ref[pl.ds(pl.multiple_of(start + r, part), part), :] = total
+            for k in range(3):
+                total = jnp.where(index[here, k : k + 1] == spots, weight[here, k : k + 1], total)
+            first_ref[rows_here, :] = total[:, :cut]
+            last_ref[rows_here, :] = total[:, cut:]
             counts = jnp.zeros((part, span), BF16)
             for k in range(nb_ref.shape[0]):
-                counts = counts + jnp.where(near[r : r + part, k : k + 1] == places, one, zero)
-            count_ref[t, r : r + part, :] = counts
+                counts = counts + jnp.where(near[here, k : k + 1] == places, one, zero)
+            count_ref[t, here, :] = counts
         return carry
 
     lax.fori_loop(0, rows // tile, step, 0)
 
 
-def spread(up_index, up_weight, neighbors, head, slots, tile, padded):
+def spread(token, up_index, up_weight, neighbors, head, steps, slots, split, tile, padded):
     rows = up_index.shape[1]
-    steps = rows // tile
+    tiles = rows // tile
     span = tile + 2 * RIM
-    return pl.pallas_call(
-        functools.partial(spread_kernel, tile),
+    cut, total = split * slots, len(steps) * slots
+    return pl.pallas_call(
+        functools.partial(spread_kernel, tile, steps),
         out_shape=[
-            jax.ShapeDtypeStruct((rows, slots), BF16),
-            jax.ShapeDtypeStruct((steps, tile, span), BF16),
+            jax.ShapeDtypeStruct((rows, cut), BF16),
+            jax.ShapeDtypeStruct((rows, total - cut), BF16),
+            jax.ShapeDtypeStruct((1, rows), F32),
+            jax.ShapeDtypeStruct((tiles, tile, span), BF16),
             jax.ShapeDtypeStruct((padded, head.shape[1]), BF16),
         ],
-        in_specs=[pl.BlockSpec(memory_space=VMEM)] * 4,
-        out_specs=[pl.BlockSpec(memory_space=VMEM)] * 3,
-        compiler_params=params(16),
-        cost_estimate=cost(40 * rows * slots, 4 * rows * slots),
+        in_specs=[pl.BlockSpec(memory_space=pltpu.HBM)] * 4 + [pl.BlockSpec(memory_space=VMEM)],
+        out_specs=[pl.BlockSpec(memory_space=VMEM)] * 5,
+        scratch_shapes=[VMEM(v.shape, v.dtype) for v in (up_index, up_weight, neighbors, head)]
+        + [pltpu.SemaphoreType.DMA((4,))],
+        compiler_params=params(16),
+        cost_estimate=cost(1, 1),
         name="spread",
-    )(up_index, up_weight, neighbors, head)
-
-
-def early_kernel(begin, end, tile, spread_ref, skip_ref, *refs):
+    )(*in_hbm(up_index, up_weight, neighbors, head), token)
+
+
+def pack_kernel(other_ref, *refs):
+    count = len(refs) // 2
+    for i in range(count):
+        mine, out = refs[i], refs[count + i]
+        slots = mine.shape[0]
+        out[:slots, :] = mine[...]
+        out[slots:, :] = other_ref[(i + 1) * slots : (i + 2) * slots, :]
+
+
+def pack(other, mine):
+    slots, width = mine[0].shape
+    return pl.pallas_call(
+        pack_kernel,
+        out_shape=[jax.ShapeDtypeStruct((2 * slots, width), BF16)] * len(mine),
+        in_specs=[pl.BlockSpec(memory_space=VMEM)] * (1 + len(mine)),
+        out_specs=[pl.BlockSpec(memory_space=VMEM)] * len(mine),
+        compiler_params=params(16),
+        cost_estimate=cost(1, 1),
+        name="pack",
+    )(other, *mine)
+
+
+def early_kernel(tile, spread_ref, own_ref, one_ref, *refs):
     tables, out = refs[:-1], refs[-1]
-    table = jnp.concatenate([r[...] for r in tables], axis=0)
+    parts = [own_ref[...], one_ref[: own_ref.shape[0], :]] + [r[...] for r in tables]
+    table = jnp.concatenate(parts, axis=0)
 
     def step(t, carry):
         rows = pl.ds(pl.multiple_of(t * tile, tile), tile)
-        out[rows, :] = skip_ref[rows, :].astype(F32) + dot(spread_ref[rows, begin:end], table)
+        out[rows, :] = dot(spread_ref[rows, :], table)
         return carry
 
-    lax.fori_loop(0, out.shape[0] // tile, step, 0)
-
-
-def early(spread_rows, skip, begin, end, tables, tile):
-    rows, width = skip.shape
-    operands = (spread_rows, skip, *tables)
-    return pl.pallas_call(
-        functools.partial(early_kernel, begin, end, tile),
+    lax.fori_loop(0, out.shape[0] // tile, step, 0, unroll=4)
+
+
+def early(spread_rows, tables, tile):
+    rows, width = spread_rows.shape[0], tables[0].shape[1]
+    return pl.pallas_call(
+        functools.partial(early_kernel, tile),
         out_shape=jax.ShapeDtypeStruct((rows, width), F32),
-        in_specs=[pl.BlockSpec(memory_space=VMEM)] * len(operands),
+        in_specs=[pl.BlockSpec(memory_space=VMEM)] * (1 + len(tables)),
         out_specs=pl.BlockSpec(memory_space=VMEM),
         compiler_params=params(16),
-        cost_estimate=cost(2 * rows * (end - begin) * width, 8 * MIB),
+        cost_estimate=cost(1, 1),
         name="early",
-    )(*operands)
-
-
-def late_kernel(begin, end, tile, sum_ref, spread_ref, *refs):
+    )(spread_rows, *tables)
+
+
+def late_kernel(tile, sum_ref, spread_ref, scale_ref, skip_ref, *refs):
     tables, (x_ref, inner_ref, outer_ref) = refs[:-3], refs[-3:]
     table = jnp.concatenate([r[...] for r in tables], axis=0)
     count = x_ref.shape[0]
 
     def step(t, carry):
-        rows = pl.ds(pl.multiple_of(t * tile, tile), tile)
-        x_ref[rows, :] = (sum_ref[rows, :] + dot(spread_ref[rows, begin:end], table)).astype(BF16)
+        start = pl.multiple_of(t * tile, tile)
+        rows = pl.ds(start, tile)
+        scale = columns(scale_ref[:, rows])[:, 0:1]
+        unpooled = scale * (sum_ref[rows, :] + dot(spread_ref[rows, :], table))
+        x_ref[rows, :] = (skip_ref[rows, :].astype(F32) + unpooled).astype(BF16)
         return carry
 
-    lax.fori_loop(0, count // tile, step, 0)
+    lax.fori_loop(0, count // tile, step, 0, unroll=4)
     odd = lax.rem(lax.axis_index("dom"), 2) == 1
     first, last = x_ref[:RIM, :], x_ref[count - RIM :, :]
     inner_ref[...] = jnp.where(odd, first, last)
     outer_ref[...] = jnp.where(odd, last, first)
 
 
-def late(sums, spread_rows, begin, end, tables, tile):
+def late(sums, spread_rows, scale, skip, tables, tile):
     rows, width = sums.shape
-    operands = (sums, spread_rows, *tables)
+    operands = (sums, spread_rows, scale, skip, *tables)
     edge = jax.ShapeDtypeStruct((RIM, width), BF16)
     return pl.pallas_call(
-        functools.partial(late_kernel, begin, end, tile),
+        functools.partial(late_kernel, tile),
         out_shape=[jax.ShapeDtypeStruct((rows, width), BF16), edge, edge],
         in_specs=[pl.BlockSpec(memory_space=VMEM)] * len(operands),
         out_specs=[pl.BlockSpec(memory_space=VMEM)] * 3,
         compiler_params=params(16),
-        cost_estimate=cost(2 * rows * (end - begin) * width, 8 * MIB),
+        cost_estimate=cost(2 * spread_rows.size * width, 8 * MIB),
         name="late",
     )(*operands)
 
 
-def tile_update(x, window, counts, w_in_ref, w_out_ref, gain_ref, head_ref):
-    width = x.shape[1]
-    agg = (dot(counts, window) * (1.0 / 6.0)).astype(BF16)
-    pre = dot(x, w_in_ref[:width, :]) + dot(agg, w_in_ref[width:, :])
-    act = (0.5 * pre * (1.0 + jnp.tanh(0.5 * pre))).astype(BF16)
-    upd = dot(act, w_out_ref[...])
-    mean = jnp.mean(upd, axis=1, keepdims=True)
-    centred = upd - mean
-    var = jnp.mean(centred * centred, axis=1, keepdims=True)
-    h = (x.astype(F32) + centred * lax.rsqrt(var + 1e-05) * gain_ref[...]).astype(BF16)
-    return h, dot_of(head_ref[...], h, 1, 1).astype(BF16)
-
-
-def inner_kernel(x_ref, count_ref, w_in_ref, w_out_ref, gain_ref, head_ref, h_ref, pred_ref):
+def staged_update(x_ref, count_ref, w_in_ref, w_out_ref, gain_ref, head_ref, windows, places, agg_ref, act_ref, h_ref):
+    tile = count_ref.shape[1]
+    width = x_ref.shape[1]
+    spans = [slice(i * tile, (i + 1) * tile) for i in range(len(places))]
+    rows = [slice(t * tile, (t + 1) * tile) for t in places]
+    for here, t, window in zip(spans, places, windows):
+        agg_ref[here, :] = (dot(count_ref[t], window()) * (1.0 / 6.0)).astype(BF16)
+    for here, there in zip(spans, rows):
+        pre = dot(x_ref[there, :], w_in_ref[:width, :]) + dot(agg_ref[here, :], w_in_ref[width:, :])
+        act_ref[here, :] = (0.5 * pre * (1.0 + jnp.tanh(0.5 * pre))).astype(BF16)
+    for here, there in zip(spans, rows):
+        upd = dot(act_ref[here, :], w_out_ref[...])
+        mean = jnp.mean(upd, axis=1, keepdims=True)
+        centred = upd - mean
+        var = jnp.mean(centred * centred, axis=1, keepdims=True)
+        change = centred * lax.rsqrt(var + 1e-05) * gain_ref[...]
+        h_ref[here, :] = (x_ref[there, :].astype(F32) + change).astype(BF16)
+    return [dot_of(head_ref[...], h_ref[here, :], 1, 1).astype(BF16) for here in spans]
+
+
+def inner_kernel(x_ref, count_ref, w_in_ref, w_out_ref, gain_ref, head_ref, h_ref, pred_ref, agg_ref, act_ref):
     tiles, tile, _ = count_ref.shape
-    for t in range(1, tiles - 1):
-        x = x_ref[t * tile : (t + 1) * tile, :]
-        window = x_ref[t * tile - RIM : (t + 1) * tile + RIM, :]
-        h, pred = tile_update(x, window, count_ref[t], w_in_ref, w_out_ref, gain_ref, head_ref)
-        h_ref[(t - 1) * tile : t * tile, :] = h
-        pred_ref[t - 1] = pred
+    places = range(1, tiles - 1)
+
+    def window(t):
+        return lambda: x_ref[t * tile - RIM : (t + 1) * tile + RIM, :]
+
+    preds = staged_update(
+        x_ref, count_ref, w_in_ref, w_out_ref, gain_ref, head_ref,
+        [window(t) for t in places], places, agg_ref, act_ref, h_ref,
+    )
+    for i, pred in enumerate(preds):
+        pred_ref[i] = pred
 
 
 def outer_kernel(members, x_ref, count_ref, w_in_ref, w_out_ref, gain_ref, head_ref, inner_ref, outer_ref, done_ref, h_ref, *refs):
-    outs, all_ref = refs[:-1], refs[-1]
+    outs, (all_ref, agg_ref, act_ref) = refs[:-3], refs[-3:]
     tiles, tile, _ = count_ref.shape
     odd = lax.rem(lax.axis_index("dom"), 2) == 1
     inner, outer = inner_ref[...], outer_ref[...]
     before, after = jnp.where(odd, inner, outer), jnp.where(odd, outer, inner)
     rows = tiles * tile
-    for place, t in enumerate((0, tiles - 1)):
-        x = x_ref[t * tile : (t + 1) * tile, :]
-        if t == 0:
-            window = jnp.concatenate([before, x_ref[: tile + RIM, :]], axis=0)
-        else:
-            window = jnp.concatenate([x_ref[rows - tile - RIM :, :], after], axis=0)
-        h, pred = tile_update(x, window, count_ref[t], w_in_ref, w_out_ref, gain_ref, head_ref)
-        h_ref[place * tile : (place + 1) * tile, :] = h
-        all_ref[t] = pred
+    windows = [
+        lambda: jnp.concatenate([before, x_ref[: tile + RIM, :]], axis=0),
+        lambda: jnp.concatenate([x_ref[rows - tile - RIM :, :], after], axis=0),
+    ]
+    preds = staged_update(
+        x_ref, count_ref, w_in_ref, w_out_ref, gain_ref, head_ref,
+        windows, (0, tiles - 1), agg_ref, act_ref, h_ref,
+    )
+    all_ref[0] = preds[0]
+    all_ref[tiles - 1] = preds[1]
     all_ref[1 : tiles - 1] = done_ref[...]
     me = lax.axis_index("mem")
     per = tiles // members
@@ -269,7 +365,7 @@
             jax.ShapeDtypeStruct(((tiles - 2) * tile, width), BF16),
             jax.ShapeDtypeStruct((tiles - 2, padded, tile), BF16),
         ],
-        [],
+        [VMEM(((tiles - 2) * tile, width), BF16)] * 2,
         (tiles - 2) * tile * width * width * 10,
         "inner",
     )
@@ -278,7 +374,7 @@
         shared + (inner, outer, pred_mid),
         [jax.ShapeDtypeStruct((2 * tile, width), BF16)]
         + [jax.ShapeDtypeStruct((padded, tiles // members * tile), BF16)] * members,
-        [VMEM((tiles, padded, tile), BF16)],
+        [VMEM((tiles, padded, tile), BF16)] + [VMEM((2 * tile, width), BF16)] * 2,
         2 * tile * width * width * 10,
         "outer",
     )
@@ -384,13 +480,13 @@
     total = terms[0][...].astype(F32)
     for term in terms[1:]:
         total = total + term[...].astype(F32)
-    out[0] = (total * scale)[: out.shape[1], :]
+    out[:, 0, :] = (total * scale)[: out.shape[0], :]
 
 
 def head_total(terms, num_vars, scale):
     return pl.pallas_call(
         functools.partial(total_kernel, scale),
-        out_shape=jax.ShapeDtypeStruct((1, num_vars, terms[0].shape[1]), F32),
+        out_shape=jax.ShapeDtypeStruct((num_vars, 1, terms[0].shape[1]), F32),
         in_specs=[pl.BlockSpec(memory_space=VMEM)] * len(terms),
         out_specs=pl.BlockSpec(memory_space=VMEM),
         compiler_params=params(16),
@@ -420,20 +516,21 @@
     slots = send_rows.shape[2]
     rows, width = fine_skip.shape
     num_vars = w_head.shape[1]
-    padded = num_vars + -num_vars % 16
+    padded = num_vars + -num_vars % 8
     tile = min(256, rows // members)
 
-    outgoing = pick(send_rows, coarse_latents)
-    tables = [outgoing[0]] + [None] * (dom_count - 1)
-    for s in range(1, dom_count):
-        tables[s] = xor_permute(outgoing[s], "dom", s)
-
-    spread_rows, counts, head = spread(
-        up_index, up_weight, neighbors, w_head.T, dom_count * slots, tile, padded
+    even = list(range(4, dom_count, 2))
+    groups = [[0], [1] + [s + 1 for s in even], [2], [3]] + [[s] for s in even]
+    steps = list(range(dom_count))
+    own, one, two, three, *far = pick(send_rows, coarse_latents, groups)
+    one = xor_permute(one, "dom", 1)
+    far = [xor_permute(v, "dom", s) for v, s in zip(pack(one, far), even)]
+    two, three = xor_permute(two, "dom", 2), xor_permute(three, "dom", 3)
+    first_rows, last_rows, scale, counts, head = spread(
+        own, up_index, up_weight, neighbors, w_head.T, steps, slots, 4, tile, padded
     )
-    split = dom_count - 2
-    sums = early(spread_rows, fine_skip, 0, split * slots, tables[:split], tile)
-    x, inner, outer = late(sums, spread_rows, split * slots, dom_count * slots, tables[split:], tile)
+    sums = early(first_rows, [own, one, two, three], tile)
+    x, inner, outer = late(sums, last_rows, scale, fine_skip, far, tile)
     inner = xor_permute(inner, "dom", 1)
     pairs = [(i, i + 1) for i in range(1, dom_count - 1, 2)]
     outer = lax.ppermute(outer, "dom", pairs + [(j, i) for i, j in pairs])
@@ -445,8 +542,8 @@
     term, by_tile = head_terms(members, mid, end, scores)
     terms = [term] + [xor_permute(term, "mem", s) for s in range(1, members)]
     grad_latent = latent_grad(head, by_tile)
-    scale = 1.0 / math.sqrt(members * rows)
-    return (grad_latent, head_total(terms, num_vars, scale).transpose(0, 2, 1))
+    factor = 1.0 / math.sqrt(members * rows)
+    return (grad_latent, head_total(terms, num_vars, factor).transpose(1, 2, 0))
 
 
 def solution(mesh):

time: 72.6 us -> 67.5 us (0.930)
  waiting for transfers between devices: 14.7 us -> 21.9 us
  local copies, waits for them, and re-layouts: 6 us -> 0.04 us
  starting transfers between devices: 26.4 us -> 22.7 us
  Pallas kernels: 23.7 us -> 21.2 us
    ppermute x17 -> x15, waiting for transfers between devices: 14.7 us -> 21.9 us  [xor_permute(): return lax.ppermute(value, axis, [(i, i ^ step) for i in range(count)])]
    unnamed x27 -> x14, local copies, waits for them, and re-layouts: 6 us -> 0.04 us
    ppermute x17 -> x15, starting transfers between devices: 22.3 us -> 17.2 us  [xor_permute(): return lax.ppermute(value, axis, [(i, i ^ step) for i in range(count)])]
    pallas_call x2, Pallas kernels: 9.34 us -> 6.1 us  [update_call(): pl.pallas_call(kernel, out_shape=out_shape, in_specs=[pl.BlockSpec(memory...]
    ppermute x1, starting transfers between devices: 4.12 us -> 5.47 us  [shards(): outer = lax.ppermute(outer, 'dom', pairs + [(j, i) for i, j in pairs])]
    pallas_call x4 -> x5, Pallas kernels: 10.7 us -> 10.9 us  [the longest x1 5.76 us: spread(): pl.pallas_call(functools.partial(spread_kernel, tile, steps), out_shape=[...]
  transfers between devices with their start and end apart: 18 -> 16, of which waited for: 9 -> 12; matrix products, arithmetic and copies ran while one was open for 0% -> 0% of each run, Pallas kernels for 23% -> 20%
where the time goes in v3:
time: 67.5 us; the launch traced here: 67.3 us
  starting transfers between devices  22.7 us (34%)
  waiting for transfers between devices  21.9 us (32%)
  Pallas kernels  21.2 us (31%)
  between operations  1.46 us (2%)
    ppermute x15, waiting for transfers between devices, xor_permute(): return lax.ppermute(value, axis, [(i, i ^ step) for i in range(count)])  21.9 us
    ppermute x15, starting transfers between devices, xor_permute(): return lax.ppermute(value, axis, [(i, i ^ step) for i in range(count)])  17.2 us
    pallas_call x2, Pallas kernels, update_call(): pl.pallas_call(kernel, out_shape=out_shape, in_specs=[pl.BlockSpec(memory...  6.1 us
    pallas_call x1, Pallas kernels, spread(): pl.pallas_call(functools.partial(spread_kernel, tile, steps), out_shape=[...  5.76 us
    ppermute x1, starting transfers between devices, shards(): outer = lax.ppermute(outer, 'dom', pairs + [(j, i) for i, j in pairs])  5.47 us
    pallas_call x1, Pallas kernels, latent_grad(): pl.pallas_call(latent_kernel, out_shape=jax.ShapeDtypeStruct((1, tiles *...  2.05 us
    pallas_call x1, Pallas kernels, pick(): pl.pallas_call(functools.partial(pick_kernel, steps), out_shape=[jax.Shap...  1.92 us
    pallas_call x1, Pallas kernels, late(): pl.pallas_call(functools.partial(late_kernel, tile), out_shape=[jax.Shape...  1.74 us
  transfers between devices with their start and end apart: 16, of which 12 were waited for; matrix products, arithmetic and copies ran while one was open for 0% of the time, Pallas kernels for 20%

profile of v3, /device:TPU:24, one launch (start us, length us, event | category | flops | bytes accessed | tf_op | source)
XLA Modules:
  0.0 67.3 jit_solution(11377600845903029702)
XLA Ops:
  0.6 1.9 %pick.1 = (bf16[128,512]{1,0:T(8,128)(2,1)S(1)}, bf16[384,512]{1,0:T(8,128)(2,1)S(1)}, bf16[128,512]{1,0:T(8,128)(2,1)S(1)}, bf16[128,512]{1,0:T(8,128)(2,1)S(1)...) custom-call(s32[1,8,128]{2,1,0:T(8,128)} %send_ref.1, bf16[1,512,512]{2,1,0:T(8,128)(2,1)} %coarse_ref.1), custom_call_target="tpu_custom_call" | custom-call | flops 536870912 | bytes 2097152 | tf_op jit(solution)/shard_map/pick/pallas_call | solution.py:88
  2.6 0.1 collective-permute-start
  2.6 1.7 %collective-permute-done.one_ref.other_ref = bf16[384,512]{1,0:T(8,128)(2,1)S(1)} collective-permute-done((bf16[384,512]{1,0:T(8,128)(2,1)S(1)}, bf16[384,512]{1,0:T(8,128)(2,1)S(1)}, u32[]{:S(2)}, u32[]{:S(2)}) %collective-permute-start) | collective-permute-done | bytes 393248 | tf_op jit(solution)/shard_map/ppermute | solution.py:59
  4.4 0.4 collective-permute-start.3
  4.8 2.5 %collective-permute-start.4 = (bf16[256,512]{1,0:T(8,128)(2,1)S(1)}, bf16[256,512]{1,0:T(8,128)(2,1)S(1)}, u32[]{:S(2)}, u32[]{:S(2)}) collective-permute-start(bf16[256,512]{1,0:T(8,128)(2,1)S(1)} %get-tuple-element.42), channel_id=1, source_target_pairs={{0,24},{4,28},{8,16},{12,20},{16,8},{20,12},{24,0},{28,4},{1,25},{... | collective-permute-start | bytes 786440 | tf_op jit(solution)/shard_map/ppermute | solution.py:59
  7.3 0.7 %collective-permute-start.1 = (bf16[128,512]{1,0:T(8,128)(2,1)S(1)}, bf16[128,512]{1,0:T(8,128)(2,1)S(1)}, u32[]{:S(2)}, u32[]{:S(2)}) collective-permute-start(bf16[128,512]{1,0:T(8,128)(2,1)S(1)} %get-tuple-element.35), channel_id=1, source_target_pairs={{0,8},{4,12},{8,0},{12,4},{16,24},{20,28},{24,16},{28,20},{1,9},{5... | collective-permute-start | bytes 393224 | tf_op jit(solution)/shard_map/ppermute | solution.py:59
  7.9 0.2 collective-permute-start.2
  8.2 5.8 %spread.1 = (bf16[2048,512]{1,0:T(8,128)(2,1)S(1)}, bf16[2048,512]{1,0:T(8,128)(2,1)S(1)}, f32[1,2048]{1,0:T(1,128)S(1)}, bf16[8,256,512]{2,1,0:T(8,128)(2,1)S(1)}, bf16[88,512]{1,0:T(8,128)(2,1)S(1)}) custom-call(s32[3,2048]{1,0:T(4,128)} %refs_0_.1, f32[3,2048]{1,0:T(4,128)} %refs_1_.1, s32[6,2048]{1,0:T(8,128)} %refs_2_.1, bf16[83,512]{1,0:T(8,128)(2,1)} %bitcast.10, ...), custom_call_target="tpu_custom_call" | custom-call | flops 1 | bytes 1 | tf_op jit(solution)/shard_map/spread/pallas_call | solution.py:181
  14.0 6.0 %collective-permute-done.1.refs_0_ = bf16[128,512]{1,0:T(8,128)(2,1)S(1)} collective-permute-done((bf16[128,512]{1,0:T(8,128)(2,1)S(1)}, bf16[128,512]{1,0:T(8,128)(2,1)S(1)}, u32[]{:S(2)}, u32[]{:S(2)}) %collective-permute-start.1) | collective-permute-done | bytes 131104 | tf_op jit(solution)/shard_map/ppermute | solution.py:59
  20.0 2.0 %collective-permute-done.2.refs_1_ = bf16[128,512]{1,0:T(8,128)(2,1)S(1)} collective-permute-done((bf16[128,512]{1,0:T(8,128)(2,1)S(1)}, bf16[128,512]{1,0:T(8,128)(2,1)S(1)}, u32[]{:S(2)}, u32[]{:S(2)}) %collective-permute-start.2) | collective-permute-done | bytes 131104 | tf_op jit(solution)/shard_map/ppermute | solution.py:59
  22.0 1.5 %early.1.sum_ref = f32[2048,512]{1,0:T(8,128)S(1)} custom-call(bf16[2048,512]{1,0:T(8,128)(2,1)S(1)} %get-tuple-element.33.spread_ref, bf16[128,512]{1,0:T(8,128)(2,1)S(1)} %get-tuple-element.31.refs_4_.own_ref, bf16[384,512]{1,0:T(8,128)(2,1)S(1)} %collective-permute-done.one_ref.other_ref, bf16[128,512]{1,0:T(8,128)(2,1)S(1)} %collective-permute-done.1.refs_0_, ...), custom_call_target="tpu_custom_call" | custom-call | flops 1 | bytes 1 | tf_op jit(solution)/shard_map/early/pallas_call | solution.py:237
  23.4 1.5 %collective-permute-done.3.refs_0_ = bf16[256,512]{1,0:T(8,128)(2,1)S(1)} collective-permute-done((bf16[256,512]{1,0:T(8,128)(2,1)S(1)}, bf16[256,512]{1,0:T(8,128)(2,1)S(1)}, u32[]{:S(2)}, u32[]{:S(2)}) %collective-permute-start.3) | collective-permute-done | bytes 262176 | tf_op jit(solution)/shard_map/ppermute | solution.py:59
  24.9 0.0 collective-permute-done.4.refs_1_
  25.0 0.0 copy-start.2
  25.0 0.0 copy-start.3
  25.0 1.7 %late.1 = (bf16[2048,512]{1,0:T(8,128)(2,1)S(1)}, bf16[128,512]{1,0:T(8,128)(2,1)S(1)}, bf16[128,512]{1,0:T(8,128)(2,1)S(1)}) custom-call(f32[2048,512]{1,0:T(8,128)S(1)} %early.1.sum_ref, bf16[2048,512]{1,0:T(8,128)(2,1)S(1)} %get-tuple-element.37.spread_ref, f32[1,2048]{1,0:T(1,128)S(1)} %get-tuple-element.38.scale_ref, bf16[2048,512]{1,0:T(8,128)(2,1)S(1)} %copy-done, ...), custom_call_target="tpu_custom_call" | custom-call | flops 1073741824 | bytes 8388608 | tf_op jit(solution)/shard_map/late/pallas_call | solution.py:272
  26.7 2.7 %collective-permute-start.5 = (bf16[128,512]{1,0:T(8,128)(2,1)S(1)}, bf16[128,512]{1,0:T(8,128)(2,1)S(1)}, u32[]{:S(2)}, u32[]{:S(2)}) collective-permute-start(bf16[128,512]{1,0:T(8,128)(2,1)S(1)} %get-tuple-element.46), channel_id=1, source_target_pairs={{0,4},{4,0},{8,12},{12,8},{16,20},{20,16},{24,28},{28,24},{1,5},{5... | collective-permute-start | bytes 393224 | tf_op jit(solution)/shard_map/ppermute | solution.py:59
  29.4 5.5 %collective-permute-start.6 = (bf16[128,512]{1,0:T(8,128)(2,1)S(1)}, bf16[128,512]{1,0:T(8,128)(2,1)S(1)}, u32[]{:S(2)}, u32[]{:S(2)}) collective-permute-start(bf16[128,512]{1,0:T(8,128)(2,1)S(1)} %get-tuple-element.47), channel_id=1, source_target_pairs={{4,8},{12,16},{20,24},{8,4},{16,12},{24,20},{5,9},{13,17},{21,25},... | collective-permute-start | bytes 393224 | tf_op jit(solution)/shard_map/ppermute | solution.py:536
  34.9 4.3 %inner.1 = (bf16[1536,512]{1,0:T(8,128)(2,1)S(1)}, bf16[6,88,256]{2,1,0:T(8,128)(2,1)S(1)}) custom-call(bf16[2048,512]{1,0:T(8,128)(2,1)S(1)} %get-tuple-element.43.x_ref, bf16[8,256,512]{2,1,0:T(8,128)(2,1)S(1)} %get-tuple-element.44.count_ref, bf16[1024,512]{1,0:T(8,128)(2,1)S(1)} %copy-done.1, bf16[512,512]{1,0:T(8,128)(2,1)S(1)} %copy-done.2, ...), custom_call_target="tpu_custom_call" | custom-call | flops 4026531840 | bytes 8388608 | tf_op jit(solution)/shard_map/inner/pallas_call | solution.py:344
  39.2 0.0 collective-permute-done.5.inner_ref
  39.2 0.0 collective-permute-done.6.outer_ref
  39.2 0.0 copy-start.4
  39.2 0.0 copy-start.5
  39.2 0.0 copy-start.6
  39.3 1.8 %outer.1 = (bf16[512,512]{1,0:T(8,128)(2,1)S(1)}, bf16[88,512]{1,0:T(8,128)(2,1)S(1)}, bf16[88,512]{1,0:T(8,128)(2,1)S(1)}, bf16[88,512]{1,0:T(8,128)(2,1)S(1)}, bf16[88,512]{1,0:T(8,128)(2,1)S(1)}) custom-call(bf16[2048,512]{1,0:T(8,128)(2,1)S(1)} %get-tuple-element.43.x_ref, bf16[8,256,512]{2,1,0:T(8,128)(2,1)S(1)} %get-tuple-element.44.count_ref, ...), custom_call_target="tpu_custom_call" | custom-call | flops 1342177280 | bytes 8388608 | tf_op jit(solution)/shard_map/outer/pallas_call | solution.py:344
  41.1 1.6 %collective-permute-start.7 = (bf16[88,512]{1,0:T(8,128)(2,1)S(1)}, bf16[88,512]{1,0:T(8,128)(2,1)S(1)}, u32[]{:S(2)}, u32[]{:S(2)}) collective-permute-start(bf16[88,512]{1,0:T(8,128)(2,1)S(1)} %get-tuple-element.51), channel_id=1, source_target_pairs={{0,1},{1,0},{2,3},{3,2},{4,5},{5,4},{6,7},{7,6},{8,9},{9,8},{10,11... | collective-permute-start | bytes 270344 | tf_op jit(solution)/shard_map/ppermute | solution.py:59
  42.6 1.5 %collective-permute-start.8 = (bf16[88,512]{1,0:T(8,128)(2,1)S(1)}, bf16[88,512]{1,0:T(8,128)(2,1)S(1)}, u32[]{:S(2)}, u32[]{:S(2)}) collective-permute-start(bf16[88,512]{1,0:T(8,128)(2,1)S(1)} %get-tuple-element.52), channel_id=1, source_target_pairs={{0,2},{1,3},{2,0},{3,1},{4,6},{5,7},{6,4},{7,5},{8,10},{9,11},{10,... | collective-permute-start | bytes 270344 | tf_op jit(solution)/shard_map/ppermute | solution.py:59
  44.2 0.5 collective-permute-start.9
  45.3 0.4 collective-permute-done.7.refs_1_
  45.7 3.2 %collective-permute-done.8.refs_2_ = bf16[88,512]{1,0:T(8,128)(2,1)S(1)} collective-permute-done((bf16[88,512]{1,0:T(8,128)(2,1)S(1)}, bf16[88,512]{1,0:T(8,128)(2,1)S(1)}, u32[]{:S(2)}, u32[]{:S(2)}) %collective-permute-start.8) | collective-permute-done | bytes 90144 | tf_op jit(solution)/shard_map/ppermute | solution.py:59
  48.9 1.1 %collective-permute-done.9.refs_3_ = bf16[88,512]{1,0:T(8,128)(2,1)S(1)} collective-permute-done((bf16[88,512]{1,0:T(8,128)(2,1)S(1)}, bf16[88,512]{1,0:T(8,128)(2,1)S(1)}, u32[]{:S(2)}, u32[]{:S(2)}) %collective-permute-start.9) | collective-permute-done | bytes 90144 | tf_op jit(solution)/shard_map/ppermute | solution.py:59
  50.1 0.0 copy-done.5
  50.1 1.0 %score.1 = (bf16[88,512]{1,0:T(8,128)(2,1)S(1)}, bf16[88,512]{1,0:T(8,128)(2,1)S(1)}, bf16[88,512]{1,0:T(8,128)(2,1)S(1)}, bf16[88,512]{1,0:T(8,128)(2,1)S(1)}) custom-call(s32[1]{0:T(128)S(6)} %copy.16.live_ref, f32[1,83]{1,0:T(1,128)S(1)} %bitcast.8, f32[1,2048]{1,0:T(1,128)S(1)} %bitcast.7, bf16[83,2048]{1,0:T(8,128)(2,1)S(1)} %copy-done.4, ...), custom_call_target="tpu_custom_call" | custom-call | flops 7208960 | bytes 1048576 | tf_op jit(solution)/shard_map/score/pallas_call | solution.py:413
  51.0 0.8 %collective-permute-start.10 = (bf16[88,512]{1,0:T(8,128)(2,1)S(1)}, bf16[88,512]{1,0:T(8,128)(2,1)S(1)}, u32[]{:S(2)}, u32[]{:S(2)}) collective-permute-start(bf16[88,512]{1,0:T(8,128)(2,1)S(1)} %get-tuple-element.55), channel_id=1, source_target_pairs={{0,1},{1,0},{2,3},{3,2},{4,5},{5,4},{6,7},{7,6},{8,9},{9,8},{10,11... | collective-permute-start | bytes 270344 | tf_op jit(solution)/shard_map/ppermute | solution.py:59
  51.9 0.6 collective-permute-start.11
  52.5 2.1 %collective-permute-start.12 = (bf16[88,512]{1,0:T(8,128)(2,1)S(1)}, bf16[88,512]{1,0:T(8,128)(2,1)S(1)}, u32[]{:S(2)}, u32[]{:S(2)}) collective-permute-start(bf16[88,512]{1,0:T(8,128)(2,1)S(1)} %get-tuple-element.57), channel_id=1, source_target_pairs={{0,3},{1,2},{2,1},{3,0},{4,7},{5,6},{6,5},{7,4},{8,11},{9,10},{10,... | collective-permute-start | bytes 270344 | tf_op jit(solution)/shard_map/ppermute | solution.py:59
  54.6 1.5 %collective-permute-done.10.refs_1_ = bf16[88,512]{1,0:T(8,128)(2,1)S(1)} collective-permute-done((bf16[88,512]{1,0:T(8,128)(2,1)S(1)}, bf16[88,512]{1,0:T(8,128)(2,1)S(1)}, u32[]{:S(2)}, u32[]{:S(2)}) %collective-permute-start.10) | collective-permute-done | bytes 90144 | tf_op jit(solution)/shard_map/ppermute | solution.py:59
  56.1 1.3 %collective-permute-done.11.refs_2_ = bf16[88,512]{1,0:T(8,128)(2,1)S(1)} collective-permute-done((bf16[88,512]{1,0:T(8,128)(2,1)S(1)}, bf16[88,512]{1,0:T(8,128)(2,1)S(1)}, u32[]{:S(2)}, u32[]{:S(2)}) %collective-permute-start.11) | collective-permute-done | bytes 90144 | tf_op jit(solution)/shard_map/ppermute | solution.py:59
  57.4 1.0 %collective-permute-done.12.refs_3_ = bf16[88,512]{1,0:T(8,128)(2,1)S(1)} collective-permute-done((bf16[88,512]{1,0:T(8,128)(2,1)S(1)}, bf16[88,512]{1,0:T(8,128)(2,1)S(1)}, u32[]{:S(2)}, u32[]{:S(2)}) %collective-permute-start.12) | collective-permute-done | bytes 90144 | tf_op jit(solution)/shard_map/ppermute | solution.py:59
  58.3 0.5 head_terms.1
  58.8 1.6 %collective-permute-start.13 = (bf16[88,512]{1,0:T(8,128)(2,1)S(1)}, bf16[88,512]{1,0:T(8,128)(2,1)S(1)}, u32[]{:S(2)}, u32[]{:S(2)}) collective-permute-start(bf16[88,512]{1,0:T(8,128)(2,1)S(1)} %get-tuple-element.59.refs_0_), channel_id=1, source_target_pairs={{0,1},{1,0},{2,3},{3,2},{4,5},{5,4},{6,7},{7,6},{8,9},{9,8},{10,11... | collective-permute-start | bytes 270344 | tf_op jit(solution)/shard_map/ppermute | solution.py:59
  60.4 0.7 %collective-permute-start.14 = (bf16[88,512]{1,0:T(8,128)(2,1)S(1)}, bf16[88,512]{1,0:T(8,128)(2,1)S(1)}, u32[]{:S(2)}, u32[]{:S(2)}) collective-permute-start(bf16[88,512]{1,0:T(8,128)(2,1)S(1)} %get-tuple-element.59.refs_0_), channel_id=1, source_target_pairs={{0,2},{1,3},{2,0},{3,1},{4,6},{5,7},{6,4},{7,5},{8,10},{9,11},{10,... | collective-permute-start | bytes 270344 | tf_op jit(solution)/shard_map/ppermute | solution.py:59
  61.1 1.2 %collective-permute-start.15 = (bf16[88,512]{1,0:T(8,128)(2,1)S(1)}, bf16[88,512]{1,0:T(8,128)(2,1)S(1)}, u32[]{:S(2)}, u32[]{:S(2)}) collective-permute-start(bf16[88,512]{1,0:T(8,128)(2,1)S(1)} %get-tuple-element.59.refs_0_), channel_id=1, source_target_pairs={{0,3},{1,2},{2,1},{3,0},{4,7},{5,6},{6,5},{7,4},{8,11},{9,10},{10,... | collective-permute-start | bytes 270344 | tf_op jit(solution)/shard_map/ppermute | solution.py:59
  62.3 2.0 %latent_grad.1 = bf16[1,2048,512]{2,1,0:T(8,128)(2,1)} custom-call(bf16[88,512]{1,0:T(8,128)(2,1)S(1)} %get-tuple-element.32.head_ref, bf16[8,88,256]{2,1,0:T(8,128)(2,1)S(1)} %get-tuple-element.58.score_ref), custom_call_target="tpu_custom_call" | custom-call | flops 184549376 | bytes 3145728 | tf_op jit(solution)/shard_map/latent_grad/pallas_call | solution.py:467
  64.4 0.0 collective-permute-done.13.refs_1_
  64.4 0.5 collective-permute-done.14.refs_2_
  64.9 1.6 %collective-permute-done.15.refs_3_ = bf16[88,512]{1,0:T(8,128)(2,1)S(1)} collective-permute-done((bf16[88,512]{1,0:T(8,128)(2,1)S(1)}, bf16[88,512]{1,0:T(8,128)(2,1)S(1)}, u32[]{:S(2)}, u32[]{:S(2)}) %collective-permute-start.15) | collective-permute-done | bytes 90144 | tf_op jit(solution)/shard_map/ppermute | solution.py:59
  66.6 0.8 %head_total.1 = f32[83,1,512]{2,1,0:T(1,128)} custom-call(bf16[88,512]{1,0:T(8,128)(2,1)S(1)} %get-tuple-element.59.refs_0_, bf16[88,512]{1,0:T(8,128)(2,1)S(1)} %collective-permute-done.13.refs_1_, bf16[88,512]{1,0:T(8,128)(2,1)S(1)} %collective-permute-done.14.refs_2_, bf16[88,512]{1,0:T(8,128)(2,1)S(1)} %collective-permute-done.15.refs_3_), custom_call_target="tpu_custom_call" | custom-call | flops 180224 | bytes 1048576 | tf_op jit(solution)/shard_map/head_total/pallas_call | solution.py:487
  (9 shorter events, 0.1 us)
Async XLA Ops:
  2.6 1.8 %collective-permute-start = (bf16[384,512]{1,0:T(8,128)(2,1)S(1)}, bf16[384,512]{1,0:T(8,128)(2,1)S(1)}, u32[]{:S(2)}, u32[]{:S(2)}) collective-permute-start(bf16[384,512]{1,0:T(8,128)(2,1)S(1)} %get-tuple-element.34), channel_id=1, source_target_pairs={{0,4},{4,0},{8,12},{12,8},{16,20},{20,16},{24,28},{28,24},{1,5},{5... | collective-permute-start | bytes 1179656 | tf_op jit(solution)/shard_map/ppermute | solution.py:59
  4.4 20.6 %collective-permute-start.3 = (bf16[256,512]{1,0:T(8,128)(2,1)S(1)}, bf16[256,512]{1,0:T(8,128)(2,1)S(1)}, u32[]{:S(2)}, u32[]{:S(2)}) collective-permute-start(bf16[256,512]{1,0:T(8,128)(2,1)S(1)} %get-tuple-element.41), channel_id=1, source_target_pairs={{0,16},{4,20},{8,24},{12,28},{16,0},{20,4},{24,8},{28,12},{1,17},{... | collective-permute-start | bytes 786440 | tf_op jit(solution)/shard_map/ppermute | solution.py:59
  4.8 20.2 %collective-permute-start.4 = (bf16[256,512]{1,0:T(8,128)(2,1)S(1)}, bf16[256,512]{1,0:T(8,128)(2,1)S(1)}, u32[]{:S(2)}, u32[]{:S(2)}) collective-permute-start(bf16[256,512]{1,0:T(8,128)(2,1)S(1)} %get-tuple-element.42), channel_id=1, source_target_pairs={{0,24},{4,28},{8,16},{12,20},{16,8},{20,12},{24,0},{28,4},{1,25},{... | collective-permute-start | bytes 786440 | tf_op jit(solution)/shard_map/ppermute | solution.py:59
  7.3 12.7 %collective-permute-start.1 = (bf16[128,512]{1,0:T(8,128)(2,1)S(1)}, bf16[128,512]{1,0:T(8,128)(2,1)S(1)}, u32[]{:S(2)}, u32[]{:S(2)}) collective-permute-start(bf16[128,512]{1,0:T(8,128)(2,1)S(1)} %get-tuple-element.35), channel_id=1, source_target_pairs={{0,8},{4,12},{8,0},{12,4},{16,24},{20,28},{24,16},{28,20},{1,9},{5... | collective-permute-start | bytes 393224 | tf_op jit(solution)/shard_map/ppermute | solution.py:59
  7.9 14.0 %collective-permute-start.2 = (bf16[128,512]{1,0:T(8,128)(2,1)S(1)}, bf16[128,512]{1,0:T(8,128)(2,1)S(1)}, u32[]{:S(2)}, u32[]{:S(2)}) collective-permute-start(bf16[128,512]{1,0:T(8,128)(2,1)S(1)} %get-tuple-element.36), channel_id=1, source_target_pairs={{0,12},{4,8},{8,4},{12,0},{16,28},{20,24},{24,20},{28,16},{1,13},{... | collective-permute-start | bytes 393224 | tf_op jit(solution)/shard_map/ppermute | solution.py:59
  22.0 3.0 %copy-start = (bf16[2048,512]{1,0:T(8,128)(2,1)S(1)}, bf16[2048,512]{1,0:T(8,128)(2,1)}, u32[]{:S(2)}) copy-start(bf16[2048,512]{1,0:T(8,128)(2,1)} %skip_ref.1) | copy-start | bytes 6291460
  24.9 9.9 %copy-start.1 = (bf16[1024,512]{1,0:T(8,128)(2,1)S(1)}, bf16[1024,512]{1,0:T(8,128)(2,1)}, u32[]{:S(2)}) copy-start(bf16[1024,512]{1,0:T(8,128)(2,1)} %w_in_ref.3) | copy-start | bytes 3145732
  25.0 9.9 %copy-start.2 = (bf16[512,512]{1,0:T(8,128)(2,1)S(1)}, bf16[512,512]{1,0:T(8,128)(2,1)}, u32[]{:S(2)}) copy-start(bf16[512,512]{1,0:T(8,128)(2,1)} %w_out_ref.3) | copy-start | bytes 1572868
  25.0 9.9 %copy-start.3 = (f32[512]{0:T(512)S(1)}, f32[512]{0:T(512)}, u32[]{:S(2)}) copy-start(f32[512]{0:T(512)} %param.26) | copy-start | bytes 6148
  26.7 12.5 %collective-permute-start.5 = (bf16[128,512]{1,0:T(8,128)(2,1)S(1)}, bf16[128,512]{1,0:T(8,128)(2,1)S(1)}, u32[]{:S(2)}, u32[]{:S(2)}) collective-permute-start(bf16[128,512]{1,0:T(8,128)(2,1)S(1)} %get-tuple-element.46), channel_id=1, source_target_pairs={{0,4},{4,0},{8,12},{12,8},{16,20},{20,16},{24,28},{28,24},{1,5},{5... | collective-permute-start | bytes 393224 | tf_op jit(solution)/shard_map/ppermute | solution.py:59
  29.4 9.8 %collective-permute-start.6 = (bf16[128,512]{1,0:T(8,128)(2,1)S(1)}, bf16[128,512]{1,0:T(8,128)(2,1)S(1)}, u32[]{:S(2)}, u32[]{:S(2)}) collective-permute-start(bf16[128,512]{1,0:T(8,128)(2,1)S(1)} %get-tuple-element.47), channel_id=1, source_target_pairs={{4,8},{12,16},{20,24},{8,4},{16,12},{24,20},{5,9},{13,17},{21,25},... | collective-permute-start | bytes 393224 | tf_op jit(solution)/shard_map/ppermute | solution.py:536
  39.2 10.8 %copy-start.4 = (bf16[83,2048]{1,0:T(8,128)(2,1)S(1)}, bf16[83,2048]{1,0:T(8,128)(2,1)}, u32[]{:S(2)}) copy-start(bf16[83,2048]{1,0:T(8,128)(2,1)} %target_ref.1) | copy-start | bytes 1019908
  39.2 10.8 %copy-start.5 = (f32[2048]{0:T(1024)S(1)}, f32[2048]{0:T(1024)}, u32[]{:S(2)}) copy-start(f32[2048]{0:T(1024)} %param.20) | copy-start | bytes 24580
  39.2 10.8 %copy-start.6 = (f32[83]{0:T(128)S(1)}, f32[83]{0:T(128)}, u32[]{:S(2)}) copy-start(f32[83]{0:T(128)} %param.23) | copy-start | bytes 1000
  41.1 4.6 %collective-permute-start.7 = (bf16[88,512]{1,0:T(8,128)(2,1)S(1)}, bf16[88,512]{1,0:T(8,128)(2,1)S(1)}, u32[]{:S(2)}, u32[]{:S(2)}) collective-permute-start(bf16[88,512]{1,0:T(8,128)(2,1)S(1)} %get-tuple-element.51), channel_id=1, source_target_pairs={{0,1},{1,0},{2,3},{3,2},{4,5},{5,4},{6,7},{7,6},{8,9},{9,8},{10,11... | collective-permute-start | bytes 270344 | tf_op jit(solution)/shard_map/ppermute | solution.py:59
  42.6 6.3 %collective-permute-start.8 = (bf16[88,512]{1,0:T(8,128)(2,1)S(1)}, bf16[88,512]{1,0:T(8,128)(2,1)S(1)}, u32[]{:S(2)}, u32[]{:S(2)}) collective-permute-start(bf16[88,512]{1,0:T(8,128)(2,1)S(1)} %get-tuple-element.52), channel_id=1, source_target_pairs={{0,2},{1,3},{2,0},{3,1},{4,6},{5,7},{6,4},{7,5},{8,10},{9,11},{10,... | collective-permute-start | bytes 270344 | tf_op jit(solution)/shard_map/ppermute | solution.py:59
  44.2 5.9 %collective-permute-start.9 = (bf16[88,512]{1,0:T(8,128)(2,1)S(1)}, bf16[88,512]{1,0:T(8,128)(2,1)S(1)}, u32[]{:S(2)}, u32[]{:S(2)}) collective-permute-start(bf16[88,512]{1,0:T(8,128)(2,1)S(1)} %get-tuple-element.53), channel_id=1, source_target_pairs={{0,3},{1,2},{2,1},{3,0},{4,7},{5,6},{6,5},{7,4},{8,11},{9,10},{10,... | collective-permute-start | bytes 270344 | tf_op jit(solution)/shard_map/ppermute | solution.py:59
  51.0 5.0 %collective-permute-start.10 = (bf16[88,512]{1,0:T(8,128)(2,1)S(1)}, bf16[88,512]{1,0:T(8,128)(2,1)S(1)}, u32[]{:S(2)}, u32[]{:S(2)}) collective-permute-start(bf16[88,512]{1,0:T(8,128)(2,1)S(1)} %get-tuple-element.55), channel_id=1, source_target_pairs={{0,1},{1,0},{2,3},{3,2},{4,5},{5,4},{6,7},{7,6},{8,9},{9,8},{10,11... | collective-permute-start | bytes 270344 | tf_op jit(solution)/shard_map/ppermute | solution.py:59
  51.9 5.5 %collective-permute-start.11 = (bf16[88,512]{1,0:T(8,128)(2,1)S(1)}, bf16[88,512]{1,0:T(8,128)(2,1)S(1)}, u32[]{:S(2)}, u32[]{:S(2)}) collective-permute-start(bf16[88,512]{1,0:T(8,128)(2,1)S(1)} %get-tuple-element.56), channel_id=1, source_target_pairs={{0,2},{1,3},{2,0},{3,1},{4,6},{5,7},{6,4},{7,5},{8,10},{9,11},{10,... | collective-permute-start | bytes 270344 | tf_op jit(solution)/shard_map/ppermute | solution.py:59
  52.5 5.8 %collective-permute-start.12 = (bf16[88,512]{1,0:T(8,128)(2,1)S(1)}, bf16[88,512]{1,0:T(8,128)(2,1)S(1)}, u32[]{:S(2)}, u32[]{:S(2)}) collective-permute-start(bf16[88,512]{1,0:T(8,128)(2,1)S(1)} %get-tuple-element.57), channel_id=1, source_target_pairs={{0,3},{1,2},{2,1},{3,0},{4,7},{5,6},{6,5},{7,4},{8,11},{9,10},{10,... | collective-permute-start | bytes 270344 | tf_op jit(solution)/shard_map/ppermute | solution.py:59
  58.8 5.6 %collective-permute-start.13 = (bf16[88,512]{1,0:T(8,128)(2,1)S(1)}, bf16[88,512]{1,0:T(8,128)(2,1)S(1)}, u32[]{:S(2)}, u32[]{:S(2)}) collective-permute-start(bf16[88,512]{1,0:T(8,128)(2,1)S(1)} %get-tuple-element.59.refs_0_), channel_id=1, source_target_pairs={{0,1},{1,0},{2,3},{3,2},{4,5},{5,4},{6,7},{7,6},{8,9},{9,8},{10,11... | collective-permute-start | bytes 270344 | tf_op jit(solution)/shard_map/ppermute | solution.py:59
  60.4 4.5 %collective-permute-start.14 = (bf16[88,512]{1,0:T(8,128)(2,1)S(1)}, bf16[88,512]{1,0:T(8,128)(2,1)S(1)}, u32[]{:S(2)}, u32[]{:S(2)}) collective-permute-start(bf16[88,512]{1,0:T(8,128)(2,1)S(1)} %get-tuple-element.59.refs_0_), channel_id=1, source_target_pairs={{0,2},{1,3},{2,0},{3,1},{4,6},{5,7},{6,4},{7,5},{8,10},{9,11},{10,... | collective-permute-start | bytes 270344 | tf_op jit(solution)/shard_map/ppermute | solution.py:59
  61.1 5.4 %collective-permute-start.15 = (bf16[88,512]{1,0:T(8,128)(2,1)S(1)}, bf16[88,512]{1,0:T(8,128)(2,1)S(1)}, u32[]{:S(2)}, u32[]{:S(2)}) collective-permute-start(bf16[88,512]{1,0:T(8,128)(2,1)S(1)} %get-tuple-element.59.refs_0_), channel_id=1, source_target_pairs={{0,3},{1,2},{2,1},{3,0},{4,7},{5,6},{6,5},{7,4},{8,11},{9,10},{10,... | collective-permute-start | bytes 270344 | tf_op jit(solution)/shard_map/ppermute | solution.py:59

commit v4 on v3

--- a/solution.py
+++ b/solution.py
@@ -75,38 +75,53 @@
     return jnp.concatenate([ref[0, pl.ds(me ^ s, 1), :] for s in steps], axis=0)
 
 
-def pick_kernel(steps, send_ref, coarse_ref, *refs):
-    outs, (rows_ref, table_ref, sems) = refs[:-3], refs[-3:]
+def first_pick_kernel(steps, send_ref, coarse_ref, out, rows_ref, table_ref, sems):
     fetch([(send_ref, rows_ref), (coarse_ref, table_ref)], sems)
+    picked(send_rows_of(rows_ref, steps), table_ref[0], [out])
+
+
+def first_pick(send_rows, coarse, steps):
+    slots, width = send_rows.shape[2], coarse.shape[2]
+    return pl.pallas_call(
+        functools.partial(first_pick_kernel, steps),
+        out_shape=[
+            jax.ShapeDtypeStruct((len(steps) * slots, width), BF16),
+            jax.ShapeDtypeStruct(send_rows.shape, jnp.int32),
+            jax.ShapeDtypeStruct(coarse.shape, BF16),
+        ],
+        in_specs=[pl.BlockSpec(memory_space=pltpu.HBM)] * 2,
+        out_specs=[pl.BlockSpec(memory_space=VMEM)] * 3,
+        scratch_shapes=[pltpu.SemaphoreType.DMA((2,))],
+        compiler_params=params(8),
+        cost_estimate=cost(1, 1),
+        name="pick_first",
+    )(*in_hbm(send_rows, coarse))
+
+
+def pick_kernel(steps, rows_ref, table_ref, *outs):
     picked(send_rows_of(rows_ref, steps), table_ref[0], outs)
 
 
-def pick(send_rows, coarse, groups):
-    _, count, slots = send_rows.shape
+def pick(rows, table, groups):
+    slots, width = rows.shape[2], table.shape[2]
     steps = [s for group in groups for s in group]
-    width = coarse.shape[2]
     return pl.pallas_call(
         functools.partial(pick_kernel, steps),
         out_shape=[jax.ShapeDtypeStruct((len(group) * slots, width), BF16) for group in groups],
-        in_specs=[pl.BlockSpec(memory_space=pltpu.HBM)] * 2,
+        in_specs=[pl.BlockSpec(memory_space=VMEM)] * 2,
         out_specs=[pl.BlockSpec(memory_space=VMEM)] * len(groups),
-        scratch_shapes=[
-            VMEM(send_rows.shape, jnp.int32),
-            VMEM(coarse.shape, BF16),
-            pltpu.SemaphoreType.DMA((2,)),
-        ],
-        compiler_params=params(16),
-        cost_estimate=cost(2 * count * slots * coarse.shape[1] * width, 2 * MIB),
+        compiler_params=params(8),
+        cost_estimate=cost(1, 1),
         name="pick",
-    )(*in_hbm(send_rows, coarse))
-
-
-def best_scale(weight):
+    )(rows, table)
+
+
+def best_scale(weight, counted):
     best = scale = jnp.ones((1, weight.shape[1]), F32)
-    for c in range(16):
+    for c in range(24):
         factor = 1.0 + 0.0017 * c
         part = weight * (1.0 / factor)
-        miss = part - part.astype(BF16).astype(F32)
+        miss = jnp.where(counted, part - part.astype(BF16).astype(F32), 0.0)
         miss = miss * miss
         miss = miss[0:1] + miss[1:2] + miss[2:3]
         scale = jnp.where(miss < best, factor, scale)
@@ -114,12 +129,26 @@
     return scale
 
 
-def spread_kernel(tile, steps, *refs):
-    sources, (first_ref, last_ref, scale_ref, count_ref, head_ref), held, sems = refs[:4], refs[5:10], refs[10:-1], refs[-1]
+def spread_kernel(tile, steps, live_ref, *refs):
+    sources, outs, scratch = refs[:7], refs[8:16], refs[16:]
+    first_ref, last_ref, scale_ref, count_ref, head_ref, area_ref, inv_ref, target_ref = outs
+    held, kw_rows, sems = scratch[:7], scratch[7], scratch[8]
     fetch(list(zip(sources, held)), sems)
-    index_ref, weight_ref, nb_ref, head_in_ref = held
+    index_ref, weight_ref, nb_ref, head_in_ref, area_in_ref, target_in_ref, kw_ref = held
+    padded, piece = target_ref.shape
+    num_vars = target_in_ref.shape[0]
+    start = pl.multiple_of(lax.axis_index("mem") * piece, piece)
+    place = start + lax.broadcasted_iota(jnp.int32, (1, piece), 1)
+    area_ref[...] = jnp.where(place < live_ref[0], area_in_ref[:, pl.ds(start, piece)], 0.0)
+    kw_rows[...] = jnp.ones(kw_rows.shape, F32)
+    kw_rows[0:1, :num_vars] = kw_ref[...]
+    width = kw_rows[...].T[:padded, 0:1]
+    inv_ref[...] = 1.0 / (width * width)
+    target_ref[...] = jnp.zeros(target_ref.shape, F32)
+    target_ref[:num_vars, :] = target_in_ref[:, pl.ds(start, piece)].astype(F32)
     me = lax.axis_index("dom")
-    rows, cut = first_ref.shape
+    rows = first_ref.shape[0]
+    cut = first_ref.shape[1] // 2
     slots = cut + last_ref.shape[1]
     span = count_ref.shape[2]
     part = 32
@@ -150,19 +179,26 @@
         w2 = jnp.where(same02 | same12, 0.0, w2)
         i1 = jnp.where(same01, -1, i1)
         i2 = jnp.where(same02 | same12, -1, i2)
-        index = narrow(jnp.concatenate([i0, i1, i2], axis=0))
+        found = jnp.concatenate([i0, i1, i2], axis=0)
         w = jnp.concatenate([w0, w1, w2], axis=0)
-        scale = best_scale(w)
+        scale = best_scale(w, found >= cut)
         scale_ref[:, lanes] = scale
-        weight = columns(w / scale).astype(BF16)
+        index = narrow(found)
+        weight = columns(w / scale)
+        high = weight.astype(BF16)
+        low = (weight - high.astype(F32)).astype(BF16)
         near = narrow(nb_ref[:, lanes] - start)
         for r in range(0, tile, part):
             here = slice(r, r + part)
             rows_here = pl.ds(pl.multiple_of(start + r, part), part)
             total = jnp.zeros((part, slots), BF16)
+            rest = jnp.zeros((part, cut), BF16)
             for k in range(3):
-                total = jnp.where(index[here, k : k + 1] == spots, weight[here, k : k + 1], total)
-            first_ref[rows_here, :] = total[:, :cut]
+                hit = index[here, k : k + 1] == spots
+                total = jnp.where(hit, high[here, k : k + 1], total)
+                rest = jnp.where(hit[:, :cut], low[here, k : k + 1], rest)
+            first_ref[rows_here, :cut] = total[:, :cut]
+            first_ref[rows_here, cut:] = rest
             last_ref[rows_here, :] = total[:, cut:]
             counts = jnp.zeros((part, span), BF16)
             for k in range(nb_ref.shape[0]):
@@ -173,7 +209,8 @@
     lax.fori_loop(0, rows // tile, step, 0)
 
 
-def spread(token, up_index, up_weight, neighbors, head, steps, slots, split, tile, padded):
+def spread(token, live_counts, sources, steps, slots, split, tile, padded, piece):
+    up_index, head = sources[0], sources[3]
     rows = up_index.shape[1]
     tiles = rows // tile
     span = tile + 2 * RIM
@@ -181,20 +218,25 @@
     return pl.pallas_call(
         functools.partial(spread_kernel, tile, steps),
         out_shape=[
-            jax.ShapeDtypeStruct((rows, cut), BF16),
+            jax.ShapeDtypeStruct((rows, 2 * cut), BF16),
             jax.ShapeDtypeStruct((rows, total - cut), BF16),
             jax.ShapeDtypeStruct((1, rows), F32),
             jax.ShapeDtypeStruct((tiles, tile, span), BF16),
             jax.ShapeDtypeStruct((padded, head.shape[1]), BF16),
+            jax.ShapeDtypeStruct((1, piece), F32),
+            jax.ShapeDtypeStruct((padded, 1), F32),
+            jax.ShapeDtypeStruct((padded, piece), F32),
         ],
-        in_specs=[pl.BlockSpec(memory_space=pltpu.HBM)] * 4 + [pl.BlockSpec(memory_space=VMEM)],
-        out_specs=[pl.BlockSpec(memory_space=VMEM)] * 5,
-        scratch_shapes=[VMEM(v.shape, v.dtype) for v in (up_index, up_weight, neighbors, head)]
-        + [pltpu.SemaphoreType.DMA((4,))],
+        in_specs=[pl.BlockSpec(memory_space=pltpu.SMEM)]
+        + [pl.BlockSpec(memory_space=pltpu.HBM)] * 7
+        + [pl.BlockSpec(memory_space=VMEM)],
+        out_specs=[pl.BlockSpec(memory_space=VMEM)] * 8,
+        scratch_shapes=[VMEM(v.shape, v.dtype) for v in sources]
+        + [VMEM((8, 128), F32), pltpu.SemaphoreType.DMA((7,))],
         compiler_params=params(16),
         cost_estimate=cost(1, 1),
         name="spread",
-    )(*in_hbm(up_index, up_weight, neighbors, head), token)
+    )(live_counts, *in_hbm(*sources), token)
 
 
 def pack_kernel(other_ref, *refs):
@@ -222,7 +264,7 @@
 def early_kernel(tile, spread_ref, own_ref, one_ref, *refs):
     tables, out = refs[:-1], refs[-1]
     parts = [own_ref[...], one_ref[: own_ref.shape[0], :]] + [r[...] for r in tables]
-    table = jnp.concatenate(parts, axis=0)
+    table = jnp.concatenate(parts + parts, axis=0)
 
     def step(t, carry):
         rows = pl.ds(pl.multiple_of(t * tile, tile), tile)
@@ -381,20 +423,9 @@
     return h_mid, h_end, preds
 
 
-def score_kernel(members, live_ref, kw_ref, area_ref, target_ref, *refs):
-    preds, outs, (kw_rows, target) = refs[:members], refs[members:-2], refs[-2:]
-    num_vars = target_ref.shape[0]
-    padded, piece = target.shape
-    start = pl.multiple_of(lax.axis_index("mem") * piece, piece)
-    lanes = pl.ds(start, piece)
-    kw_rows[...] = jnp.ones(kw_rows.shape, F32)
-    kw_rows[0:1, :num_vars] = kw_ref[...]
-    width = kw_rows[...].T[:padded, 0:1]
-    inv_sq = 1.0 / (width * width)
-    target[...] = jnp.zeros(target.shape, F32)
-    target[:num_vars, :] = target_ref[:, lanes].astype(F32)
-    place = start + lax.broadcasted_iota(jnp.int32, (1, piece), 1)
-    weight = jnp.where(place < live_ref[0], area_ref[:, lanes], 0.0)
+def score_kernel(members, weight_ref, inv_ref, target_ref, *refs):
+    preds, outs = refs[:members], refs[members:]
+    inv_sq, weight = inv_ref[...], weight_ref[...]
     values = [r[...].astype(F32) for r in preds]
     sums = [jnp.zeros(v.shape, F32) for v in values]
     for i in range(members):
@@ -403,23 +434,22 @@
             sums[i] = sums[i] + phi
             sums[j] = sums[j] - phi
     for i in range(members):
-        total = sums[i] * (1.0 / members) - slope(values[i] - target[...], inv_sq)
+        total = sums[i] * (1.0 / members) - slope(values[i] - target_ref[...], inv_sq)
         outs[i][...] = (weight * total).astype(BF16)
 
 
-def score(live_counts, kernel_width, area, targets, preds):
+def score(weight, inv_sq, target, preds):
     members = len(preds)
     shape = preds[0].shape
     return pl.pallas_call(
         functools.partial(score_kernel, members),
         out_shape=[jax.ShapeDtypeStruct(shape, BF16)] * members,
-        in_specs=[pl.BlockSpec(memory_space=pltpu.SMEM)] + [pl.BlockSpec(memory_space=VMEM)] * (3 + members),
+        in_specs=[pl.BlockSpec(memory_space=VMEM)] * (3 + members),
         out_specs=[pl.BlockSpec(memory_space=VMEM)] * members,
-        scratch_shapes=[VMEM((8, 128), F32), VMEM(shape, F32)],
         compiler_params=params(16),
         cost_estimate=cost(10 * preds[0].size * members * members, MIB, preds[0].size * members * members),
         name="score",
-    )(live_counts, kernel_width, area, targets, *preds)
+    )(weight, inv_sq, target, *preds)
 
 
 def head_kernel(members, mid_ref, end_ref, *refs):
@@ -520,14 +550,15 @@
     tile = min(256, rows // members)
 
     even = list(range(4, dom_count, 2))
-    groups = [[0], [1] + [s + 1 for s in even], [2], [3]] + [[s] for s in even]
     steps = list(range(dom_count))
-    own, one, two, three, *far = pick(send_rows, coarse_latents, groups)
+    one, sent, table = first_pick(send_rows, coarse_latents, [1] + [s + 1 for s in even])
     one = xor_permute(one, "dom", 1)
+    own, two, three, *far = pick(sent, table, [[0], [2], [3]] + [[s] for s in even])
     far = [xor_permute(v, "dom", s) for v, s in zip(pack(one, far), even)]
     two, three = xor_permute(two, "dom", 2), xor_permute(three, "dom", 3)
-    first_rows, last_rows, scale, counts, head = spread(
-        own, up_index, up_weight, neighbors, w_head.T, steps, slots, 4, tile, padded
+    sources = (up_index, up_weight, neighbors, w_head.T, area[None, :], targets, kernel_width[None, :])
+    first_rows, last_rows, scale, counts, head, weight, inv_sq, target = spread(
+        own, live_counts, sources, steps, slots, 4, tile, padded, rows // members
     )
     sums = early(first_rows, [own, one, two, three], tile)
     x, inner, outer = late(sums, last_rows, scale, fine_skip, far, tile)
@@ -537,7 +568,7 @@
 
     mid, end, preds = update(members, x, counts, w_in, w_out, ln_gain[None, :], head, inner, outer)
     preds = [preds[0]] + [xor_permute(preds[s], "mem", s) for s in range(1, members)]
-    scores = score(live_counts, kernel_width[None, :], area[None, :], targets, preds)
+    scores = score(weight, inv_sq, target, preds)
     scores = [scores[0]] + [xor_permute(scores[s], "mem", s) for s in range(1, members)]
     term, by_tile = head_terms(members, mid, end, scores)
     terms = [term] + [xor_permute(term, "mem", s) for s in range(1, members)]

time: 67.5 us -> 67.3 us (level)
  waiting for transfers between devices: 21.9 us -> 19.1 us
  Pallas kernels: 21.2 us -> 23.9 us
    ppermute x15, waiting for transfers between devices: 21.9 us -> 19.1 us  [xor_permute(): return lax.ppermute(value, axis, [(i, i ^ step) for i in range(count)])]
    pallas_call x0 -> x1, Pallas kernels: none -> 1.58 us  [first_pick(): pl.pallas_call(functools.partial(first_pick_kernel, steps), out_shape=[ja...]
    pallas_call x1, Pallas kernels: 5.76 us -> 7.11 us  [spread(): pl.pallas_call(functools.partial(spread_kernel, tile, steps), out_shape=[...]
    pallas_call x1, Pallas kernels: 1.92 us -> 0.64 us  [pick(): pl.pallas_call(functools.partial(pick_kernel, steps), out_shape=[jax.Shap...]
    pallas_call x1, Pallas kernels: 1.45 us -> 2.53 us  [early(): pl.pallas_call(functools.partial(early_kernel, tile), out_shape=jax.Shape...]
    ppermute x15, starting transfers between devices: 17.2 us -> 18.2 us  [xor_permute(): return lax.ppermute(value, axis, [(i, i ^ step) for i in range(count)])]
    ppermute x1, starting transfers between devices: 5.47 us -> 4.46 us  [shards(): outer = lax.ppermute(outer, 'dom', pairs + [(j, i) for i, j in pairs])]
  transfers between devices with their start and end apart: 16 -> 16, of which waited for: 12 -> 11; matrix products, arithmetic and copies ran while one was open for 0% -> 0% of each run, Pallas kernels for 20% -> 25%
where the time goes in v4:
time: 67.3 us; the launch traced here: 67.1 us
  Pallas kernels  23.9 us (36%)
  starting transfers between devices  22.7 us (34%)
  waiting for transfers between devices  19.1 us (28%)
  between operations  1.45 us (2%)
    ppermute x15, waiting for transfers between devices, xor_permute(): return lax.ppermute(value, axis, [(i, i ^ step) for i in range(count)])  19.1 us
    ppermute x15, starting transfers between devices, xor_permute(): return lax.ppermute(value, axis, [(i, i ^ step) for i in range(count)])  18.2 us
    pallas_call x1, Pallas kernels, spread(): pl.pallas_call(functools.partial(spread_kernel, tile, steps), out_shape=[...  7.11 us
    pallas_call x2, Pallas kernels, update_call(): pl.pallas_call(kernel, out_shape=out_shape, in_specs=[pl.BlockSpec(memory...  6.1 us
    ppermute x1, starting transfers between devices, shards(): outer = lax.ppermute(outer, 'dom', pairs + [(j, i) for i, j in pairs])  4.46 us
    pallas_call x1, Pallas kernels, early(): pl.pallas_call(functools.partial(early_kernel, tile), out_shape=jax.Shape...  2.53 us
    pallas_call x1, Pallas kernels, latent_grad(): pl.pallas_call(latent_kernel, out_shape=jax.ShapeDtypeStruct((1, tiles *...  2.05 us
    pallas_call x1, Pallas kernels, late(): pl.pallas_call(functools.partial(late_kernel, tile), out_shape=[jax.Shape...  1.73 us
  transfers between devices with their start and end apart: 16, of which 11 were waited for; matrix products, arithmetic and copies ran while one was open for 0% of the time, Pallas kernels for 25%

profile of v4, /device:TPU:24, one launch (start us, length us, event | category | flops | bytes accessed | tf_op | source)
XLA Modules:
  0.0 67.1 jit_solution(4504135157749622982)
XLA Ops:
  0.6 1.6 %pick_first.1 = (bf16[384,512]{1,0:T(8,128)(2,1)S(1)}, s32[1,8,128]{2,1,0:T(8,128)S(1)}, bf16[1,512,512]{2,1,0:T(8,128)(2,1)S(1)}) custom-call(s32[1,8,128]{2,1,0:T(8,128)} %send_ref.1, bf16[1,512,512]{2,1,0:T(8,128)(2,1)} %coarse_ref.1), custom_call_target="tpu_custom_call" | custom-call | flops 1 | bytes 1 | tf_op jit(solution)/shard_map/pick_first/pallas_call | solution.py:85
  2.2 0.1 collective-permute-start
  2.3 0.6 pick.1
  2.9 1.1 %collective-permute-done.one_ref.other_ref = bf16[384,512]{1,0:T(8,128)(2,1)S(1)} collective-permute-done((bf16[384,512]{1,0:T(8,128)(2,1)S(1)}, bf16[384,512]{1,0:T(8,128)(2,1)S(1)}, u32[]{:S(2)}, u32[]{:S(2)}) %collective-permute-start) | collective-permute-done | bytes 393248 | tf_op jit(solution)/shard_map/ppermute | solution.py:59
  4.0 0.4 collective-permute-start.3
  4.4 2.5 %collective-permute-start.4 = (bf16[256,512]{1,0:T(8,128)(2,1)S(1)}, bf16[256,512]{1,0:T(8,128)(2,1)S(1)}, u32[]{:S(2)}, u32[]{:S(2)}) collective-permute-start(bf16[256,512]{1,0:T(8,128)(2,1)S(1)} %get-tuple-element.49), channel_id=1, source_target_pairs={{0,24},{4,28},{8,16},{12,20},{16,8},{20,12},{24,0},{28,4},{1,25},{... | collective-permute-start | bytes 786440 | tf_op jit(solution)/shard_map/ppermute | solution.py:59
  6.9 0.7 %collective-permute-start.1 = (bf16[128,512]{1,0:T(8,128)(2,1)S(1)}, bf16[128,512]{1,0:T(8,128)(2,1)S(1)}, u32[]{:S(2)}, u32[]{:S(2)}) collective-permute-start(bf16[128,512]{1,0:T(8,128)(2,1)S(1)} %get-tuple-element.42), channel_id=1, source_target_pairs={{0,8},{4,12},{8,0},{12,4},{16,24},{20,28},{24,16},{28,20},{1,9},{5... | collective-permute-start | bytes 393224 | tf_op jit(solution)/shard_map/ppermute | solution.py:59
  7.6 0.2 collective-permute-start.2
  8.5 7.1 %spread.1 = (bf16[2048,1024]{1,0:T(8,128)(2,1)S(1)}, bf16[2048,512]{1,0:T(8,128)(2,1)S(1)}, f32[1,2048]{1,0:T(1,128)S(1)}, bf16[8,256,512]{2,1,0:T(8,128)(2,1)S(...) custom-call(s32[1]{0:T(128)S(6)} %copy.16.live_ref, ...), custom_call_target="tpu_custom_call" | custom-call | flops 1 | bytes 1 | tf_op jit(solution)/shard_map/spread/pallas_call | solution.py:218
  15.6 4.0 %collective-permute-done.1.refs_0_ = bf16[128,512]{1,0:T(8,128)(2,1)S(1)} collective-permute-done((bf16[128,512]{1,0:T(8,128)(2,1)S(1)}, bf16[128,512]{1,0:T(8,128)(2,1)S(1)}, u32[]{:S(2)}, u32[]{:S(2)}) %collective-permute-start.1) | collective-permute-done | bytes 131104 | tf_op jit(solution)/shard_map/ppermute | solution.py:59
  19.6 2.0 %collective-permute-done.2.refs_1_ = bf16[128,512]{1,0:T(8,128)(2,1)S(1)} collective-permute-done((bf16[128,512]{1,0:T(8,128)(2,1)S(1)}, bf16[128,512]{1,0:T(8,128)(2,1)S(1)}, u32[]{:S(2)}, u32[]{:S(2)}) %collective-permute-start.2) | collective-permute-done | bytes 131104 | tf_op jit(solution)/shard_map/ppermute | solution.py:59
  21.6 2.5 %early.1.sum_ref = f32[2048,512]{1,0:T(8,128)S(1)} custom-call(bf16[2048,1024]{1,0:T(8,128)(2,1)S(1)} %get-tuple-element.40.spread_ref, bf16[128,512]{1,0:T(8,128)(2,1)S(1)} %get-tuple-element.38.refs_7_.own_ref, bf16[384,512]{1,0:T(8,128)(2,1)S(1)} %collective-permute-done.one_ref.other_ref, bf16[128,512]{1,0:T(8,128)(2,1)S(1)} %collective-permute-done.1.refs_0_, ...), custom_call_target="tpu_custom_call" | custom-call | flops 1 | bytes 1 | tf_op jit(solution)/shard_map/early/pallas_call | solution.py:279
  24.2 0.4 collective-permute-done.3.refs_0_
  24.6 0.0 collective-permute-done.4.refs_1_
  24.6 0.0 copy-done
  24.6 0.0 copy-start.2
  24.6 0.0 copy-start.3
  24.6 1.7 %late.1 = (bf16[2048,512]{1,0:T(8,128)(2,1)S(1)}, bf16[128,512]{1,0:T(8,128)(2,1)S(1)}, bf16[128,512]{1,0:T(8,128)(2,1)S(1)}) custom-call(f32[2048,512]{1,0:T(8,128)S(1)} %early.1.sum_ref, bf16[2048,512]{1,0:T(8,128)(2,1)S(1)} %get-tuple-element.44.spread_ref, f32[1,2048]{1,0:T(1,128)S(1)} %get-tuple-element.45.scale_ref, bf16[2048,512]{1,0:T(8,128)(2,1)S(1)} %copy-done, ...), custom_call_target="tpu_custom_call" | custom-call | flops 1073741824 | bytes 8388608 | tf_op jit(solution)/shard_map/late/pallas_call | solution.py:314
  26.4 3.7 %collective-permute-start.5 = (bf16[128,512]{1,0:T(8,128)(2,1)S(1)}, bf16[128,512]{1,0:T(8,128)(2,1)S(1)}, u32[]{:S(2)}, u32[]{:S(2)}) collective-permute-start(bf16[128,512]{1,0:T(8,128)(2,1)S(1)} %get-tuple-element.53), channel_id=1, source_target_pairs={{0,4},{4,0},{8,12},{12,8},{16,20},{20,16},{24,28},{28,24},{1,5},{5... | collective-permute-start | bytes 393224 | tf_op jit(solution)/shard_map/ppermute | solution.py:59
  30.1 4.5 %collective-permute-start.6 = (bf16[128,512]{1,0:T(8,128)(2,1)S(1)}, bf16[128,512]{1,0:T(8,128)(2,1)S(1)}, u32[]{:S(2)}, u32[]{:S(2)}) collective-permute-start(bf16[128,512]{1,0:T(8,128)(2,1)S(1)} %get-tuple-element.54), channel_id=1, source_target_pairs={{4,8},{12,16},{20,24},{8,4},{16,12},{24,20},{5,9},{13,17},{21,25},... | collective-permute-start | bytes 393224 | tf_op jit(solution)/shard_map/ppermute | solution.py:567
  34.5 0.0 copy-done.1
  34.5 0.0 copy-done.2
  34.6 4.3 %inner.1 = (bf16[1536,512]{1,0:T(8,128)(2,1)S(1)}, bf16[6,88,256]{2,1,0:T(8,128)(2,1)S(1)}) custom-call(bf16[2048,512]{1,0:T(8,128)(2,1)S(1)} %get-tuple-element.50.x_ref, bf16[8,256,512]{2,1,0:T(8,128)(2,1)S(1)} %get-tuple-element.51.count_ref, bf16[1024,512]{1,0:T(8,128)(2,1)S(1)} %copy-done.1, bf16[512,512]{1,0:T(8,128)(2,1)S(1)} %copy-done.2, ...), custom_call_target="tpu_custom_call" | custom-call | flops 4026531840 | bytes 8388608 | tf_op jit(solution)/shard_map/inner/pallas_call | solution.py:386
  38.9 0.0 collective-permute-done.5.inner_ref
  38.9 0.0 collective-permute-done.6.outer_ref
  38.9 1.8 %outer.1 = (bf16[512,512]{1,0:T(8,128)(2,1)S(1)}, bf16[88,512]{1,0:T(8,128)(2,1)S(1)}, bf16[88,512]{1,0:T(8,128)(2,1)S(1)}, bf16[88,512]{1,0:T(8,128)(2,1)S(1)}, bf16[88,512]{1,0:T(8,128)(2,1)S(1)}) custom-call(bf16[2048,512]{1,0:T(8,128)(2,1)S(1)} %get-tuple-element.50.x_ref, bf16[8,256,512]{2,1,0:T(8,128)(2,1)S(1)} %get-tuple-element.51.count_ref, ...), custom_call_target="tpu_custom_call" | custom-call | flops 1342177280 | bytes 8388608 | tf_op jit(solution)/shard_map/outer/pallas_call | solution.py:386
  40.7 1.5 %collective-permute-start.7 = (bf16[88,512]{1,0:T(8,128)(2,1)S(1)}, bf16[88,512]{1,0:T(8,128)(2,1)S(1)}, u32[]{:S(2)}, u32[]{:S(2)}) collective-permute-start(bf16[88,512]{1,0:T(8,128)(2,1)S(1)} %get-tuple-element.61), channel_id=1, source_target_pairs={{0,1},{1,0},{2,3},{3,2},{4,5},{5,4},{6,7},{7,6},{8,9},{9,8},{10,11... | collective-permute-start | bytes 270344 | tf_op jit(solution)/shard_map/ppermute | solution.py:59
  42.3 1.5 %collective-permute-start.8 = (bf16[88,512]{1,0:T(8,128)(2,1)S(1)}, bf16[88,512]{1,0:T(8,128)(2,1)S(1)}, u32[]{:S(2)}, u32[]{:S(2)}) collective-permute-start(bf16[88,512]{1,0:T(8,128)(2,1)S(1)} %get-tuple-element.62), channel_id=1, source_target_pairs={{0,2},{1,3},{2,0},{3,1},{4,6},{5,7},{6,4},{7,5},{8,10},{9,11},{10,... | collective-permute-start | bytes 270344 | tf_op jit(solution)/shard_map/ppermute | solution.py:59
  43.8 0.5 collective-permute-start.9
  44.3 1.0 %collective-permute-done.7.refs_1_ = bf16[88,512]{1,0:T(8,128)(2,1)S(1)} collective-permute-done((bf16[88,512]{1,0:T(8,128)(2,1)S(1)}, bf16[88,512]{1,0:T(8,128)(2,1)S(1)}, u32[]{:S(2)}, u32[]{:S(2)}) %collective-permute-start.7) | collective-permute-done | bytes 90144 | tf_op jit(solution)/shard_map/ppermute | solution.py:59
  45.3 1.5 %collective-permute-done.8.refs_2_ = bf16[88,512]{1,0:T(8,128)(2,1)S(1)} collective-permute-done((bf16[88,512]{1,0:T(8,128)(2,1)S(1)}, bf16[88,512]{1,0:T(8,128)(2,1)S(1)}, u32[]{:S(2)}, u32[]{:S(2)}) %collective-permute-start.8) | collective-permute-done | bytes 90144 | tf_op jit(solution)/shard_map/ppermute | solution.py:59
  46.8 3.1 %collective-permute-done.9.refs_3_ = bf16[88,512]{1,0:T(8,128)(2,1)S(1)} collective-permute-done((bf16[88,512]{1,0:T(8,128)(2,1)S(1)}, bf16[88,512]{1,0:T(8,128)(2,1)S(1)}, u32[]{:S(2)}, u32[]{:S(2)}) %collective-permute-start.9) | collective-permute-done | bytes 90144 | tf_op jit(solution)/shard_map/ppermute | solution.py:59
  49.9 0.9 %score.1 = (bf16[88,512]{1,0:T(8,128)(2,1)S(1)}, bf16[88,512]{1,0:T(8,128)(2,1)S(1)}, bf16[88,512]{1,0:T(8,128)(2,1)S(1)}, bf16[88,512]{1,0:T(8,128)(2,1)S(1)}) custom-call(f32[1,512]{1,0:T(1,128)S(1)} %get-tuple-element.57.weight_ref, f32[88,1]{1,0:T(8,128)S(1)} %get-tuple-element.58.inv_ref, f32[88,512]{1,0:T(8,128)S(1)} %get-tuple-element.59.target_ref, ...), custom_call_target="tpu_custom_call" | custom-call | flops 7208960 | bytes 1048576 | tf_op jit(solution)/shard_map/score/pallas_call | solution.py:444
  50.9 0.1 collective-permute-start.10
  50.9 1.3 %collective-permute-start.11 = (bf16[88,512]{1,0:T(8,128)(2,1)S(1)}, bf16[88,512]{1,0:T(8,128)(2,1)S(1)}, u32[]{:S(2)}, u32[]{:S(2)}) collective-permute-start(bf16[88,512]{1,0:T(8,128)(2,1)S(1)} %get-tuple-element.66), channel_id=1, source_target_pairs={{0,2},{1,3},{2,0},{3,1},{4,6},{5,7},{6,4},{7,5},{8,10},{9,11},{10,... | collective-permute-start | bytes 270344 | tf_op jit(solution)/shard_map/ppermute | solution.py:59
  52.2 2.2 %collective-permute-start.12 = (bf16[88,512]{1,0:T(8,128)(2,1)S(1)}, bf16[88,512]{1,0:T(8,128)(2,1)S(1)}, u32[]{:S(2)}, u32[]{:S(2)}) collective-permute-start(bf16[88,512]{1,0:T(8,128)(2,1)S(1)} %get-tuple-element.67), channel_id=1, source_target_pairs={{0,3},{1,2},{2,1},{3,0},{4,7},{5,6},{6,5},{7,4},{8,11},{9,10},{10,... | collective-permute-start | bytes 270344 | tf_op jit(solution)/shard_map/ppermute | solution.py:59
  54.4 1.0 %collective-permute-done.10.refs_1_ = bf16[88,512]{1,0:T(8,128)(2,1)S(1)} collective-permute-done((bf16[88,512]{1,0:T(8,128)(2,1)S(1)}, bf16[88,512]{1,0:T(8,128)(2,1)S(1)}, u32[]{:S(2)}, u32[]{:S(2)}) %collective-permute-start.10) | collective-permute-done | bytes 90144 | tf_op jit(solution)/shard_map/ppermute | solution.py:59
  55.4 2.8 %collective-permute-done.11.refs_2_ = bf16[88,512]{1,0:T(8,128)(2,1)S(1)} collective-permute-done((bf16[88,512]{1,0:T(8,128)(2,1)S(1)}, bf16[88,512]{1,0:T(8,128)(2,1)S(1)}, u32[]{:S(2)}, u32[]{:S(2)}) %collective-permute-start.11) | collective-permute-done | bytes 90144 | tf_op jit(solution)/shard_map/ppermute | solution.py:59
  58.2 0.0 collective-permute-done.12.refs_3_
  58.2 0.5 head_terms.1
  58.7 1.3 %collective-permute-start.13 = (bf16[88,512]{1,0:T(8,128)(2,1)S(1)}, bf16[88,512]{1,0:T(8,128)(2,1)S(1)}, u32[]{:S(2)}, u32[]{:S(2)}) collective-permute-start(bf16[88,512]{1,0:T(8,128)(2,1)S(1)} %get-tuple-element.69.refs_0_), channel_id=1, source_target_pairs={{0,1},{1,0},{2,3},{3,2},{4,5},{5,4},{6,7},{7,6},{8,9},{9,8},{10,11... | collective-permute-start | bytes 270344 | tf_op jit(solution)/shard_map/ppermute | solution.py:59
  60.0 1.0 %collective-permute-start.14 = (bf16[88,512]{1,0:T(8,128)(2,1)S(1)}, bf16[88,512]{1,0:T(8,128)(2,1)S(1)}, u32[]{:S(2)}, u32[]{:S(2)}) collective-permute-start(bf16[88,512]{1,0:T(8,128)(2,1)S(1)} %get-tuple-element.69.refs_0_), channel_id=1, source_target_pairs={{0,2},{1,3},{2,0},{3,1},{4,6},{5,7},{6,4},{7,5},{8,10},{9,11},{10,... | collective-permute-start | bytes 270344 | tf_op jit(solution)/shard_map/ppermute | solution.py:59
  60.9 1.3 %collective-permute-start.15 = (bf16[88,512]{1,0:T(8,128)(2,1)S(1)}, bf16[88,512]{1,0:T(8,128)(2,1)S(1)}, u32[]{:S(2)}, u32[]{:S(2)}) collective-permute-start(bf16[88,512]{1,0:T(8,128)(2,1)S(1)} %get-tuple-element.69.refs_0_), channel_id=1, source_target_pairs={{0,3},{1,2},{2,1},{3,0},{4,7},{5,6},{6,5},{7,4},{8,11},{9,10},{10,... | collective-permute-start | bytes 270344 | tf_op jit(solution)/shard_map/ppermute | solution.py:59
  62.3 2.1 %latent_grad.1 = bf16[1,2048,512]{2,1,0:T(8,128)(2,1)} custom-call(bf16[88,512]{1,0:T(8,128)(2,1)S(1)} %get-tuple-element.39.head_ref, bf16[8,88,256]{2,1,0:T(8,128)(2,1)S(1)} %get-tuple-element.68.score_ref), custom_call_target="tpu_custom_call" | custom-call | flops 184549376 | bytes 3145728 | tf_op jit(solution)/shard_map/latent_grad/pallas_call | solution.py:497
  64.3 0.0 collective-permute-done.13.refs_1_
  64.3 0.2 collective-permute-done.14.refs_2_
  64.5 1.9 %collective-permute-done.15.refs_3_ = bf16[88,512]{1,0:T(8,128)(2,1)S(1)} collective-permute-done((bf16[88,512]{1,0:T(8,128)(2,1)S(1)}, bf16[88,512]{1,0:T(8,128)(2,1)S(1)}, u32[]{:S(2)}, u32[]{:S(2)}) %collective-permute-start.15) | collective-permute-done | bytes 90144 | tf_op jit(solution)/shard_map/ppermute | solution.py:59
  66.4 0.8 %head_total.1 = f32[83,1,512]{2,1,0:T(1,128)} custom-call(bf16[88,512]{1,0:T(8,128)(2,1)S(1)} %get-tuple-element.69.refs_0_, bf16[88,512]{1,0:T(8,128)(2,1)S(1)} %collective-permute-done.13.refs_1_, bf16[88,512]{1,0:T(8,128)(2,1)S(1)} %collective-permute-done.14.refs_2_, bf16[88,512]{1,0:T(8,128)(2,1)S(1)} %collective-permute-done.15.refs_3_), custom_call_target="tpu_custom_call" | custom-call | flops 180224 | bytes 1048576 | tf_op jit(solution)/shard_map/head_total/pallas_call | solution.py:517
  (4 shorter events, 0.0 us)
Async XLA Ops:
  2.2 1.8 %collective-permute-start = (bf16[384,512]{1,0:T(8,128)(2,1)S(1)}, bf16[384,512]{1,0:T(8,128)(2,1)S(1)}, u32[]{:S(2)}, u32[]{:S(2)}) collective-permute-start(bf16[384,512]{1,0:T(8,128)(2,1)S(1)} %get-tuple-element.41), channel_id=1, source_target_pairs={{0,4},{4,0},{8,12},{12,8},{16,20},{20,16},{24,28},{28,24},{1,5},{5... | collective-permute-start | bytes 1179656 | tf_op jit(solution)/shard_map/ppermute | solution.py:59
  4.0 20.6 %collective-permute-start.3 = (bf16[256,512]{1,0:T(8,128)(2,1)S(1)}, bf16[256,512]{1,0:T(8,128)(2,1)S(1)}, u32[]{:S(2)}, u32[]{:S(2)}) collective-permute-start(bf16[256,512]{1,0:T(8,128)(2,1)S(1)} %get-tuple-element.48), channel_id=1, source_target_pairs={{0,16},{4,20},{8,24},{12,28},{16,0},{20,4},{24,8},{28,12},{1,17},{... | collective-permute-start | bytes 786440 | tf_op jit(solution)/shard_map/ppermute | solution.py:59
  4.4 20.2 %collective-permute-start.4 = (bf16[256,512]{1,0:T(8,128)(2,1)S(1)}, bf16[256,512]{1,0:T(8,128)(2,1)S(1)}, u32[]{:S(2)}, u32[]{:S(2)}) collective-permute-start(bf16[256,512]{1,0:T(8,128)(2,1)S(1)} %get-tuple-element.49), channel_id=1, source_target_pairs={{0,24},{4,28},{8,16},{12,20},{16,8},{20,12},{24,0},{28,4},{1,25},{... | collective-permute-start | bytes 786440 | tf_op jit(solution)/shard_map/ppermute | solution.py:59
  6.9 12.7 %collective-permute-start.1 = (bf16[128,512]{1,0:T(8,128)(2,1)S(1)}, bf16[128,512]{1,0:T(8,128)(2,1)S(1)}, u32[]{:S(2)}, u32[]{:S(2)}) collective-permute-start(bf16[128,512]{1,0:T(8,128)(2,1)S(1)} %get-tuple-element.42), channel_id=1, source_target_pairs={{0,8},{4,12},{8,0},{12,4},{16,24},{20,28},{24,16},{28,20},{1,9},{5... | collective-permute-start | bytes 393224 | tf_op jit(solution)/shard_map/ppermute | solution.py:59
  7.6 14.0 %collective-permute-start.2 = (bf16[128,512]{1,0:T(8,128)(2,1)S(1)}, bf16[128,512]{1,0:T(8,128)(2,1)S(1)}, u32[]{:S(2)}, u32[]{:S(2)}) collective-permute-start(bf16[128,512]{1,0:T(8,128)(2,1)S(1)} %get-tuple-element.43), channel_id=1, source_target_pairs={{0,12},{4,8},{8,4},{12,0},{16,28},{20,24},{24,20},{28,16},{1,13},{... | collective-permute-start | bytes 393224 | tf_op jit(solution)/shard_map/ppermute | solution.py:59
  21.6 3.0 %copy-start = (bf16[2048,512]{1,0:T(8,128)(2,1)S(1)}, bf16[2048,512]{1,0:T(8,128)(2,1)}, u32[]{:S(2)}) copy-start(bf16[2048,512]{1,0:T(8,128)(2,1)} %skip_ref.1) | copy-start | bytes 6291460
  24.6 9.9 %copy-start.1 = (bf16[1024,512]{1,0:T(8,128)(2,1)S(1)}, bf16[1024,512]{1,0:T(8,128)(2,1)}, u32[]{:S(2)}) copy-start(bf16[1024,512]{1,0:T(8,128)(2,1)} %w_in_ref.3) | copy-start | bytes 3145732
  24.6 9.9 %copy-start.2 = (bf16[512,512]{1,0:T(8,128)(2,1)S(1)}, bf16[512,512]{1,0:T(8,128)(2,1)}, u32[]{:S(2)}) copy-start(bf16[512,512]{1,0:T(8,128)(2,1)} %w_out_ref.3) | copy-start | bytes 1572868
  24.6 9.9 %copy-start.3 = (f32[512]{0:T(512)S(1)}, f32[512]{0:T(512)}, u32[]{:S(2)}) copy-start(f32[512]{0:T(512)} %param.26) | copy-start | bytes 6148
  26.4 12.5 %collective-permute-start.5 = (bf16[128,512]{1,0:T(8,128)(2,1)S(1)}, bf16[128,512]{1,0:T(8,128)(2,1)S(1)}, u32[]{:S(2)}, u32[]{:S(2)}) collective-permute-start(bf16[128,512]{1,0:T(8,128)(2,1)S(1)} %get-tuple-element.53), channel_id=1, source_target_pairs={{0,4},{4,0},{8,12},{12,8},{16,20},{20,16},{24,28},{28,24},{1,5},{5... | collective-permute-start | bytes 393224 | tf_op jit(solution)/shard_map/ppermute | solution.py:59
  30.1 8.8 %collective-permute-start.6 = (bf16[128,512]{1,0:T(8,128)(2,1)S(1)}, bf16[128,512]{1,0:T(8,128)(2,1)S(1)}, u32[]{:S(2)}, u32[]{:S(2)}) collective-permute-start(bf16[128,512]{1,0:T(8,128)(2,1)S(1)} %get-tuple-element.54), channel_id=1, source_target_pairs={{4,8},{12,16},{20,24},{8,4},{16,12},{24,20},{5,9},{13,17},{21,25},... | collective-permute-start | bytes 393224 | tf_op jit(solution)/shard_map/ppermute | solution.py:567
  40.7 4.6 %collective-permute-start.7 = (bf16[88,512]{1,0:T(8,128)(2,1)S(1)}, bf16[88,512]{1,0:T(8,128)(2,1)S(1)}, u32[]{:S(2)}, u32[]{:S(2)}) collective-permute-start(bf16[88,512]{1,0:T(8,128)(2,1)S(1)} %get-tuple-element.61), channel_id=1, source_target_pairs={{0,1},{1,0},{2,3},{3,2},{4,5},{5,4},{6,7},{7,6},{8,9},{9,8},{10,11... | collective-permute-start | bytes 270344 | tf_op jit(solution)/shard_map/ppermute | solution.py:59
  42.3 4.5 %collective-permute-start.8 = (bf16[88,512]{1,0:T(8,128)(2,1)S(1)}, bf16[88,512]{1,0:T(8,128)(2,1)S(1)}, u32[]{:S(2)}, u32[]{:S(2)}) collective-permute-start(bf16[88,512]{1,0:T(8,128)(2,1)S(1)} %get-tuple-element.62), channel_id=1, source_target_pairs={{0,2},{1,3},{2,0},{3,1},{4,6},{5,7},{6,4},{7,5},{8,10},{9,11},{10,... | collective-permute-start | bytes 270344 | tf_op jit(solution)/shard_map/ppermute | solution.py:59
  43.8 6.1 %collective-permute-start.9 = (bf16[88,512]{1,0:T(8,128)(2,1)S(1)}, bf16[88,512]{1,0:T(8,128)(2,1)S(1)}, u32[]{:S(2)}, u32[]{:S(2)}) collective-permute-start(bf16[88,512]{1,0:T(8,128)(2,1)S(1)} %get-tuple-element.63), channel_id=1, source_target_pairs={{0,3},{1,2},{2,1},{3,0},{4,7},{5,6},{6,5},{7,4},{8,11},{9,10},{10,... | collective-permute-start | bytes 270344 | tf_op jit(solution)/shard_map/ppermute | solution.py:59
  50.9 4.6 %collective-permute-start.10 = (bf16[88,512]{1,0:T(8,128)(2,1)S(1)}, bf16[88,512]{1,0:T(8,128)(2,1)S(1)}, u32[]{:S(2)}, u32[]{:S(2)}) collective-permute-start(bf16[88,512]{1,0:T(8,128)(2,1)S(1)} %get-tuple-element.65), channel_id=1, source_target_pairs={{0,1},{1,0},{2,3},{3,2},{4,5},{5,4},{6,7},{7,6},{8,9},{9,8},{10,11... | collective-permute-start | bytes 270344 | tf_op jit(solution)/shard_map/ppermute | solution.py:59
  50.9 7.3 %collective-permute-start.11 = (bf16[88,512]{1,0:T(8,128)(2,1)S(1)}, bf16[88,512]{1,0:T(8,128)(2,1)S(1)}, u32[]{:S(2)}, u32[]{:S(2)}) collective-permute-start(bf16[88,512]{1,0:T(8,128)(2,1)S(1)} %get-tuple-element.66), channel_id=1, source_target_pairs={{0,2},{1,3},{2,0},{3,1},{4,6},{5,7},{6,4},{7,5},{8,10},{9,11},{10,... | collective-permute-start | bytes 270344 | tf_op jit(solution)/shard_map/ppermute | solution.py:59
  52.2 6.0 %collective-permute-start.12 = (bf16[88,512]{1,0:T(8,128)(2,1)S(1)}, bf16[88,512]{1,0:T(8,128)(2,1)S(1)}, u32[]{:S(2)}, u32[]{:S(2)}) collective-permute-start(bf16[88,512]{1,0:T(8,128)(2,1)S(1)} %get-tuple-element.67), channel_id=1, source_target_pairs={{0,3},{1,2},{2,1},{3,0},{4,7},{5,6},{6,5},{7,4},{8,11},{9,10},{10,... | collective-permute-start | bytes 270344 | tf_op jit(solution)/shard_map/ppermute | solution.py:59
  58.7 5.6 %collective-permute-start.13 = (bf16[88,512]{1,0:T(8,128)(2,1)S(1)}, bf16[88,512]{1,0:T(8,128)(2,1)S(1)}, u32[]{:S(2)}, u32[]{:S(2)}) collective-permute-start(bf16[88,512]{1,0:T(8,128)(2,1)S(1)} %get-tuple-element.69.refs_0_), channel_id=1, source_target_pairs={{0,1},{1,0},{2,3},{3,2},{4,5},{5,4},{6,7},{7,6},{8,9},{9,8},{10,11... | collective-permute-start | bytes 270344 | tf_op jit(solution)/shard_map/ppermute | solution.py:59
  60.0 4.5 %collective-permute-start.14 = (bf16[88,512]{1,0:T(8,128)(2,1)S(1)}, bf16[88,512]{1,0:T(8,128)(2,1)S(1)}, u32[]{:S(2)}, u32[]{:S(2)}) collective-permute-start(bf16[88,512]{1,0:T(8,128)(2,1)S(1)} %get-tuple-element.69.refs_0_), channel_id=1, source_target_pairs={{0,2},{1,3},{2,0},{3,1},{4,6},{5,7},{6,4},{7,5},{8,10},{9,11},{10,... | collective-permute-start | bytes 270344 | tf_op jit(solution)/shard_map/ppermute | solution.py:59
  60.9 5.4 %collective-permute-start.15 = (bf16[88,512]{1,0:T(8,128)(2,1)S(1)}, bf16[88,512]{1,0:T(8,128)(2,1)S(1)}, u32[]{:S(2)}, u32[]{:S(2)}) collective-permute-start(bf16[88,512]{1,0:T(8,128)(2,1)S(1)} %get-tuple-element.69.refs_0_), channel_id=1, source_target_pairs={{0,3},{1,2},{2,1},{3,0},{4,7},{5,6},{6,5},{7,4},{8,11},{9,10},{10,... | collective-permute-start | bytes 270344 | tf_op jit(solution)/shard_map/ppermute | solution.py:59

commit v5 on v4

--- a/solution.py
+++ b/solution.py
@@ -50,8 +50,9 @@
         copy.wait()
 
 
-def slope(diff, inv_sq):
-    return -(diff * inv_sq) * jnp.exp(-0.5 * diff * diff * inv_sq)
+def slope(diff, inv_width):
+    ratio = diff * inv_width
+    return ratio * jnp.exp(ratio * ratio * -0.5)
 
 
 def xor_permute(value, axis, step):
@@ -59,11 +60,23 @@
     return lax.ppermute(value, axis, [(i, i ^ step) for i in range(count)])
 
 
+def mem_trade(steps, values):
+    return [v if s == 0 else xor_permute(v, "mem", s) for s, v in zip(steps, values)]
+
+
+def mem_steps(members):
+    return [0] + list(range(members - 1, 0, -1))
+
+
+def one_hot(rows, length):
+    cols = columns(rows.astype(F32))
+    spots = lax.broadcasted_iota(jnp.int32, (rows.shape[1], length), 1).astype(F32)
+    hot = [(cols[:, k : k + 1] == spots).astype(F32).astype(BF16) for k in range(rows.shape[0])]
+    return jnp.concatenate(hot, axis=0)
+
+
 def picked(rows, table, outs):
-    cols = columns(rows.astype(F32))
-    spots = lax.broadcasted_iota(jnp.int32, (rows.shape[1], table.shape[0]), 1).astype(F32)
-    hot = [(cols[:, k : k + 1] == spots).astype(F32).astype(BF16) for k in range(rows.shape[0])]
-    found = dot(jnp.concatenate(hot, axis=0), table).astype(BF16)
+    found = dot(one_hot(rows, table.shape[0]), table).astype(BF16)
     start = 0
     for out in outs:
         out[...] = found[start : start + out.shape[0], :]
@@ -76,8 +89,14 @@
 
 
 def first_pick_kernel(steps, send_ref, coarse_ref, out, rows_ref, table_ref, sems):
-    fetch([(send_ref, rows_ref), (coarse_ref, table_ref)], sems)
-    picked(send_rows_of(rows_ref, steps), table_ref[0], [out])
+    rows_copy = pltpu.make_async_copy(send_ref, rows_ref, sems.at[0])
+    table_copy = pltpu.make_async_copy(coarse_ref, table_ref, sems.at[1])
+    rows_copy.start()
+    table_copy.start()
+    rows_copy.wait()
+    hot = one_hot(send_rows_of(rows_ref, steps), table_ref.shape[1])
+    table_copy.wait()
+    out[...] = dot(hot, table_ref[0]).astype(BF16)
 
 
 def first_pick(send_rows, coarse, steps):
@@ -143,7 +162,7 @@
     kw_rows[...] = jnp.ones(kw_rows.shape, F32)
     kw_rows[0:1, :num_vars] = kw_ref[...]
     width = kw_rows[...].T[:padded, 0:1]
-    inv_ref[...] = 1.0 / (width * width)
+    inv_ref[...] = 1.0 / width
     target_ref[...] = jnp.zeros(target_ref.shape, F32)
     target_ref[:num_vars, :] = target_in_ref[:, pl.ds(start, piece)].astype(F32)
     me = lax.axis_index("dom")
@@ -261,55 +280,55 @@
     )(other, *mine)
 
 
-def early_kernel(tile, spread_ref, own_ref, one_ref, *refs):
+def early_kernel(tile, spread_ref, scale_ref, skip_ref, own_ref, one_ref, *refs):
     tables, out = refs[:-1], refs[-1]
     parts = [own_ref[...], one_ref[: own_ref.shape[0], :]] + [r[...] for r in tables]
     table = jnp.concatenate(parts + parts, axis=0)
-
-    def step(t, carry):
-        rows = pl.ds(pl.multiple_of(t * tile, tile), tile)
-        out[rows, :] = dot(spread_ref[rows, :], table)
-        return carry
-
-    lax.fori_loop(0, out.shape[0] // tile, step, 0, unroll=4)
-
-
-def early(spread_rows, tables, tile):
-    rows, width = spread_rows.shape[0], tables[0].shape[1]
-    return pl.pallas_call(
-        functools.partial(early_kernel, tile),
-        out_shape=jax.ShapeDtypeStruct((rows, width), F32),
-        in_specs=[pl.BlockSpec(memory_space=VMEM)] * (1 + len(tables)),
-        out_specs=pl.BlockSpec(memory_space=VMEM),
-        compiler_params=params(16),
-        cost_estimate=cost(1, 1),
-        name="early",
-    )(spread_rows, *tables)
-
-
-def late_kernel(tile, sum_ref, spread_ref, scale_ref, skip_ref, *refs):
-    tables, (x_ref, inner_ref, outer_ref) = refs[:-3], refs[-3:]
-    table = jnp.concatenate([r[...] for r in tables], axis=0)
-    count = x_ref.shape[0]
 
     def step(t, carry):
         start = pl.multiple_of(t * tile, tile)
         rows = pl.ds(start, tile)
         scale = columns(scale_ref[:, rows])[:, 0:1]
-        unpooled = scale * (sum_ref[rows, :] + dot(spread_ref[rows, :], table))
-        x_ref[rows, :] = (skip_ref[rows, :].astype(F32) + unpooled).astype(BF16)
+        out[rows, :] = skip_ref[rows, :].astype(F32) + scale * dot(spread_ref[rows, :], table)
         return carry
 
-    lax.fori_loop(0, count // tile, step, 0, unroll=4)
+    lax.fori_loop(0, out.shape[0] // tile, step, 0, unroll=4)
+
+
+def early(spread_rows, scale, skip, tables, tile):
+    return pl.pallas_call(
+        functools.partial(early_kernel, tile),
+        out_shape=jax.ShapeDtypeStruct(skip.shape, F32),
+        in_specs=[pl.BlockSpec(memory_space=VMEM)] * (3 + len(tables)),
+        out_specs=pl.BlockSpec(memory_space=VMEM),
+        compiler_params=params(16),
+        cost_estimate=cost(1, 1),
+        name="early",
+    )(spread_rows, scale, skip, *tables)
+
+
+def late_kernel(tile, sum_ref, spread_ref, scale_ref, *refs):
+    tables, (x_ref, inner_ref, outer_ref) = refs[:-3], refs[-3:]
+    table = jnp.concatenate([r[...] for r in tables], axis=0)
+    count = x_ref.shape[0]
+
+    def step(t, carry):
+        start = pl.multiple_of(t * tile, tile)
+        rows = pl.ds(start, tile)
+        scale = columns(scale_ref[:, rows])[:, 0:1]
+        x_ref[rows, :] = (sum_ref[rows, :] + scale * dot(spread_ref[rows, :], table)).astype(BF16)
+        return carry
+
+    lax.fori_loop(0, count // tile, step, 0, unroll=count // tile)
     odd = lax.rem(lax.axis_index("dom"), 2) == 1
     first, last = x_ref[:RIM, :], x_ref[count - RIM :, :]
     inner_ref[...] = jnp.where(odd, first, last)
     outer_ref[...] = jnp.where(odd, last, first)
 
 
-def late(sums, spread_rows, scale, skip, tables, tile):
+def late(sums, spread_rows, scale, tables, tile):
     rows, width = sums.shape
-    operands = (sums, spread_rows, scale, skip, *tables)
+    operands = (sums, spread_rows, scale, *tables)
     edge = jax.ShapeDtypeStruct((RIM, width), BF16)
     return pl.pallas_call(
         functools.partial(late_kernel, tile),
@@ -377,7 +396,7 @@
     all_ref[1 : tiles - 1] = done_ref[...]
     me = lax.axis_index("mem")
     per = tiles // members
-    for s, out in enumerate(outs):
+    for s, out in zip(mem_steps(members), outs):
         for k in range(per):
             out[:, k * tile : (k + 1) * tile] = all_ref[(me ^ s) * per + k]
 
@@ -425,20 +444,21 @@
 
 def score_kernel(members, weight_ref, inv_ref, target_ref, *refs):
     preds, outs = refs[:members], refs[members:]
-    inv_sq, weight = inv_ref[...], weight_ref[...]
+    inv_width, weight = inv_ref[...], weight_ref[...]
+    weight = weight * -inv_width
     values = [r[...].astype(F32) for r in preds]
     sums = [jnp.zeros(v.shape, F32) for v in values]
     for i in range(members):
         for j in range(i + 1, members):
-            phi = slope(values[i] - values[j], inv_sq)
+            phi = slope(values[i] - values[j], inv_width)
             sums[i] = sums[i] + phi
             sums[j] = sums[j] - phi
     for i in range(members):
-        total = sums[i] * (1.0 / members) - slope(values[i] - target_ref[...], inv_sq)
+        total = sums[i] * (1.0 / members) - slope(values[i] - target_ref[...], inv_width)
         outs[i][...] = (weight * total).astype(BF16)
 
 
-def score(weight, inv_sq, target, preds):
+def score(weight, inv_width, target, preds):
     members = len(preds)
     shape = preds[0].shape
     return pl.pallas_call(
@@ -449,7 +469,7 @@
         compiler_params=params(16),
         cost_estimate=cost(10 * preds[0].size * members * members, MIB, preds[0].size * members * members),
         name="score",
-    )(weight, inv_sq, target, *preds)
+    )(weight, inv_width, target, *preds)
 
 
 def head_kernel(members, mid_ref, end_ref, *refs):
@@ -457,9 +477,9 @@
     tiles, _, tile = all_ref.shape
     me = lax.axis_index("mem")
     per = tiles // members
-    for s in range(members):
+    for s, value in zip(mem_steps(members), scores):
         for k in range(per):
-            all_ref[(me ^ s) * per + k] = scores[s][:, k * tile : (k + 1) * tile]
+            all_ref[(me ^ s) * per + k] = value[:, k * tile : (k + 1) * tile]
     total = dot(all_ref[0], end_ref[:tile, :]) + dot(all_ref[tiles - 1], end_ref[tile:, :])
     for t in range(1, tiles - 1):
         total = total + dot(all_ref[t], mid_ref[(t - 1) * tile : t * tile, :])
@@ -557,21 +577,21 @@
     far = [xor_permute(v, "dom", s) for v, s in zip(pack(one, far), even)]
     two, three = xor_permute(two, "dom", 2), xor_permute(three, "dom", 3)
     sources = (up_index, up_weight, neighbors, w_head.T, area[None, :], targets, kernel_width[None, :])
-    first_rows, last_rows, scale, counts, head, weight, inv_sq, target = spread(
+    first_rows, last_rows, scale, counts, head, weight, inv_width, target = spread(
         own, live_counts, sources, steps, slots, 4, tile, padded, rows // members
     )
-    sums = early(first_rows, [own, one, two, three], tile)
-    x, inner, outer = late(sums, last_rows, scale, fine_skip, far, tile)
-    inner = xor_permute(inner, "dom", 1)
+    sums = early(first_rows, scale, fine_skip, [own, one, two, three], tile)
+    x, inner, outer = late(sums, last_rows, scale, far, tile)
     pairs = [(i, i + 1) for i in range(1, dom_count - 1, 2)]
     outer = lax.ppermute(outer, "dom", pairs + [(j, i) for i, j in pairs])
+    inner = xor_permute(inner, "dom", 1)
 
     mid, end, preds = update(members, x, counts, w_in, w_out, ln_gain[None, :], head, inner, outer)
-    preds = [preds[0]] + [xor_permute(preds[s], "mem", s) for s in range(1, members)]
-    scores = score(weight, inv_sq, target, preds)
-    scores = [scores[0]] + [xor_permute(scores[s], "mem", s) for s in range(1, members)]
+    trade = functools.partial(mem_trade, mem_steps(members))
+    preds = trade(preds)
+    scores = trade(score(weight, inv_width, target, preds))
     term, by_tile = head_terms(members, mid, end, scores)
-    terms = [term] + [xor_permute(term, "mem", s) for s in range(1, members)]
+    terms = trade([term] * members)
     grad_latent = latent_grad(head, by_tile)
     factor = 1.0 / math.sqrt(members * rows)
     return (grad_latent, head_total(terms, num_vars, factor).transpose(1, 2, 0))

time: 67.3 us -> 65.8 us (0.978)
  waiting for transfers between devices: 19.1 us -> 17.6 us
    ppermute x15, waiting for transfers between devices: 19.1 us -> 17.6 us  [xor_permute(): return lax.ppermute(value, axis, [(i, i ^ step) for i in range(count)])]
  transfers between devices with their start and end apart: 16 -> 16, of which waited for: 11 -> 10; matrix products, arithmetic and copies ran while one was open for 0% -> 0% of each run, Pallas kernels for 25% -> 26%
where the time goes in v5:
time: 65.8 us; the launch traced here: 65.6 us
  Pallas kernels  23.9 us (36%)
  starting transfers between devices  22.7 us (34%)
  waiting for transfers between devices  17.6 us (27%)
  between operations  1.43 us (2%)
    ppermute x15, starting transfers between devices, xor_permute(): return lax.ppermute(value, axis, [(i, i ^ step) for i in range(count)])  18.5 us
    ppermute x15, waiting for transfers between devices, xor_permute(): return lax.ppermute(value, axis, [(i, i ^ step) for i in range(count)])  17.6 us
    pallas_call x1, Pallas kernels, spread(): pl.pallas_call(functools.partial(spread_kernel, tile, steps), out_shape=[...  7.11 us
    pallas_call x2, Pallas kernels, update_call(): pl.pallas_call(kernel, out_shape=out_shape, in_specs=[pl.BlockSpec(memory...  6.25 us
    ppermute x1, starting transfers between devices, shards(): outer = lax.ppermute(outer, 'dom', pairs + [(j, i) for i, j in pairs])  4.25 us
    pallas_call x1, Pallas kernels, early(): pl.pallas_call(functools.partial(early_kernel, tile), out_shape=jax.Shape...  2.73 us
    pallas_call x1, Pallas kernels, latent_grad(): pl.pallas_call(latent_kernel, out_shape=jax.ShapeDtypeStruct((1, tiles *...  2.05 us
    pallas_call x1, Pallas kernels, first_pick(): pl.pallas_call(functools.partial(first_pick_kernel, steps), out_shape=[ja...  1.6 us
  transfers between devices with their start and end apart: 16, of which 10 were waited for; matrix products, arithmetic and copies ran while one was open for 0% of the time, Pallas kernels for 26%

profile of v5, /device:TPU:24, one launch (start us, length us, event | category | flops | bytes accessed | tf_op | source)
XLA Modules:
  0.0 65.6 jit_solution(11646432742044758673)
XLA Ops:
  0.6 0.0 copy-start
  0.6 1.6 %pick_first.1 = (bf16[384,512]{1,0:T(8,128)(2,1)S(1)}, s32[1,8,128]{2,1,0:T(8,128)S(1)}, bf16[1,512,512]{2,1,0:T(8,128)(2,1)S(1)}) custom-call(s32[1,8,128]{2,1,0:T(8,128)} %send_ref.1, bf16[1,512,512]{2,1,0:T(8,128)(2,1)} %coarse_ref.1), custom_call_target="tpu_custom_call" | custom-call | flops 1 | bytes 1 | tf_op jit(solution)/shard_map/pick_first/pallas_call | solution.py:104
  2.2 0.1 collective-permute-start
  2.3 0.6 pick.1
  3.0 1.1 %collective-permute-done.one_ref.other_ref = bf16[384,512]{1,0:T(8,128)(2,1)S(1)} collective-permute-done((bf16[384,512]{1,0:T(8,128)(2,1)S(1)}, bf16[384,512]{1,0:T(8,128)(2,1)S(1)}, u32[]{:S(2)}, u32[]{:S(2)}) %collective-permute-start) | collective-permute-done | bytes 393248 | tf_op jit(solution)/shard_map/ppermute | solution.py:60
  4.1 0.4 collective-permute-start.3
  4.5 2.5 %collective-permute-start.4 = (bf16[256,512]{1,0:T(8,128)(2,1)S(1)}, bf16[256,512]{1,0:T(8,128)(2,1)S(1)}, u32[]{:S(2)}, u32[]{:S(2)}) collective-permute-start(bf16[256,512]{1,0:T(8,128)(2,1)S(1)} %get-tuple-element.49), channel_id=1, source_target_pairs={{0,24},{4,28},{8,16},{12,20},{16,8},{20,12},{24,0},{28,4},{1,25},{... | collective-permute-start | bytes 786440 | tf_op jit(solution)/shard_map/ppermute | solution.py:60
  6.9 0.7 %collective-permute-start.1 = (bf16[128,512]{1,0:T(8,128)(2,1)S(1)}, bf16[128,512]{1,0:T(8,128)(2,1)S(1)}, u32[]{:S(2)}, u32[]{:S(2)}) collective-permute-start(bf16[128,512]{1,0:T(8,128)(2,1)S(1)} %get-tuple-element.43), channel_id=1, source_target_pairs={{0,8},{4,12},{8,0},{12,4},{16,24},{20,28},{24,16},{28,20},{1,9},{5... | collective-permute-start | bytes 393224 | tf_op jit(solution)/shard_map/ppermute | solution.py:60
  7.6 0.2 collective-permute-start.2
  8.5 7.1 %spread.1 = (bf16[2048,1024]{1,0:T(8,128)(2,1)S(1)}, bf16[2048,512]{1,0:T(8,128)(2,1)S(1)}, f32[1,2048]{1,0:T(1,128)S(1)}, bf16[8,256,512]{2,1,0:T(8,128)(2,1)S(...) custom-call(s32[1]{0:T(128)S(6)} %copy.16.live_ref, ...), custom_call_target="tpu_custom_call" | custom-call | flops 1 | bytes 1 | tf_op jit(solution)/shard_map/spread/pallas_call | solution.py:237
  15.6 4.0 %collective-permute-done.1.refs_0_ = bf16[128,512]{1,0:T(8,128)(2,1)S(1)} collective-permute-done((bf16[128,512]{1,0:T(8,128)(2,1)S(1)}, bf16[128,512]{1,0:T(8,128)(2,1)S(1)}, u32[]{:S(2)}, u32[]{:S(2)}) %collective-permute-start.1) | collective-permute-done | bytes 131104 | tf_op jit(solution)/shard_map/ppermute | solution.py:60
  19.7 2.0 %collective-permute-done.2.refs_1_ = bf16[128,512]{1,0:T(8,128)(2,1)S(1)} collective-permute-done((bf16[128,512]{1,0:T(8,128)(2,1)S(1)}, bf16[128,512]{1,0:T(8,128)(2,1)S(1)}, u32[]{:S(2)}, u32[]{:S(2)}) %collective-permute-start.2) | collective-permute-done | bytes 131104 | tf_op jit(solution)/shard_map/ppermute | solution.py:60
  21.7 0.0 copy-done
  21.7 2.7 %early.1.sum_ref = f32[2048,512]{1,0:T(8,128)S(1)} custom-call(bf16[2048,1024]{1,0:T(8,128)(2,1)S(1)} %get-tuple-element.40.spread_ref, f32[1,2048]{1,0:T(1,128)S(1)} %get-tuple-element.41.scale_ref, bf16[2048,512]{1,0:T(8,128)(2,1)S(1)} %copy-done, bf16[128,512]{1,0:T(8,128)(2,1)S(1)} %get-tuple-element.38.refs_7_.own_ref, ...), custom_call_target="tpu_custom_call" | custom-call | flops 1 | bytes 1 | tf_op jit(solution)/shard_map/early/pallas_call | solution.py:299
  24.4 0.2 collective-permute-done.3.refs_0_
  24.6 0.0 collective-permute-done.4.refs_1_
  24.6 1.4 %late.1 = (bf16[2048,512]{1,0:T(8,128)(2,1)S(1)}, bf16[128,512]{1,0:T(8,128)(2,1)S(1)}, bf16[128,512]{1,0:T(8,128)(2,1)S(1)}) custom-call(f32[2048,512]{1,0:T(8,128)S(1)} %early.1.sum_ref, bf16[2048,512]{1,0:T(8,128)(2,1)S(1)} %get-tuple-element.45.spread_ref, f32[1,2048]{1,0:T(1,128)S(1)} %get-tuple-element.41.scale_ref, ...), custom_call_target="tpu_custom_call" | custom-call | flops 1073741824 | bytes 8388608 | tf_op jit(solution)/shard_map/late/pallas_call | solution.py:333
  26.1 3.9 %collective-permute-start.5 = (bf16[128,512]{1,0:T(8,128)(2,1)S(1)}, bf16[128,512]{1,0:T(8,128)(2,1)S(1)}, u32[]{:S(2)}, u32[]{:S(2)}) collective-permute-start(bf16[128,512]{1,0:T(8,128)(2,1)S(1)} %get-tuple-element.53), channel_id=1, source_target_pairs={{0,4},{4,0},{8,12},{12,8},{16,20},{20,16},{24,28},{28,24},{1,5},{5... | collective-permute-start | bytes 393224 | tf_op jit(solution)/shard_map/ppermute | solution.py:60
  30.0 4.3 %collective-permute-start.6 = (bf16[128,512]{1,0:T(8,128)(2,1)S(1)}, bf16[128,512]{1,0:T(8,128)(2,1)S(1)}, u32[]{:S(2)}, u32[]{:S(2)}) collective-permute-start(bf16[128,512]{1,0:T(8,128)(2,1)S(1)} %get-tuple-element.54), channel_id=1, source_target_pairs={{4,8},{12,16},{20,24},{8,4},{16,12},{24,20},{5,9},{13,17},{21,25},... | collective-permute-start | bytes 393224 | tf_op jit(solution)/shard_map/ppermute | solution.py:586
  34.3 0.0 copy-done.1
  34.3 0.0 copy-done.2
  34.3 0.0 copy-done.3
  34.3 4.4 %inner.1 = (bf16[1536,512]{1,0:T(8,128)(2,1)S(1)}, bf16[6,88,256]{2,1,0:T(8,128)(2,1)S(1)}) custom-call(bf16[2048,512]{1,0:T(8,128)(2,1)S(1)} %get-tuple-element.50.x_ref, bf16[8,256,512]{2,1,0:T(8,128)(2,1)S(1)} %get-tuple-element.51.count_ref, bf16[1024,512]{1,0:T(8,128)(2,1)S(1)} %copy-done.1, bf16[512,512]{1,0:T(8,128)(2,1)S(1)} %copy-done.2, ...), custom_call_target="tpu_custom_call" | custom-call | flops 4026531840 | bytes 8388608 | tf_op jit(solution)/shard_map/inner/pallas_call | solution.py:405
  38.8 0.0 collective-permute-done.5.inner_ref
  38.8 0.0 collective-permute-done.6.outer_ref
  38.8 1.8 %outer.1 = (bf16[512,512]{1,0:T(8,128)(2,1)S(1)}, bf16[88,512]{1,0:T(8,128)(2,1)S(1)}, bf16[88,512]{1,0:T(8,128)(2,1)S(1)}, bf16[88,512]{1,0:T(8,128)(2,1)S(1)}, bf16[88,512]{1,0:T(8,128)(2,1)S(1)}) custom-call(bf16[2048,512]{1,0:T(8,128)(2,1)S(1)} %get-tuple-element.50.x_ref, bf16[8,256,512]{2,1,0:T(8,128)(2,1)S(1)} %get-tuple-element.51.count_ref, ...), custom_call_target="tpu_custom_call" | custom-call | flops 1342177280 | bytes 8388608 | tf_op jit(solution)/shard_map/outer/pallas_call | solution.py:405
  40.6 2.5 %collective-permute-start.7 = (bf16[88,512]{1,0:T(8,128)(2,1)S(1)}, bf16[88,512]{1,0:T(8,128)(2,1)S(1)}, u32[]{:S(2)}, u32[]{:S(2)}) collective-permute-start(bf16[88,512]{1,0:T(8,128)(2,1)S(1)} %get-tuple-element.61), channel_id=1, source_target_pairs={{0,3},{1,2},{2,1},{3,0},{4,7},{5,6},{6,5},{7,4},{8,11},{9,10},{10,... | collective-permute-start | bytes 270344 | tf_op jit(solution)/shard_map/ppermute | solution.py:60
  43.1 0.5 collective-permute-start.8
  43.6 0.6 collective-permute-start.9
  44.2 1.9 %collective-permute-done.7.refs_1_ = bf16[88,512]{1,0:T(8,128)(2,1)S(1)} collective-permute-done((bf16[88,512]{1,0:T(8,128)(2,1)S(1)}, bf16[88,512]{1,0:T(8,128)(2,1)S(1)}, u32[]{:S(2)}, u32[]{:S(2)}) %collective-permute-start.7) | collective-permute-done | bytes 90144 | tf_op jit(solution)/shard_map/ppermute | solution.py:60
  46.1 2.9 %collective-permute-done.8.refs_2_ = bf16[88,512]{1,0:T(8,128)(2,1)S(1)} collective-permute-done((bf16[88,512]{1,0:T(8,128)(2,1)S(1)}, bf16[88,512]{1,0:T(8,128)(2,1)S(1)}, u32[]{:S(2)}, u32[]{:S(2)}) %collective-permute-start.8) | collective-permute-done | bytes 90144 | tf_op jit(solution)/shard_map/ppermute | solution.py:60
  49.0 0.0 collective-permute-done.9.refs_3_
  49.0 0.8 %score.1 = (bf16[88,512]{1,0:T(8,128)(2,1)S(1)}, bf16[88,512]{1,0:T(8,128)(2,1)S(1)}, bf16[88,512]{1,0:T(8,128)(2,1)S(1)}, bf16[88,512]{1,0:T(8,128)(2,1)S(1)}) custom-call(f32[1,512]{1,0:T(1,128)S(1)} %get-tuple-element.57.weight_ref, f32[88,1]{1,0:T(8,128)S(1)} %get-tuple-element.58.inv_ref, f32[88,512]{1,0:T(8,128)S(1)} %get-tuple-element.59.target_ref, ...), custom_call_target="tpu_custom_call" | custom-call | flops 7208960 | bytes 1048576 | tf_op jit(solution)/shard_map/score/pallas_call | solution.py:464
  49.8 1.3 %collective-permute-start.10 = (bf16[88,512]{1,0:T(8,128)(2,1)S(1)}, bf16[88,512]{1,0:T(8,128)(2,1)S(1)}, u32[]{:S(2)}, u32[]{:S(2)}) collective-permute-start(bf16[88,512]{1,0:T(8,128)(2,1)S(1)} %get-tuple-element.65), channel_id=1, source_target_pairs={{0,3},{1,2},{2,1},{3,0},{4,7},{5,6},{6,5},{7,4},{8,11},{9,10},{10,... | collective-permute-start | bytes 270344 | tf_op jit(solution)/shard_map/ppermute | solution.py:60
  51.0 0.9 %collective-permute-start.11 = (bf16[88,512]{1,0:T(8,128)(2,1)S(1)}, bf16[88,512]{1,0:T(8,128)(2,1)S(1)}, u32[]{:S(2)}, u32[]{:S(2)}) collective-permute-start(bf16[88,512]{1,0:T(8,128)(2,1)S(1)} %get-tuple-element.66), channel_id=1, source_target_pairs={{0,2},{1,3},{2,0},{3,1},{4,6},{5,7},{6,4},{7,5},{8,10},{9,11},{10,... | collective-permute-start | bytes 270344 | tf_op jit(solution)/shard_map/ppermute | solution.py:60
  51.9 1.4 %collective-permute-start.12 = (bf16[88,512]{1,0:T(8,128)(2,1)S(1)}, bf16[88,512]{1,0:T(8,128)(2,1)S(1)}, u32[]{:S(2)}, u32[]{:S(2)}) collective-permute-start(bf16[88,512]{1,0:T(8,128)(2,1)S(1)} %get-tuple-element.67), channel_id=1, source_target_pairs={{0,1},{1,0},{2,3},{3,2},{4,5},{5,4},{6,7},{7,6},{8,9},{9,8},{10,11... | collective-permute-start | bytes 270344 | tf_op jit(solution)/shard_map/ppermute | solution.py:60
  53.3 2.9 %collective-permute-done.10.refs_1_ = bf16[88,512]{1,0:T(8,128)(2,1)S(1)} collective-permute-done((bf16[88,512]{1,0:T(8,128)(2,1)S(1)}, bf16[88,512]{1,0:T(8,128)(2,1)S(1)}, u32[]{:S(2)}, u32[]{:S(2)}) %collective-permute-start.10) | collective-permute-done | bytes 90144 | tf_op jit(solution)/shard_map/ppermute | solution.py:60
  56.2 1.5 %collective-permute-done.11.refs_2_ = bf16[88,512]{1,0:T(8,128)(2,1)S(1)} collective-permute-done((bf16[88,512]{1,0:T(8,128)(2,1)S(1)}, bf16[88,512]{1,0:T(8,128)(2,1)S(1)}, u32[]{:S(2)}, u32[]{:S(2)}) %collective-permute-start.11) | collective-permute-done | bytes 90144 | tf_op jit(solution)/shard_map/ppermute | solution.py:60
  57.7 0.0 collective-permute-done.12.refs_3_
  57.7 0.5 head_terms.1
  58.2 1.2 %collective-permute-start.13 = (bf16[88,512]{1,0:T(8,128)(2,1)S(1)}, bf16[88,512]{1,0:T(8,128)(2,1)S(1)}, u32[]{:S(2)}, u32[]{:S(2)}) collective-permute-start(bf16[88,512]{1,0:T(8,128)(2,1)S(1)} %get-tuple-element.69.refs_0_), channel_id=1, source_target_pairs={{0,3},{1,2},{2,1},{3,0},{4,7},{5,6},{6,5},{7,4},{8,11},{9,10},{10,... | collective-permute-start | bytes 270344 | tf_op jit(solution)/shard_map/ppermute | solution.py:60
  59.4 0.9 %collective-permute-start.14 = (bf16[88,512]{1,0:T(8,128)(2,1)S(1)}, bf16[88,512]{1,0:T(8,128)(2,1)S(1)}, u32[]{:S(2)}, u32[]{:S(2)}) collective-permute-start(bf16[88,512]{1,0:T(8,128)(2,1)S(1)} %get-tuple-element.69.refs_0_), channel_id=1, source_target_pairs={{0,2},{1,3},{2,0},{3,1},{4,6},{5,7},{6,4},{7,5},{8,10},{9,11},{10,... | collective-permute-start | bytes 270344 | tf_op jit(solution)/shard_map/ppermute | solution.py:60
  60.3 1.4 %collective-permute-start.15 = (bf16[88,512]{1,0:T(8,128)(2,1)S(1)}, bf16[88,512]{1,0:T(8,128)(2,1)S(1)}, u32[]{:S(2)}, u32[]{:S(2)}) collective-permute-start(bf16[88,512]{1,0:T(8,128)(2,1)S(1)} %get-tuple-element.69.refs_0_), channel_id=1, source_target_pairs={{0,1},{1,0},{2,3},{3,2},{4,5},{5,4},{6,7},{7,6},{8,9},{9,8},{10,11... | collective-permute-start | bytes 270344 | tf_op jit(solution)/shard_map/ppermute | solution.py:60
  61.7 2.1 %latent_grad.1 = bf16[1,2048,512]{2,1,0:T(8,128)(2,1)} custom-call(bf16[88,512]{1,0:T(8,128)(2,1)S(1)} %get-tuple-element.39.head_ref, bf16[8,88,256]{2,1,0:T(8,128)(2,1)S(1)} %get-tuple-element.68.score_ref), custom_call_target="tpu_custom_call" | custom-call | flops 184549376 | bytes 3145728 | tf_op jit(solution)/shard_map/latent_grad/pallas_call | solution.py:517
  63.8 0.0 collective-permute-done.13.refs_1_
  63.8 0.8 %collective-permute-done.14.refs_2_ = bf16[88,512]{1,0:T(8,128)(2,1)S(1)} collective-permute-done((bf16[88,512]{1,0:T(8,128)(2,1)S(1)}, bf16[88,512]{1,0:T(8,128)(2,1)S(1)}, u32[]{:S(2)}, u32[]{:S(2)}) %collective-permute-start.14) | collective-permute-done | bytes 90144 | tf_op jit(solution)/shard_map/ppermute | solution.py:60
  64.6 0.2 collective-permute-done.15.refs_3_
  64.9 0.8 %head_total.1 = f32[83,1,512]{2,1,0:T(1,128)} custom-call(bf16[88,512]{1,0:T(8,128)(2,1)S(1)} %get-tuple-element.69.refs_0_, bf16[88,512]{1,0:T(8,128)(2,1)S(1)} %collective-permute-done.13.refs_1_, bf16[88,512]{1,0:T(8,128)(2,1)S(1)} %collective-permute-done.14.refs_2_, bf16[88,512]{1,0:T(8,128)(2,1)S(1)} %collective-permute-done.15.refs_3_), custom_call_target="tpu_custom_call" | custom-call | flops 180224 | bytes 1048576 | tf_op jit(solution)/shard_map/head_total/pallas_call | solution.py:537
  (4 shorter events, 0.0 us)
Async XLA Ops:
  0.6 21.0 %copy-start = (bf16[2048,512]{1,0:T(8,128)(2,1)S(1)}, bf16[2048,512]{1,0:T(8,128)(2,1)}, u32[]{:S(2)}) copy-start(bf16[2048,512]{1,0:T(8,128)(2,1)} %skip_ref.1) | copy-start | bytes 6291460
  2.2 1.8 %collective-permute-start = (bf16[384,512]{1,0:T(8,128)(2,1)S(1)}, bf16[384,512]{1,0:T(8,128)(2,1)S(1)}, u32[]{:S(2)}, u32[]{:S(2)}) collective-permute-start(bf16[384,512]{1,0:T(8,128)(2,1)S(1)} %get-tuple-element.42), channel_id=1, source_target_pairs={{0,4},{4,0},{8,12},{12,8},{16,20},{20,16},{24,28},{28,24},{1,5},{5... | collective-permute-start | bytes 1179656 | tf_op jit(solution)/shard_map/ppermute | solution.py:60
  4.1 20.6 %collective-permute-start.3 = (bf16[256,512]{1,0:T(8,128)(2,1)S(1)}, bf16[256,512]{1,0:T(8,128)(2,1)S(1)}, u32[]{:S(2)}, u32[]{:S(2)}) collective-permute-start(bf16[256,512]{1,0:T(8,128)(2,1)S(1)} %get-tuple-element.48), channel_id=1, source_target_pairs={{0,16},{4,20},{8,24},{12,28},{16,0},{20,4},{24,8},{28,12},{1,17},{... | collective-permute-start | bytes 786440 | tf_op jit(solution)/shard_map/ppermute | solution.py:60
  4.5 20.2 %collective-permute-start.4 = (bf16[256,512]{1,0:T(8,128)(2,1)S(1)}, bf16[256,512]{1,0:T(8,128)(2,1)S(1)}, u32[]{:S(2)}, u32[]{:S(2)}) collective-permute-start(bf16[256,512]{1,0:T(8,128)(2,1)S(1)} %get-tuple-element.49), channel_id=1, source_target_pairs={{0,24},{4,28},{8,16},{12,20},{16,8},{20,12},{24,0},{28,4},{1,25},{... | collective-permute-start | bytes 786440 | tf_op jit(solution)/shard_map/ppermute | solution.py:60
  6.9 12.7 %collective-permute-start.1 = (bf16[128,512]{1,0:T(8,128)(2,1)S(1)}, bf16[128,512]{1,0:T(8,128)(2,1)S(1)}, u32[]{:S(2)}, u32[]{:S(2)}) collective-permute-start(bf16[128,512]{1,0:T(8,128)(2,1)S(1)} %get-tuple-element.43), channel_id=1, source_target_pairs={{0,8},{4,12},{8,0},{12,4},{16,24},{20,28},{24,16},{28,20},{1,9},{5... | collective-permute-start | bytes 393224 | tf_op jit(solution)/shard_map/ppermute | solution.py:60
  7.6 14.0 %collective-permute-start.2 = (bf16[128,512]{1,0:T(8,128)(2,1)S(1)}, bf16[128,512]{1,0:T(8,128)(2,1)S(1)}, u32[]{:S(2)}, u32[]{:S(2)}) collective-permute-start(bf16[128,512]{1,0:T(8,128)(2,1)S(1)} %get-tuple-element.44), channel_id=1, source_target_pairs={{0,12},{4,8},{8,4},{12,0},{16,28},{20,24},{24,20},{28,16},{1,13},{... | collective-permute-start | bytes 393224 | tf_op jit(solution)/shard_map/ppermute | solution.py:60
  24.6 9.7 %copy-start.1 = (bf16[1024,512]{1,0:T(8,128)(2,1)S(1)}, bf16[1024,512]{1,0:T(8,128)(2,1)}, u32[]{:S(2)}) copy-start(bf16[1024,512]{1,0:T(8,128)(2,1)} %w_in_ref.3) | copy-start | bytes 3145732
  24.6 9.7 %copy-start.2 = (bf16[512,512]{1,0:T(8,128)(2,1)S(1)}, bf16[512,512]{1,0:T(8,128)(2,1)}, u32[]{:S(2)}) copy-start(bf16[512,512]{1,0:T(8,128)(2,1)} %w_out_ref.3) | copy-start | bytes 1572868
  24.6 9.7 %copy-start.3 = (f32[512]{0:T(512)S(1)}, f32[512]{0:T(512)}, u32[]{:S(2)}) copy-start(f32[512]{0:T(512)} %param.26) | copy-start | bytes 6148
  26.1 12.7 %collective-permute-start.5 = (bf16[128,512]{1,0:T(8,128)(2,1)S(1)}, bf16[128,512]{1,0:T(8,128)(2,1)S(1)}, u32[]{:S(2)}, u32[]{:S(2)}) collective-permute-start(bf16[128,512]{1,0:T(8,128)(2,1)S(1)} %get-tuple-element.53), channel_id=1, source_target_pairs={{0,4},{4,0},{8,12},{12,8},{16,20},{20,16},{24,28},{28,24},{1,5},{5... | collective-permute-start | bytes 393224 | tf_op jit(solution)/shard_map/ppermute | solution.py:60
  30.0 8.7 %collective-permute-start.6 = (bf16[128,512]{1,0:T(8,128)(2,1)S(1)}, bf16[128,512]{1,0:T(8,128)(2,1)S(1)}, u32[]{:S(2)}, u32[]{:S(2)}) collective-permute-start(bf16[128,512]{1,0:T(8,128)(2,1)S(1)} %get-tuple-element.54), channel_id=1, source_target_pairs={{4,8},{12,16},{20,24},{8,4},{16,12},{24,20},{5,9},{13,17},{21,25},... | collective-permute-start | bytes 393224 | tf_op jit(solution)/shard_map/ppermute | solution.py:586
  40.6 5.5 %collective-permute-start.7 = (bf16[88,512]{1,0:T(8,128)(2,1)S(1)}, bf16[88,512]{1,0:T(8,128)(2,1)S(1)}, u32[]{:S(2)}, u32[]{:S(2)}) collective-permute-start(bf16[88,512]{1,0:T(8,128)(2,1)S(1)} %get-tuple-element.61), channel_id=1, source_target_pairs={{0,3},{1,2},{2,1},{3,0},{4,7},{5,6},{6,5},{7,4},{8,11},{9,10},{10,... | collective-permute-start | bytes 270344 | tf_op jit(solution)/shard_map/ppermute | solution.py:60
  43.1 5.8 %collective-permute-start.8 = (bf16[88,512]{1,0:T(8,128)(2,1)S(1)}, bf16[88,512]{1,0:T(8,128)(2,1)S(1)}, u32[]{:S(2)}, u32[]{:S(2)}) collective-permute-start(bf16[88,512]{1,0:T(8,128)(2,1)S(1)} %get-tuple-element.62), channel_id=1, source_target_pairs={{0,2},{1,3},{2,0},{3,1},{4,6},{5,7},{6,4},{7,5},{8,10},{9,11},{10,... | collective-permute-start | bytes 270344 | tf_op jit(solution)/shard_map/ppermute | solution.py:60
  43.6 5.4 %collective-permute-start.9 = (bf16[88,512]{1,0:T(8,128)(2,1)S(1)}, bf16[88,512]{1,0:T(8,128)(2,1)S(1)}, u32[]{:S(2)}, u32[]{:S(2)}) collective-permute-start(bf16[88,512]{1,0:T(8,128)(2,1)S(1)} %get-tuple-element.63), channel_id=1, source_target_pairs={{0,1},{1,0},{2,3},{3,2},{4,5},{5,4},{6,7},{7,6},{8,9},{9,8},{10,11... | collective-permute-start | bytes 270344 | tf_op jit(solution)/shard_map/ppermute | solution.py:60
  49.8 6.4 %collective-permute-start.10 = (bf16[88,512]{1,0:T(8,128)(2,1)S(1)}, bf16[88,512]{1,0:T(8,128)(2,1)S(1)}, u32[]{:S(2)}, u32[]{:S(2)}) collective-permute-start(bf16[88,512]{1,0:T(8,128)(2,1)S(1)} %get-tuple-element.65), channel_id=1, source_target_pairs={{0,3},{1,2},{2,1},{3,0},{4,7},{5,6},{6,5},{7,4},{8,11},{9,10},{10,... | collective-permute-start | bytes 270344 | tf_op jit(solution)/shard_map/ppermute | solution.py:60
  51.0 6.7 %collective-permute-start.11 = (bf16[88,512]{1,0:T(8,128)(2,1)S(1)}, bf16[88,512]{1,0:T(8,128)(2,1)S(1)}, u32[]{:S(2)}, u32[]{:S(2)}) collective-permute-start(bf16[88,512]{1,0:T(8,128)(2,1)S(1)} %get-tuple-element.66), channel_id=1, source_target_pairs={{0,2},{1,3},{2,0},{3,1},{4,6},{5,7},{6,4},{7,5},{8,10},{9,11},{10,... | collective-permute-start | bytes 270344 | tf_op jit(solution)/shard_map/ppermute | solution.py:60
  51.9 5.8 %collective-permute-start.12 = (bf16[88,512]{1,0:T(8,128)(2,1)S(1)}, bf16[88,512]{1,0:T(8,128)(2,1)S(1)}, u32[]{:S(2)}, u32[]{:S(2)}) collective-permute-start(bf16[88,512]{1,0:T(8,128)(2,1)S(1)} %get-tuple-element.67), channel_id=1, source_target_pairs={{0,1},{1,0},{2,3},{3,2},{4,5},{5,4},{6,7},{7,6},{8,9},{9,8},{10,11... | collective-permute-start | bytes 270344 | tf_op jit(solution)/shard_map/ppermute | solution.py:60
  58.2 5.6 %collective-permute-start.13 = (bf16[88,512]{1,0:T(8,128)(2,1)S(1)}, bf16[88,512]{1,0:T(8,128)(2,1)S(1)}, u32[]{:S(2)}, u32[]{:S(2)}) collective-permute-start(bf16[88,512]{1,0:T(8,128)(2,1)S(1)} %get-tuple-element.69.refs_0_), channel_id=1, source_target_pairs={{0,3},{1,2},{2,1},{3,0},{4,7},{5,6},{6,5},{7,4},{8,11},{9,10},{10,... | collective-permute-start | bytes 270344 | tf_op jit(solution)/shard_map/ppermute | solution.py:60
  59.4 5.2 %collective-permute-start.14 = (bf16[88,512]{1,0:T(8,128)(2,1)S(1)}, bf16[88,512]{1,0:T(8,128)(2,1)S(1)}, u32[]{:S(2)}, u32[]{:S(2)}) collective-permute-start(bf16[88,512]{1,0:T(8,128)(2,1)S(1)} %get-tuple-element.69.refs_0_), channel_id=1, source_target_pairs={{0,2},{1,3},{2,0},{3,1},{4,6},{5,7},{6,4},{7,5},{8,10},{9,11},{10,... | collective-permute-start | bytes 270344 | tf_op jit(solution)/shard_map/ppermute | solution.py:60
  60.3 4.5 %collective-permute-start.15 = (bf16[88,512]{1,0:T(8,128)(2,1)S(1)}, bf16[88,512]{1,0:T(8,128)(2,1)S(1)}, u32[]{:S(2)}, u32[]{:S(2)}) collective-permute-start(bf16[88,512]{1,0:T(8,128)(2,1)S(1)} %get-tuple-element.69.refs_0_), channel_id=1, source_target_pairs={{0,1},{1,0},{2,3},{3,2},{4,5},{5,4},{6,7},{7,6},{8,9},{9,8},{10,11... | collective-permute-start | bytes 270344 | tf_op jit(solution)/shard_map/ppermute | solution.py:60

commit v6 on v5

--- a/solution.py
+++ b/solution.py
@@ -149,8 +149,8 @@
 
 
 def spread_kernel(tile, steps, live_ref, *refs):
-    sources, outs, scratch = refs[:7], refs[8:16], refs[16:]
-    first_ref, last_ref, scale_ref, count_ref, head_ref, area_ref, inv_ref, target_ref = outs
+    sources, outs, scratch = refs[:7], refs[8:17], refs[17:]
+    first_ref, mid_ref, last_ref, scale_ref, count_ref, head_ref, area_ref, inv_ref, target_ref = outs
     held, kw_rows, sems = scratch[:7], scratch[7], scratch[8]
     fetch(list(zip(sources, held)), sems)
     index_ref, weight_ref, nb_ref, head_in_ref, area_in_ref, target_in_ref, kw_ref = held
@@ -167,7 +167,8 @@
     target_ref[:num_vars, :] = target_in_ref[:, pl.ds(start, piece)].astype(F32)
     me = lax.axis_index("dom")
     rows = first_ref.shape[0]
-    cut = first_ref.shape[1] // 2
+    near = first_ref.shape[1] // 2
+    cut = near + mid_ref.shape[1] // 2
     slots = cut + last_ref.shape[1]
     span = count_ref.shape[2]
     part = 32
@@ -206,7 +207,7 @@
         weight = columns(w / scale)
         high = weight.astype(BF16)
         low = (weight - high.astype(F32)).astype(BF16)
-        near = narrow(nb_ref[:, lanes] - start)
+        around = narrow(nb_ref[:, lanes] - start)
         for r in range(0, tile, part):
             here = slice(r, r + part)
             rows_here = pl.ds(pl.multiple_of(start + r, part), part)
@@ -216,19 +217,21 @@
                 hit = index[here, k : k + 1] == spots
                 total = jnp.where(hit, high[here, k : k + 1], total)
                 rest = jnp.where(hit[:, :cut], low[here, k : k + 1], rest)
-            first_ref[rows_here, :cut] = total[:, :cut]
-            first_ref[rows_here, cut:] = rest
+            first_ref[rows_here, :near] = total[:, :near]
+            first_ref[rows_here, near:] = rest[:, :near]
+            mid_ref[rows_here, : cut - near] = total[:, near:cut]
+            mid_ref[rows_here, cut - near :] = rest[:, near:]
             last_ref[rows_here, :] = total[:, cut:]
             counts = jnp.zeros((part, span), BF16)
             for k in range(nb_ref.shape[0]):
-                counts = counts + jnp.where(near[here, k : k + 1] == places, one, zero)
+                counts = counts + jnp.where(around[here, k : k + 1] == places, one, zero)
             count_ref[t, here, :] = counts
         return carry
 
     lax.fori_loop(0, rows // tile, step, 0)
 
 
-def spread(token, live_counts, sources, steps, slots, split, tile, padded, piece):
+def spread(token, live_counts, sources, steps, slots, near, split, tile, padded, piece):
     up_index, head = sources[0], sources[3]
     rows = up_index.shape[1]
     tiles = rows // tile
@@ -237,7 +240,8 @@
     return pl.pallas_call(
         functools.partial(spread_kernel, tile, steps),
         out_shape=[
-            jax.ShapeDtypeStruct((rows, 2 * cut), BF16),
+            jax.ShapeDtypeStruct((rows, 2 * near * slots), BF16),
+            jax.ShapeDtypeStruct((rows, 2 * (cut - near * slots)), BF16),
             jax.ShapeDtypeStruct((rows, total - cut), BF16),
             jax.ShapeDtypeStruct((1, rows), F32),
             jax.ShapeDtypeStruct((tiles, tile, span), BF16),
@@ -249,7 +253,7 @@
         in_specs=[pl.BlockSpec(memory_space=pltpu.SMEM)]
         + [pl.BlockSpec(memory_space=pltpu.HBM)] * 7
         + [pl.BlockSpec(memory_space=VMEM)],
-        out_specs=[pl.BlockSpec(memory_space=VMEM)] * 8,
+        out_specs=[pl.BlockSpec(memory_space=VMEM)] * 9,
         scratch_shapes=[VMEM(v.shape, v.dtype) for v in sources]
         + [VMEM((8, 128), F32), pltpu.SemaphoreType.DMA((7,))],
         compiler_params=params(16),
@@ -280,31 +284,31 @@
     )(other, *mine)
 
 
-def early_kernel(tile, spread_ref, scale_ref, skip_ref, own_ref, one_ref, *refs):
+def part_kernel(tile, lengths, spread_ref, scale_ref, base_ref, *refs):
     tables, out = refs[:-1], refs[-1]
-    parts = [own_ref[...], one_ref[: own_ref.shape[0], :]] + [r[...] for r in tables]
+    parts = [r[:length, :] for r, length in zip(tables, lengths)]
     table = jnp.concatenate(parts + parts, axis=0)
 
     def step(t, carry):
         start = pl.multiple_of(t * tile, tile)
         rows = pl.ds(start, tile)
         scale = columns(scale_ref[:, rows])[:, 0:1]
-        out[rows, :] = skip_ref[rows, :].astype(F32) + scale * dot(spread_ref[rows, :], table)
+        out[rows, :] = base_ref[rows, :].astype(F32) + scale * dot(spread_ref[rows, :], table)
         return carry
 
     lax.fori_loop(0, out.shape[0] // tile, step, 0, unroll=4)
 
 
-def early(spread_rows, scale, skip, tables, tile):
-    return pl.pallas_call(
-        functools.partial(early_kernel, tile),
-        out_shape=jax.ShapeDtypeStruct(skip.shape, F32),
+def add_part(spread_rows, scale, base, tables, lengths, tile, name):
+    return pl.pallas_call(
+        functools.partial(part_kernel, tile, lengths),
+        out_shape=jax.ShapeDtypeStruct(base.shape, F32),
         in_specs=[pl.BlockSpec(memory_space=VMEM)] * (3 + len(tables)),
         out_specs=pl.BlockSpec(memory_space=VMEM),
         compiler_params=params(16),
         cost_estimate=cost(1, 1),
-        name="early",
-    )(spread_rows, scale, skip, *tables)
+        name=name,
+    )(spread_rows, scale, base, *tables)
 
 
 def late_kernel(tile, sum_ref, spread_ref, scale_ref, *refs):
@@ -577,11 +581,13 @@
     far = [xor_permute(v, "dom", s) for v, s in zip(pack(one, far), even)]
     two, three = xor_permute(two, "dom", 2), xor_permute(three, "dom", 3)
     sources = (up_index, up_weight, neighbors, w_head.T, area[None, :], targets, kernel_width[None, :])
-    first_rows, last_rows, scale, counts, head, weight, inv_width, target = spread(
-        own, live_counts, sources, steps, slots, 4, tile, padded, rows // members
+    split = dom_count - 2
+    first_rows, mid_rows, last_rows, scale, counts, head, weight, inv_width, target = spread(
+        own, live_counts, sources, steps, slots, 4, split, tile, padded, rows // members
     )
-    sums = early(first_rows, scale, fine_skip, [own, one, two, three], tile)
-    x, inner, outer = late(sums, last_rows, scale, far, tile)
+    sums = add_part(first_rows, scale, fine_skip, [own, one, two, three], [slots] * 4, tile, "early")
+    sums = add_part(mid_rows, scale, sums, far[:-1], [2 * slots] * (len(far) - 1), tile, "middle")
+    x, inner, outer = late(sums, last_rows, scale, far[-1:], tile)
     pairs = [(i, i + 1) for i in range(1, dom_count - 1, 2)]
     outer = lax.ppermute(outer, "dom", pairs + [(j, i) for i, j in pairs])
     inner = xor_permute(inner, "dom", 1)

time: 65.8 us -> 65.6 us (level)
  starting transfers between devices: 22.7 us -> 21.2 us
  Pallas kernels: 23.9 us -> 25.1 us
    pallas_call x1 -> x2, Pallas kernels: 2.73 us -> 4.32 us  [add_part(): pl.pallas_call(functools.partial(part_kernel, tile, lengths), out_shape=j...]
    ppermute x1, starting transfers between devices: 4.25 us -> 2.83 us  [shards(): outer = lax.ppermute(outer, 'dom', pairs + [(j, i) for i, j in pairs])]
  transfers between devices with their start and end apart: 16 -> 16, of which waited for: 10 -> 12; matrix products, arithmetic and copies ran while one was open for 0% -> 0% of each run, Pallas kernels for 26% -> 28%
where the time goes in v6:
time: 65.6 us; the launch traced here: 65.4 us
  Pallas kernels  25.1 us (38%)
  starting transfers between devices  21.2 us (32%)
  waiting for transfers between devices  17.6 us (27%)
  between operations  1.47 us (2%)
    ppermute x15, starting transfers between devices, xor_permute(): return lax.ppermute(value, axis, [(i, i ^ step) for i in range(count)])  18.4 us
    ppermute x15, waiting for transfers between devices, xor_permute(): return lax.ppermute(value, axis, [(i, i ^ step) for i in range(count)])  17.6 us
    pallas_call x1, Pallas kernels, spread(): pl.pallas_call(functools.partial(spread_kernel, tile, steps), out_shape=[...  7.23 us
    pallas_call x2, Pallas kernels, update_call(): pl.pallas_call(kernel, out_shape=out_shape, in_specs=[pl.BlockSpec(memory...  6.1 us
    pallas_call x2, Pallas kernels, add_part(): pl.pallas_call(functools.partial(part_kernel, tile, lengths), out_shape=j...  4.32 us
    ppermute x1, starting transfers between devices, shards(): outer = lax.ppermute(outer, 'dom', pairs + [(j, i) for i, j in pairs])  2.83 us
    pallas_call x1, Pallas kernels, latent_grad(): pl.pallas_call(latent_kernel, out_shape=jax.ShapeDtypeStruct((1, tiles *...  2.05 us
    pallas_call x1, Pallas kernels, first_pick(): pl.pallas_call(functools.partial(first_pick_kernel, steps), out_shape=[ja...  1.6 us
  transfers between devices with their start and end apart: 16, of which 12 were waited for; matrix products, arithmetic and copies ran while one was open for 0% of the time, Pallas kernels for 28%

profile of v6, /device:TPU:24, one launch (start us, length us, event | category | flops | bytes accessed | tf_op | source)
XLA Modules:
  0.0 65.4 jit_solution(421925084400506717)
XLA Ops:
  0.6 0.0 copy-start
  0.6 1.6 %pick_first.1 = (bf16[384,512]{1,0:T(8,128)(2,1)S(1)}, s32[1,8,128]{2,1,0:T(8,128)S(1)}, bf16[1,512,512]{2,1,0:T(8,128)(2,1)S(1)}) custom-call(s32[1,8,128]{2,1,0:T(8,128)} %send_ref.1, bf16[1,512,512]{2,1,0:T(8,128)(2,1)} %coarse_ref.1), custom_call_target="tpu_custom_call" | custom-call | flops 1 | bytes 1 | tf_op jit(solution)/shard_map/pick_first/pallas_call | solution.py:104
  2.2 0.1 collective-permute-start
  2.3 0.6 pick.1
  3.0 1.1 %collective-permute-done.refs_1_.other_ref = bf16[384,512]{1,0:T(8,128)(2,1)S(1)} collective-permute-done((bf16[384,512]{1,0:T(8,128)(2,1)S(1)}, bf16[384,512]{1,0:T(8,128)(2,1)S(1)}, u32[]{:S(2)}, u32[]{:S(2)}) %collective-permute-start) | collective-permute-done | bytes 393248 | tf_op jit(solution)/shard_map/ppermute | solution.py:60
  4.1 0.4 collective-permute-start.3
  4.5 2.5 %collective-permute-start.4 = (bf16[256,512]{1,0:T(8,128)(2,1)S(1)}, bf16[256,512]{1,0:T(8,128)(2,1)S(1)}, u32[]{:S(2)}, u32[]{:S(2)}) collective-permute-start(bf16[256,512]{1,0:T(8,128)(2,1)S(1)} %get-tuple-element.51), channel_id=1, source_target_pairs={{0,24},{4,28},{8,16},{12,20},{16,8},{20,12},{24,0},{28,4},{1,25},{... | collective-permute-start | bytes 786440 | tf_op jit(solution)/shard_map/ppermute | solution.py:60
  6.9 0.7 %collective-permute-start.1 = (bf16[128,512]{1,0:T(8,128)(2,1)S(1)}, bf16[128,512]{1,0:T(8,128)(2,1)S(1)}, u32[]{:S(2)}, u32[]{:S(2)}) collective-permute-start(bf16[128,512]{1,0:T(8,128)(2,1)S(1)} %get-tuple-element.45), channel_id=1, source_target_pairs={{0,8},{4,12},{8,0},{12,4},{16,24},{20,28},{24,16},{28,20},{1,9},{5... | collective-permute-start | bytes 393224 | tf_op jit(solution)/shard_map/ppermute | solution.py:60
  7.6 0.2 collective-permute-start.2
  8.5 7.2 %spread.1 = (bf16[2048,1024]{1,0:T(8,128)(2,1)S(1)}, bf16[2048,512]{1,0:T(8,128)(2,1)S(1)}, bf16[2048,256]{1,0:T(8,128)(2,1)S(1)}, f32[1,2048]{1,0:T(1,128)S(1)}...) custom-call(s32[1]{0:T(128)S(6)} %copy.16.live_ref, ...), custom_call_target="tpu_custom_call" | custom-call | flops 1 | bytes 1 | tf_op jit(solution)/shard_map/spread/pallas_call | solution.py:240
  15.8 3.9 %collective-permute-done.1.refs_2_ = bf16[128,512]{1,0:T(8,128)(2,1)S(1)} collective-permute-done((bf16[128,512]{1,0:T(8,128)(2,1)S(1)}, bf16[128,512]{1,0:T(8,128)(2,1)S(1)}, u32[]{:S(2)}, u32[]{:S(2)}) %collective-permute-start.1) | collective-permute-done | bytes 131104 | tf_op jit(solution)/shard_map/ppermute | solution.py:60
  19.7 2.0 %collective-permute-done.2.refs_3_ = bf16[128,512]{1,0:T(8,128)(2,1)S(1)} collective-permute-done((bf16[128,512]{1,0:T(8,128)(2,1)S(1)}, bf16[128,512]{1,0:T(8,128)(2,1)S(1)}, u32[]{:S(2)}, u32[]{:S(2)}) %collective-permute-start.2) | collective-permute-done | bytes 131104 | tf_op jit(solution)/shard_map/ppermute | solution.py:60
  21.7 2.7 %early.1.base_ref = f32[2048,512]{1,0:T(8,128)S(1)} custom-call(bf16[2048,1024]{1,0:T(8,128)(2,1)S(1)} %get-tuple-element.43.spread_ref, f32[1,2048]{1,0:T(1,128)S(1)} %get-tuple-element.42.scale_ref, bf16[2048,512]{1,0:T(8,128)(2,1)S(1)} %copy-done, bf16[128,512]{1,0:T(8,128)(2,1)S(1)} %get-tuple-element.39.refs_7_.refs_0_, ...), custom_call_target="tpu_custom_call" | custom-call | flops 1 | bytes 1 | tf_op jit(solution)/shard_map/early/pallas_call | solution.py:303
  24.4 0.3 collective-permute-done.3.refs_0_
  24.6 1.6 %middle.1.sum_ref = f32[2048,512]{1,0:T(8,128)S(1)} custom-call(bf16[2048,512]{1,0:T(8,128)(2,1)S(1)} %get-tuple-element.41.spread_ref, f32[1,2048]{1,0:T(1,128)S(1)} %get-tuple-element.42.scale_ref, f32[2048,512]{1,0:T(8,128)S(1)} %early.1.base_ref, bf16[256,512]{1,0:T(8,128)(2,1)S(1)} %collective-permute-done.3.refs_0_), custom_call_target="tpu_custom_call" | custom-call | flops 1 | bytes 1 | tf_op jit(solution)/shard_map/middle/pallas_call | solution.py:303
  26.3 0.0 collective-permute-done.4.refs_0_
  26.3 0.0 copy-start.1
  26.3 0.0 copy-start.2
  26.3 0.0 copy-start.3
  26.3 1.1 %late.1 = (bf16[2048,512]{1,0:T(8,128)(2,1)S(1)}, bf16[128,512]{1,0:T(8,128)(2,1)S(1)}, bf16[128,512]{1,0:T(8,128)(2,1)S(1)}) custom-call(f32[2048,512]{1,0:T(8,128)S(1)} %middle.1.sum_ref, bf16[2048,256]{1,0:T(8,128)(2,1)S(1)} %get-tuple-element.50.spread_ref, f32[1,2048]{1,0:T(1,128)S(1)} %get-tuple-element.42.scale_ref, ...), custom_call_target="tpu_custom_call" | custom-call | flops 536870912 | bytes 8388608 | tf_op jit(solution)/shard_map/late/pallas_call | solution.py:337
  27.4 3.8 %collective-permute-start.5 = (bf16[128,512]{1,0:T(8,128)(2,1)S(1)}, bf16[128,512]{1,0:T(8,128)(2,1)S(1)}, u32[]{:S(2)}, u32[]{:S(2)}) collective-permute-start(bf16[128,512]{1,0:T(8,128)(2,1)S(1)} %get-tuple-element.55), channel_id=1, source_target_pairs={{0,4},{4,0},{8,12},{12,8},{16,20},{20,16},{24,28},{28,24},{1,5},{5... | collective-permute-start | bytes 393224 | tf_op jit(solution)/shard_map/ppermute | solution.py:60
  31.3 2.8 %collective-permute-start.6 = (bf16[128,512]{1,0:T(8,128)(2,1)S(1)}, bf16[128,512]{1,0:T(8,128)(2,1)S(1)}, u32[]{:S(2)}, u32[]{:S(2)}) collective-permute-start(bf16[128,512]{1,0:T(8,128)(2,1)S(1)} %get-tuple-element.56), channel_id=1, source_target_pairs={{4,8},{12,16},{20,24},{8,4},{16,12},{24,20},{5,9},{13,17},{21,25},... | collective-permute-start | bytes 393224 | tf_op jit(solution)/shard_map/ppermute | solution.py:592
  34.1 4.3 %inner.1 = (bf16[1536,512]{1,0:T(8,128)(2,1)S(1)}, bf16[6,88,256]{2,1,0:T(8,128)(2,1)S(1)}) custom-call(bf16[2048,512]{1,0:T(8,128)(2,1)S(1)} %get-tuple-element.52.x_ref, bf16[8,256,512]{2,1,0:T(8,128)(2,1)S(1)} %get-tuple-element.53.count_ref, bf16[1024,512]{1,0:T(8,128)(2,1)S(1)} %copy-done.1, bf16[512,512]{1,0:T(8,128)(2,1)S(1)} %copy-done.2, ...), custom_call_target="tpu_custom_call" | custom-call | flops 4026531840 | bytes 8388608 | tf_op jit(solution)/shard_map/inner/pallas_call | solution.py:409
  38.4 0.0 collective-permute-done.5.inner_ref
  38.4 0.0 collective-permute-done.6.outer_ref
  38.5 1.8 %outer.1 = (bf16[512,512]{1,0:T(8,128)(2,1)S(1)}, bf16[88,512]{1,0:T(8,128)(2,1)S(1)}, bf16[88,512]{1,0:T(8,128)(2,1)S(1)}, bf16[88,512]{1,0:T(8,128)(2,1)S(1)}, bf16[88,512]{1,0:T(8,128)(2,1)S(1)}) custom-call(bf16[2048,512]{1,0:T(8,128)(2,1)S(1)} %get-tuple-element.52.x_ref, bf16[8,256,512]{2,1,0:T(8,128)(2,1)S(1)} %get-tuple-element.53.count_ref, ...), custom_call_target="tpu_custom_call" | custom-call | flops 1342177280 | bytes 8388608 | tf_op jit(solution)/shard_map/outer/pallas_call | solution.py:409
  40.3 2.5 %collective-permute-start.7 = (bf16[88,512]{1,0:T(8,128)(2,1)S(1)}, bf16[88,512]{1,0:T(8,128)(2,1)S(1)}, u32[]{:S(2)}, u32[]{:S(2)}) collective-permute-start(bf16[88,512]{1,0:T(8,128)(2,1)S(1)} %get-tuple-element.63), channel_id=1, source_target_pairs={{0,3},{1,2},{2,1},{3,0},{4,7},{5,6},{6,5},{7,4},{8,11},{9,10},{10,... | collective-permute-start | bytes 270344 | tf_op jit(solution)/shard_map/ppermute | solution.py:60
  42.8 0.5 collective-permute-start.8
  43.3 0.5 collective-permute-start.9
  43.8 2.4 %collective-permute-done.7.refs_1_ = bf16[88,512]{1,0:T(8,128)(2,1)S(1)} collective-permute-done((bf16[88,512]{1,0:T(8,128)(2,1)S(1)}, bf16[88,512]{1,0:T(8,128)(2,1)S(1)}, u32[]{:S(2)}, u32[]{:S(2)}) %collective-permute-start.7) | collective-permute-done | bytes 90144 | tf_op jit(solution)/shard_map/ppermute | solution.py:60
  46.2 1.1 %collective-permute-done.8.refs_2_ = bf16[88,512]{1,0:T(8,128)(2,1)S(1)} collective-permute-done((bf16[88,512]{1,0:T(8,128)(2,1)S(1)}, bf16[88,512]{1,0:T(8,128)(2,1)S(1)}, u32[]{:S(2)}, u32[]{:S(2)}) %collective-permute-start.8) | collective-permute-done | bytes 90144 | tf_op jit(solution)/shard_map/ppermute | solution.py:60
  47.3 0.5 collective-permute-done.9.refs_3_
  47.8 0.8 %score.1 = (bf16[88,512]{1,0:T(8,128)(2,1)S(1)}, bf16[88,512]{1,0:T(8,128)(2,1)S(1)}, bf16[88,512]{1,0:T(8,128)(2,1)S(1)}, bf16[88,512]{1,0:T(8,128)(2,1)S(1)}) custom-call(f32[1,512]{1,0:T(1,128)S(1)} %get-tuple-element.59.weight_ref, f32[88,1]{1,0:T(8,128)S(1)} %get-tuple-element.60.inv_ref, f32[88,512]{1,0:T(8,128)S(1)} %get-tuple-element.61.target_ref, ...), custom_call_target="tpu_custom_call" | custom-call | flops 7208960 | bytes 1048576 | tf_op jit(solution)/shard_map/score/pallas_call | solution.py:468
  48.6 1.6 %collective-permute-start.10 = (bf16[88,512]{1,0:T(8,128)(2,1)S(1)}, bf16[88,512]{1,0:T(8,128)(2,1)S(1)}, u32[]{:S(2)}, u32[]{:S(2)}) collective-permute-start(bf16[88,512]{1,0:T(8,128)(2,1)S(1)} %get-tuple-element.67), channel_id=1, source_target_pairs={{0,3},{1,2},{2,1},{3,0},{4,7},{5,6},{6,5},{7,4},{8,11},{9,10},{10,... | collective-permute-start | bytes 270344 | tf_op jit(solution)/shard_map/ppermute | solution.py:60
  50.1 0.5 collective-permute-start.11
  50.7 1.5 %collective-permute-start.12 = (bf16[88,512]{1,0:T(8,128)(2,1)S(1)}, bf16[88,512]{1,0:T(8,128)(2,1)S(1)}, u32[]{:S(2)}, u32[]{:S(2)}) collective-permute-start(bf16[88,512]{1,0:T(8,128)(2,1)S(1)} %get-tuple-element.69), channel_id=1, source_target_pairs={{0,1},{1,0},{2,3},{3,2},{4,5},{5,4},{6,7},{7,6},{8,9},{9,8},{10,11... | collective-permute-start | bytes 270344 | tf_op jit(solution)/shard_map/ppermute | solution.py:60
  52.1 2.0 %collective-permute-done.10.refs_1_ = bf16[88,512]{1,0:T(8,128)(2,1)S(1)} collective-permute-done((bf16[88,512]{1,0:T(8,128)(2,1)S(1)}, bf16[88,512]{1,0:T(8,128)(2,1)S(1)}, u32[]{:S(2)}, u32[]{:S(2)}) %collective-permute-start.10) | collective-permute-done | bytes 90144 | tf_op jit(solution)/shard_map/ppermute | solution.py:60
  54.1 0.9 %collective-permute-done.11.refs_2_ = bf16[88,512]{1,0:T(8,128)(2,1)S(1)} collective-permute-done((bf16[88,512]{1,0:T(8,128)(2,1)S(1)}, bf16[88,512]{1,0:T(8,128)(2,1)S(1)}, u32[]{:S(2)}, u32[]{:S(2)}) %collective-permute-start.11) | collective-permute-done | bytes 90144 | tf_op jit(solution)/shard_map/ppermute | solution.py:60
  55.0 1.5 %collective-permute-done.12.refs_3_ = bf16[88,512]{1,0:T(8,128)(2,1)S(1)} collective-permute-done((bf16[88,512]{1,0:T(8,128)(2,1)S(1)}, bf16[88,512]{1,0:T(8,128)(2,1)S(1)}, u32[]{:S(2)}, u32[]{:S(2)}) %collective-permute-start.12) | collective-permute-done | bytes 90144 | tf_op jit(solution)/shard_map/ppermute | solution.py:60
  56.6 0.5 head_terms.1
  57.0 2.2 %collective-permute-start.13 = (bf16[88,512]{1,0:T(8,128)(2,1)S(1)}, bf16[88,512]{1,0:T(8,128)(2,1)S(1)}, u32[]{:S(2)}, u32[]{:S(2)}) collective-permute-start(bf16[88,512]{1,0:T(8,128)(2,1)S(1)} %get-tuple-element.71.refs_0_), channel_id=1, source_target_pairs={{0,3},{1,2},{2,1},{3,0},{4,7},{5,6},{6,5},{7,4},{8,11},{9,10},{10,... | collective-permute-start | bytes 270344 | tf_op jit(solution)/shard_map/ppermute | solution.py:60
  59.3 0.8 %collective-permute-start.14 = (bf16[88,512]{1,0:T(8,128)(2,1)S(1)}, bf16[88,512]{1,0:T(8,128)(2,1)S(1)}, u32[]{:S(2)}, u32[]{:S(2)}) collective-permute-start(bf16[88,512]{1,0:T(8,128)(2,1)S(1)} %get-tuple-element.71.refs_0_), channel_id=1, source_target_pairs={{0,2},{1,3},{2,0},{3,1},{4,6},{5,7},{6,4},{7,5},{8,10},{9,11},{10,... | collective-permute-start | bytes 270344 | tf_op jit(solution)/shard_map/ppermute | solution.py:60
  60.1 0.5 collective-permute-start.15
  60.6 2.1 %latent_grad.1 = bf16[1,2048,512]{2,1,0:T(8,128)(2,1)} custom-call(bf16[88,512]{1,0:T(8,128)(2,1)S(1)} %get-tuple-element.40.head_ref, bf16[8,88,256]{2,1,0:T(8,128)(2,1)S(1)} %get-tuple-element.70.score_ref), custom_call_target="tpu_custom_call" | custom-call | flops 184549376 | bytes 3145728 | tf_op jit(solution)/shard_map/latent_grad/pallas_call | solution.py:521
  62.6 0.0 collective-permute-done.13.refs_1_
  62.7 1.1 %collective-permute-done.14.refs_2_ = bf16[88,512]{1,0:T(8,128)(2,1)S(1)} collective-permute-done((bf16[88,512]{1,0:T(8,128)(2,1)S(1)}, bf16[88,512]{1,0:T(8,128)(2,1)S(1)}, u32[]{:S(2)}, u32[]{:S(2)}) %collective-permute-start.14) | collective-permute-done | bytes 90144 | tf_op jit(solution)/shard_map/ppermute | solution.py:60
  63.8 0.8 %collective-permute-done.15.refs_3_ = bf16[88,512]{1,0:T(8,128)(2,1)S(1)} collective-permute-done((bf16[88,512]{1,0:T(8,128)(2,1)S(1)}, bf16[88,512]{1,0:T(8,128)(2,1)S(1)}, u32[]{:S(2)}, u32[]{:S(2)}) %collective-permute-start.15) | collective-permute-done | bytes 90144 | tf_op jit(solution)/shard_map/ppermute | solution.py:60
  64.6 0.8 %head_total.1 = f32[83,1,512]{2,1,0:T(1,128)} custom-call(bf16[88,512]{1,0:T(8,128)(2,1)S(1)} %get-tuple-element.71.refs_0_, bf16[88,512]{1,0:T(8,128)(2,1)S(1)} %collective-permute-done.13.refs_1_, bf16[88,512]{1,0:T(8,128)(2,1)S(1)} %collective-permute-done.14.refs_2_, bf16[88,512]{1,0:T(8,128)(2,1)S(1)} %collective-permute-done.15.refs_3_), custom_call_target="tpu_custom_call" | custom-call | flops 180224 | bytes 1048576 | tf_op jit(solution)/shard_map/head_total/pallas_call | solution.py:541
  (5 shorter events, 0.0 us)
Async XLA Ops:
  0.6 21.0 %copy-start = (bf16[2048,512]{1,0:T(8,128)(2,1)S(1)}, bf16[2048,512]{1,0:T(8,128)(2,1)}, u32[]{:S(2)}) copy-start(bf16[2048,512]{1,0:T(8,128)(2,1)} %base_ref.1) | copy-start | bytes 6291460
  2.2 1.8 %collective-permute-start = (bf16[384,512]{1,0:T(8,128)(2,1)S(1)}, bf16[384,512]{1,0:T(8,128)(2,1)S(1)}, u32[]{:S(2)}, u32[]{:S(2)}) collective-permute-start(bf16[384,512]{1,0:T(8,128)(2,1)S(1)} %get-tuple-element.44), channel_id=1, source_target_pairs={{0,4},{4,0},{8,12},{12,8},{16,20},{20,16},{24,28},{28,24},{1,5},{5... | collective-permute-start | bytes 1179656 | tf_op jit(solution)/shard_map/ppermute | solution.py:60
  4.1 20.6 %collective-permute-start.3 = (bf16[256,512]{1,0:T(8,128)(2,1)S(1)}, bf16[256,512]{1,0:T(8,128)(2,1)S(1)}, u32[]{:S(2)}, u32[]{:S(2)}) collective-permute-start(bf16[256,512]{1,0:T(8,128)(2,1)S(1)} %get-tuple-element.49), channel_id=1, source_target_pairs={{0,16},{4,20},{8,24},{12,28},{16,0},{20,4},{24,8},{28,12},{1,17},{... | collective-permute-start | bytes 786440 | tf_op jit(solution)/shard_map/ppermute | solution.py:60
  4.5 21.8 %collective-permute-start.4 = (bf16[256,512]{1,0:T(8,128)(2,1)S(1)}, bf16[256,512]{1,0:T(8,128)(2,1)S(1)}, u32[]{:S(2)}, u32[]{:S(2)}) collective-permute-start(bf16[256,512]{1,0:T(8,128)(2,1)S(1)} %get-tuple-element.51), channel_id=1, source_target_pairs={{0,24},{4,28},{8,16},{12,20},{16,8},{20,12},{24,0},{28,4},{1,25},{... | collective-permute-start | bytes 786440 | tf_op jit(solution)/shard_map/ppermute | solution.py:60
  6.9 12.7 %collective-permute-start.1 = (bf16[128,512]{1,0:T(8,128)(2,1)S(1)}, bf16[128,512]{1,0:T(8,128)(2,1)S(1)}, u32[]{:S(2)}, u32[]{:S(2)}) collective-permute-start(bf16[128,512]{1,0:T(8,128)(2,1)S(1)} %get-tuple-element.45), channel_id=1, source_target_pairs={{0,8},{4,12},{8,0},{12,4},{16,24},{20,28},{24,16},{28,20},{1,9},{5... | collective-permute-start | bytes 393224 | tf_op jit(solution)/shard_map/ppermute | solution.py:60
  7.6 14.0 %collective-permute-start.2 = (bf16[128,512]{1,0:T(8,128)(2,1)S(1)}, bf16[128,512]{1,0:T(8,128)(2,1)S(1)}, u32[]{:S(2)}, u32[]{:S(2)}) collective-permute-start(bf16[128,512]{1,0:T(8,128)(2,1)S(1)} %get-tuple-element.46), channel_id=1, source_target_pairs={{0,12},{4,8},{8,4},{12,0},{16,28},{20,24},{24,20},{28,16},{1,13},{... | collective-permute-start | bytes 393224 | tf_op jit(solution)/shard_map/ppermute | solution.py:60
  26.3 7.8 %copy-start.1 = (bf16[1024,512]{1,0:T(8,128)(2,1)S(1)}, bf16[1024,512]{1,0:T(8,128)(2,1)}, u32[]{:S(2)}) copy-start(bf16[1024,512]{1,0:T(8,128)(2,1)} %w_in_ref.3) | copy-start | bytes 3145732
  26.3 7.8 %copy-start.2 = (bf16[512,512]{1,0:T(8,128)(2,1)S(1)}, bf16[512,512]{1,0:T(8,128)(2,1)}, u32[]{:S(2)}) copy-start(bf16[512,512]{1,0:T(8,128)(2,1)} %w_out_ref.3) | copy-start | bytes 1572868
  26.3 7.8 %copy-start.3 = (f32[512]{0:T(512)S(1)}, f32[512]{0:T(512)}, u32[]{:S(2)}) copy-start(f32[512]{0:T(512)} %param.26) | copy-start | bytes 6148
  27.4 11.0 %collective-permute-start.5 = (bf16[128,512]{1,0:T(8,128)(2,1)S(1)}, bf16[128,512]{1,0:T(8,128)(2,1)S(1)}, u32[]{:S(2)}, u32[]{:S(2)}) collective-permute-start(bf16[128,512]{1,0:T(8,128)(2,1)S(1)} %get-tuple-element.55), channel_id=1, source_target_pairs={{0,4},{4,0},{8,12},{12,8},{16,20},{20,16},{24,28},{28,24},{1,5},{5... | collective-permute-start | bytes 393224 | tf_op jit(solution)/shard_map/ppermute | solution.py:60
  31.3 7.2 %collective-permute-start.6 = (bf16[128,512]{1,0:T(8,128)(2,1)S(1)}, bf16[128,512]{1,0:T(8,128)(2,1)S(1)}, u32[]{:S(2)}, u32[]{:S(2)}) collective-permute-start(bf16[128,512]{1,0:T(8,128)(2,1)S(1)} %get-tuple-element.56), channel_id=1, source_target_pairs={{4,8},{12,16},{20,24},{8,4},{16,12},{24,20},{5,9},{13,17},{21,25},... | collective-permute-start | bytes 393224 | tf_op jit(solution)/shard_map/ppermute | solution.py:592
  40.3 6.0 %collective-permute-start.7 = (bf16[88,512]{1,0:T(8,128)(2,1)S(1)}, bf16[88,512]{1,0:T(8,128)(2,1)S(1)}, u32[]{:S(2)}, u32[]{:S(2)}) collective-permute-start(bf16[88,512]{1,0:T(8,128)(2,1)S(1)} %get-tuple-element.63), channel_id=1, source_target_pairs={{0,3},{1,2},{2,1},{3,0},{4,7},{5,6},{6,5},{7,4},{8,11},{9,10},{10,... | collective-permute-start | bytes 270344 | tf_op jit(solution)/shard_map/ppermute | solution.py:60
  42.8 4.5 %collective-permute-start.8 = (bf16[88,512]{1,0:T(8,128)(2,1)S(1)}, bf16[88,512]{1,0:T(8,128)(2,1)S(1)}, u32[]{:S(2)}, u32[]{:S(2)}) collective-permute-start(bf16[88,512]{1,0:T(8,128)(2,1)S(1)} %get-tuple-element.64), channel_id=1, source_target_pairs={{0,2},{1,3},{2,0},{3,1},{4,6},{5,7},{6,4},{7,5},{8,10},{9,11},{10,... | collective-permute-start | bytes 270344 | tf_op jit(solution)/shard_map/ppermute | solution.py:60
  43.3 4.5 %collective-permute-start.9 = (bf16[88,512]{1,0:T(8,128)(2,1)S(1)}, bf16[88,512]{1,0:T(8,128)(2,1)S(1)}, u32[]{:S(2)}, u32[]{:S(2)}) collective-permute-start(bf16[88,512]{1,0:T(8,128)(2,1)S(1)} %get-tuple-element.65), channel_id=1, source_target_pairs={{0,1},{1,0},{2,3},{3,2},{4,5},{5,4},{6,7},{7,6},{8,9},{9,8},{10,11... | collective-permute-start | bytes 270344 | tf_op jit(solution)/shard_map/ppermute | solution.py:60
  48.6 5.5 %collective-permute-start.10 = (bf16[88,512]{1,0:T(8,128)(2,1)S(1)}, bf16[88,512]{1,0:T(8,128)(2,1)S(1)}, u32[]{:S(2)}, u32[]{:S(2)}) collective-permute-start(bf16[88,512]{1,0:T(8,128)(2,1)S(1)} %get-tuple-element.67), channel_id=1, source_target_pairs={{0,3},{1,2},{2,1},{3,0},{4,7},{5,6},{6,5},{7,4},{8,11},{9,10},{10,... | collective-permute-start | bytes 270344 | tf_op jit(solution)/shard_map/ppermute | solution.py:60
  50.1 4.9 %collective-permute-start.11 = (bf16[88,512]{1,0:T(8,128)(2,1)S(1)}, bf16[88,512]{1,0:T(8,128)(2,1)S(1)}, u32[]{:S(2)}, u32[]{:S(2)}) collective-permute-start(bf16[88,512]{1,0:T(8,128)(2,1)S(1)} %get-tuple-element.68), channel_id=1, source_target_pairs={{0,2},{1,3},{2,0},{3,1},{4,6},{5,7},{6,4},{7,5},{8,10},{9,11},{10,... | collective-permute-start | bytes 270344 | tf_op jit(solution)/shard_map/ppermute | solution.py:60
  50.7 5.9 %collective-permute-start.12 = (bf16[88,512]{1,0:T(8,128)(2,1)S(1)}, bf16[88,512]{1,0:T(8,128)(2,1)S(1)}, u32[]{:S(2)}, u32[]{:S(2)}) collective-permute-start(bf16[88,512]{1,0:T(8,128)(2,1)S(1)} %get-tuple-element.69), channel_id=1, source_target_pairs={{0,1},{1,0},{2,3},{3,2},{4,5},{5,4},{6,7},{7,6},{8,9},{9,8},{10,11... | collective-permute-start | bytes 270344 | tf_op jit(solution)/shard_map/ppermute | solution.py:60
  57.0 5.6 %collective-permute-start.13 = (bf16[88,512]{1,0:T(8,128)(2,1)S(1)}, bf16[88,512]{1,0:T(8,128)(2,1)S(1)}, u32[]{:S(2)}, u32[]{:S(2)}) collective-permute-start(bf16[88,512]{1,0:T(8,128)(2,1)S(1)} %get-tuple-element.71.refs_0_), channel_id=1, source_target_pairs={{0,3},{1,2},{2,1},{3,0},{4,7},{5,6},{6,5},{7,4},{8,11},{9,10},{10,... | collective-permute-start | bytes 270344 | tf_op jit(solution)/shard_map/ppermute | solution.py:60
  59.3 4.5 %collective-permute-start.14 = (bf16[88,512]{1,0:T(8,128)(2,1)S(1)}, bf16[88,512]{1,0:T(8,128)(2,1)S(1)}, u32[]{:S(2)}, u32[]{:S(2)}) collective-permute-start(bf16[88,512]{1,0:T(8,128)(2,1)S(1)} %get-tuple-element.71.refs_0_), channel_id=1, source_target_pairs={{0,2},{1,3},{2,0},{3,1},{4,6},{5,7},{6,4},{7,5},{8,10},{9,11},{10,... | collective-permute-start | bytes 270344 | tf_op jit(solution)/shard_map/ppermute | solution.py:60
  60.1 4.5 %collective-permute-start.15 = (bf16[88,512]{1,0:T(8,128)(2,1)S(1)}, bf16[88,512]{1,0:T(8,128)(2,1)S(1)}, u32[]{:S(2)}, u32[]{:S(2)}) collective-permute-start(bf16[88,512]{1,0:T(8,128)(2,1)S(1)} %get-tuple-element.71.refs_0_), channel_id=1, source_target_pairs={{0,1},{1,0},{2,3},{3,2},{4,5},{5,4},{6,7},{7,6},{8,9},{9,8},{10,11... | collective-permute-start | bytes 270344 | tf_op jit(solution)/shard_map/ppermute | solution.py:60

commit v7 on v6

--- a/solution.py
+++ b/solution.py
@@ -448,18 +448,20 @@
 
 def score_kernel(members, weight_ref, inv_ref, target_ref, *refs):
     preds, outs = refs[:members], refs[members:]
-    inv_width, weight = inv_ref[...], weight_ref[...]
-    weight = weight * -inv_width
-    values = [r[...].astype(F32) for r in preds]
-    sums = [jnp.zeros(v.shape, F32) for v in values]
-    for i in range(members):
-        for j in range(i + 1, members):
-            phi = slope(values[i] - values[j], inv_width)
-            sums[i] = sums[i] + phi
-            sums[j] = sums[j] - phi
-    for i in range(members):
-        total = sums[i] * (1.0 / members) - slope(values[i] - target_ref[...], inv_width)
-        outs[i][...] = (weight * total).astype(BF16)
+    inv_width = inv_ref[...]
+    for start in range(0, target_ref.shape[1], 128):
+        lanes = slice(start, start + 128)
+        weight = weight_ref[:, lanes] * -inv_width
+        values = [r[:, lanes].astype(F32) for r in preds]
+        sums = [jnp.zeros(v.shape, F32) for v in values]
+        for i in range(members):
+            for j in range(i + 1, members):
+                phi = slope(values[i] - values[j], inv_width)
+                sums[i] = sums[i] + phi
+                sums[j] = sums[j] - phi
+        for i in range(members):
+            total = sums[i] * (1.0 / members) - slope(values[i] - target_ref[:, lanes], inv_width)
+            outs[i][:, lanes] = (weight * total).astype(BF16)
 
 
 def score(weight, inv_width, target, preds):

time: 65.6 us -> 65.4 us (level)
  no operation moved by 1% of the time
where the time goes in v7:
time: 65.4 us; the launch traced here: 65.3 us
  Pallas kernels  25 us (38%)
  starting transfers between devices  21 us (32%)
  waiting for transfers between devices  17.7 us (27%)
  between operations  1.47 us (2%)
    ppermute x15, starting transfers between devices, xor_permute(): return lax.ppermute(value, axis, [(i, i ^ step) for i in range(count)])  18.4 us
    ppermute x15, waiting for transfers between devices, xor_permute(): return lax.ppermute(value, axis, [(i, i ^ step) for i in range(count)])  17.7 us
    pallas_call x1, Pallas kernels, spread(): pl.pallas_call(functools.partial(spread_kernel, tile, steps), out_shape=[...  7.23 us
    pallas_call x2, Pallas kernels, update_call(): pl.pallas_call(kernel, out_shape=out_shape, in_specs=[pl.BlockSpec(memory...  6.1 us
    pallas_call x2, Pallas kernels, add_part(): pl.pallas_call(functools.partial(part_kernel, tile, lengths), out_shape=j...  4.32 us
    ppermute x1, starting transfers between devices, shards(): outer = lax.ppermute(outer, 'dom', pairs + [(j, i) for i, j in pairs])  2.65 us
    pallas_call x1, Pallas kernels, latent_grad(): pl.pallas_call(latent_kernel, out_shape=jax.ShapeDtypeStruct((1, tiles *...  2.05 us
    pallas_call x1, Pallas kernels, first_pick(): pl.pallas_call(functools.partial(first_pick_kernel, steps), out_shape=[ja...  1.6 us
  transfers between devices with their start and end apart: 16, of which 12 were waited for; matrix products, arithmetic and copies ran while one was open for 0% of the time, Pallas kernels for 28%

profile of v7, /device:TPU:24, one launch (start us, length us, event | category | flops | bytes accessed | tf_op | source)
XLA Modules:
  0.0 65.3 jit_solution(16249206272087764542)
XLA Ops:
  0.6 0.0 copy-start
  0.6 1.6 %pick_first.1 = (bf16[384,512]{1,0:T(8,128)(2,1)S(1)}, s32[1,8,128]{2,1,0:T(8,128)S(1)}, bf16[1,512,512]{2,1,0:T(8,128)(2,1)S(1)}) custom-call(s32[1,8,128]{2,1,0:T(8,128)} %send_ref.1, bf16[1,512,512]{2,1,0:T(8,128)(2,1)} %coarse_ref.1), custom_call_target="tpu_custom_call" | custom-call | flops 1 | bytes 1 | tf_op jit(solution)/shard_map/pick_first/pallas_call | solution.py:104
  2.2 0.1 collective-permute-start
  2.3 0.6 pick.1
  3.0 1.1 %collective-permute-done.refs_1_.other_ref = bf16[384,512]{1,0:T(8,128)(2,1)S(1)} collective-permute-done((bf16[384,512]{1,0:T(8,128)(2,1)S(1)}, bf16[384,512]{1,0:T(8,128)(2,1)S(1)}, u32[]{:S(2)}, u32[]{:S(2)}) %collective-permute-start) | collective-permute-done | bytes 393248 | tf_op jit(solution)/shard_map/ppermute | solution.py:60
  4.1 0.4 collective-permute-start.3
  4.5 2.5 %collective-permute-start.4 = (bf16[256,512]{1,0:T(8,128)(2,1)S(1)}, bf16[256,512]{1,0:T(8,128)(2,1)S(1)}, u32[]{:S(2)}, u32[]{:S(2)}) collective-permute-start(bf16[256,512]{1,0:T(8,128)(2,1)S(1)} %get-tuple-element.51), channel_id=1, source_target_pairs={{0,24},{4,28},{8,16},{12,20},{16,8},{20,12},{24,0},{28,4},{1,25},{... | collective-permute-start | bytes 786440 | tf_op jit(solution)/shard_map/ppermute | solution.py:60
  6.9 0.7 %collective-permute-start.1 = (bf16[128,512]{1,0:T(8,128)(2,1)S(1)}, bf16[128,512]{1,0:T(8,128)(2,1)S(1)}, u32[]{:S(2)}, u32[]{:S(2)}) collective-permute-start(bf16[128,512]{1,0:T(8,128)(2,1)S(1)} %get-tuple-element.45), channel_id=1, source_target_pairs={{0,8},{4,12},{8,0},{12,4},{16,24},{20,28},{24,16},{28,20},{1,9},{5... | collective-permute-start | bytes 393224 | tf_op jit(solution)/shard_map/ppermute | solution.py:60
  7.6 0.2 collective-permute-start.2
  8.5 7.2 %spread.1 = (bf16[2048,1024]{1,0:T(8,128)(2,1)S(1)}, bf16[2048,512]{1,0:T(8,128)(2,1)S(1)}, bf16[2048,256]{1,0:T(8,128)(2,1)S(1)}, f32[1,2048]{1,0:T(1,128)S(1)}...) custom-call(s32[1]{0:T(128)S(6)} %copy.16.live_ref, ...), custom_call_target="tpu_custom_call" | custom-call | flops 1 | bytes 1 | tf_op jit(solution)/shard_map/spread/pallas_call | solution.py:240
  15.8 3.9 %collective-permute-done.1.refs_2_ = bf16[128,512]{1,0:T(8,128)(2,1)S(1)} collective-permute-done((bf16[128,512]{1,0:T(8,128)(2,1)S(1)}, bf16[128,512]{1,0:T(8,128)(2,1)S(1)}, u32[]{:S(2)}, u32[]{:S(2)}) %collective-permute-start.1) | collective-permute-done | bytes 131104 | tf_op jit(solution)/shard_map/ppermute | solution.py:60
  19.7 2.0 %collective-permute-done.2.refs_3_ = bf16[128,512]{1,0:T(8,128)(2,1)S(1)} collective-permute-done((bf16[128,512]{1,0:T(8,128)(2,1)S(1)}, bf16[128,512]{1,0:T(8,128)(2,1)S(1)}, u32[]{:S(2)}, u32[]{:S(2)}) %collective-permute-start.2) | collective-permute-done | bytes 131104 | tf_op jit(solution)/shard_map/ppermute | solution.py:60
  21.7 2.7 %early.1.base_ref = f32[2048,512]{1,0:T(8,128)S(1)} custom-call(bf16[2048,1024]{1,0:T(8,128)(2,1)S(1)} %get-tuple-element.43.spread_ref, f32[1,2048]{1,0:T(1,128)S(1)} %get-tuple-element.42.scale_ref, bf16[2048,512]{1,0:T(8,128)(2,1)S(1)} %copy-done, bf16[128,512]{1,0:T(8,128)(2,1)S(1)} %get-tuple-element.39.refs_7_.refs_0_, ...), custom_call_target="tpu_custom_call" | custom-call | flops 1 | bytes 1 | tf_op jit(solution)/shard_map/early/pallas_call | solution.py:303
  24.4 0.3 collective-permute-done.3.refs_0_
  24.6 1.6 %middle.1.sum_ref = f32[2048,512]{1,0:T(8,128)S(1)} custom-call(bf16[2048,512]{1,0:T(8,128)(2,1)S(1)} %get-tuple-element.41.spread_ref, f32[1,2048]{1,0:T(1,128)S(1)} %get-tuple-element.42.scale_ref, f32[2048,512]{1,0:T(8,128)S(1)} %early.1.base_ref, bf16[256,512]{1,0:T(8,128)(2,1)S(1)} %collective-permute-done.3.refs_0_), custom_call_target="tpu_custom_call" | custom-call | flops 1 | bytes 1 | tf_op jit(solution)/shard_map/middle/pallas_call | solution.py:303
  26.3 0.0 collective-permute-done.4.refs_0_
  26.3 0.0 copy-start.1
  26.3 0.0 copy-start.2
  26.3 0.0 copy-start.3
  26.3 1.1 %late.1 = (bf16[2048,512]{1,0:T(8,128)(2,1)S(1)}, bf16[128,512]{1,0:T(8,128)(2,1)S(1)}, bf16[128,512]{1,0:T(8,128)(2,1)S(1)}) custom-call(f32[2048,512]{1,0:T(8,128)S(1)} %middle.1.sum_ref, bf16[2048,256]{1,0:T(8,128)(2,1)S(1)} %get-tuple-element.50.spread_ref, f32[1,2048]{1,0:T(1,128)S(1)} %get-tuple-element.42.scale_ref, ...), custom_call_target="tpu_custom_call" | custom-call | flops 536870912 | bytes 8388608 | tf_op jit(solution)/shard_map/late/pallas_call | solution.py:337
  27.4 3.8 %collective-permute-start.5 = (bf16[128,512]{1,0:T(8,128)(2,1)S(1)}, bf16[128,512]{1,0:T(8,128)(2,1)S(1)}, u32[]{:S(2)}, u32[]{:S(2)}) collective-permute-start(bf16[128,512]{1,0:T(8,128)(2,1)S(1)} %get-tuple-element.55), channel_id=1, source_target_pairs={{0,4},{4,0},{8,12},{12,8},{16,20},{20,16},{24,28},{28,24},{1,5},{5... | collective-permute-start | bytes 393224 | tf_op jit(solution)/shard_map/ppermute | solution.py:60
  31.3 2.7 %collective-permute-start.6 = (bf16[128,512]{1,0:T(8,128)(2,1)S(1)}, bf16[128,512]{1,0:T(8,128)(2,1)S(1)}, u32[]{:S(2)}, u32[]{:S(2)}) collective-permute-start(bf16[128,512]{1,0:T(8,128)(2,1)S(1)} %get-tuple-element.56), channel_id=1, source_target_pairs={{4,8},{12,16},{20,24},{8,4},{16,12},{24,20},{5,9},{13,17},{21,25},... | collective-permute-start | bytes 393224 | tf_op jit(solution)/shard_map/ppermute | solution.py:594
  34.0 4.3 %inner.1 = (bf16[1536,512]{1,0:T(8,128)(2,1)S(1)}, bf16[6,88,256]{2,1,0:T(8,128)(2,1)S(1)}) custom-call(bf16[2048,512]{1,0:T(8,128)(2,1)S(1)} %get-tuple-element.52.x_ref, bf16[8,256,512]{2,1,0:T(8,128)(2,1)S(1)} %get-tuple-element.53.count_ref, bf16[1024,512]{1,0:T(8,128)(2,1)S(1)} %copy-done.1, bf16[512,512]{1,0:T(8,128)(2,1)S(1)} %copy-done.2, ...), custom_call_target="tpu_custom_call" | custom-call | flops 4026531840 | bytes 8388608 | tf_op jit(solution)/shard_map/inner/pallas_call | solution.py:409
  38.3 0.0 collective-permute-done.5.inner_ref
  38.3 0.0 collective-permute-done.6.outer_ref
  38.3 1.8 %outer.1 = (bf16[512,512]{1,0:T(8,128)(2,1)S(1)}, bf16[88,512]{1,0:T(8,128)(2,1)S(1)}, bf16[88,512]{1,0:T(8,128)(2,1)S(1)}, bf16[88,512]{1,0:T(8,128)(2,1)S(1)}, bf16[88,512]{1,0:T(8,128)(2,1)S(1)}) custom-call(bf16[2048,512]{1,0:T(8,128)(2,1)S(1)} %get-tuple-element.52.x_ref, bf16[8,256,512]{2,1,0:T(8,128)(2,1)S(1)} %get-tuple-element.53.count_ref, ...), custom_call_target="tpu_custom_call" | custom-call | flops 1342177280 | bytes 8388608 | tf_op jit(solution)/shard_map/outer/pallas_call | solution.py:409
  40.1 2.5 %collective-permute-start.7 = (bf16[88,512]{1,0:T(8,128)(2,1)S(1)}, bf16[88,512]{1,0:T(8,128)(2,1)S(1)}, u32[]{:S(2)}, u32[]{:S(2)}) collective-permute-start(bf16[88,512]{1,0:T(8,128)(2,1)S(1)} %get-tuple-element.63), channel_id=1, source_target_pairs={{0,3},{1,2},{2,1},{3,0},{4,7},{5,6},{6,5},{7,4},{8,11},{9,10},{10,... | collective-permute-start | bytes 270344 | tf_op jit(solution)/shard_map/ppermute | solution.py:60
  42.6 0.5 collective-permute-start.8
  43.1 0.6 collective-permute-start.9
  43.7 2.4 %collective-permute-done.7.refs_1_ = bf16[88,512]{1,0:T(8,128)(2,1)S(1)} collective-permute-done((bf16[88,512]{1,0:T(8,128)(2,1)S(1)}, bf16[88,512]{1,0:T(8,128)(2,1)S(1)}, u32[]{:S(2)}, u32[]{:S(2)}) %collective-permute-start.7) | collective-permute-done | bytes 90144 | tf_op jit(solution)/shard_map/ppermute | solution.py:60
  46.1 1.1 %collective-permute-done.8.refs_2_ = bf16[88,512]{1,0:T(8,128)(2,1)S(1)} collective-permute-done((bf16[88,512]{1,0:T(8,128)(2,1)S(1)}, bf16[88,512]{1,0:T(8,128)(2,1)S(1)}, u32[]{:S(2)}, u32[]{:S(2)}) %collective-permute-start.8) | collective-permute-done | bytes 90144 | tf_op jit(solution)/shard_map/ppermute | solution.py:60
  47.1 0.5 collective-permute-done.9.refs_3_
  47.6 0.7 %score.1 = (bf16[88,512]{1,0:T(8,128)(2,1)S(1)}, bf16[88,512]{1,0:T(8,128)(2,1)S(1)}, bf16[88,512]{1,0:T(8,128)(2,1)S(1)}, bf16[88,512]{1,0:T(8,128)(2,1)S(1)}) custom-call(f32[1,512]{1,0:T(1,128)S(1)} %get-tuple-element.59.weight_ref, f32[88,1]{1,0:T(8,128)S(1)} %get-tuple-element.60.inv_ref, f32[88,512]{1,0:T(8,128)S(1)} %get-tuple-element.61.target_ref, ...), custom_call_target="tpu_custom_call" | custom-call | flops 7208960 | bytes 1048576 | tf_op jit(solution)/shard_map/score/pallas_call | solution.py:470
  48.3 1.6 %collective-permute-start.10 = (bf16[88,512]{1,0:T(8,128)(2,1)S(1)}, bf16[88,512]{1,0:T(8,128)(2,1)S(1)}, u32[]{:S(2)}, u32[]{:S(2)}) collective-permute-start(bf16[88,512]{1,0:T(8,128)(2,1)S(1)} %get-tuple-element.67), channel_id=1, source_target_pairs={{0,3},{1,2},{2,1},{3,0},{4,7},{5,6},{6,5},{7,4},{8,11},{9,10},{10,... | collective-permute-start | bytes 270344 | tf_op jit(solution)/shard_map/ppermute | solution.py:60
  49.9 0.6 collective-permute-start.11
  50.5 1.4 %collective-permute-start.12 = (bf16[88,512]{1,0:T(8,128)(2,1)S(1)}, bf16[88,512]{1,0:T(8,128)(2,1)S(1)}, u32[]{:S(2)}, u32[]{:S(2)}) collective-permute-start(bf16[88,512]{1,0:T(8,128)(2,1)S(1)} %get-tuple-element.69), channel_id=1, source_target_pairs={{0,1},{1,0},{2,3},{3,2},{4,5},{5,4},{6,7},{7,6},{8,9},{9,8},{10,11... | collective-permute-start | bytes 270344 | tf_op jit(solution)/shard_map/ppermute | solution.py:60
  51.9 2.0 %collective-permute-done.10.refs_1_ = bf16[88,512]{1,0:T(8,128)(2,1)S(1)} collective-permute-done((bf16[88,512]{1,0:T(8,128)(2,1)S(1)}, bf16[88,512]{1,0:T(8,128)(2,1)S(1)}, u32[]{:S(2)}, u32[]{:S(2)}) %collective-permute-start.10) | collective-permute-done | bytes 90144 | tf_op jit(solution)/shard_map/ppermute | solution.py:60
  53.8 0.9 %collective-permute-done.11.refs_2_ = bf16[88,512]{1,0:T(8,128)(2,1)S(1)} collective-permute-done((bf16[88,512]{1,0:T(8,128)(2,1)S(1)}, bf16[88,512]{1,0:T(8,128)(2,1)S(1)}, u32[]{:S(2)}, u32[]{:S(2)}) %collective-permute-start.11) | collective-permute-done | bytes 90144 | tf_op jit(solution)/shard_map/ppermute | solution.py:60
  54.8 1.7 %collective-permute-done.12.refs_3_ = bf16[88,512]{1,0:T(8,128)(2,1)S(1)} collective-permute-done((bf16[88,512]{1,0:T(8,128)(2,1)S(1)}, bf16[88,512]{1,0:T(8,128)(2,1)S(1)}, u32[]{:S(2)}, u32[]{:S(2)}) %collective-permute-start.12) | collective-permute-done | bytes 90144 | tf_op jit(solution)/shard_map/ppermute | solution.py:60
  56.5 0.5 head_terms.1
  56.9 2.1 %collective-permute-start.13 = (bf16[88,512]{1,0:T(8,128)(2,1)S(1)}, bf16[88,512]{1,0:T(8,128)(2,1)S(1)}, u32[]{:S(2)}, u32[]{:S(2)}) collective-permute-start(bf16[88,512]{1,0:T(8,128)(2,1)S(1)} %get-tuple-element.71.refs_0_), channel_id=1, source_target_pairs={{0,3},{1,2},{2,1},{3,0},{4,7},{5,6},{6,5},{7,4},{8,11},{9,10},{10,... | collective-permute-start | bytes 270344 | tf_op jit(solution)/shard_map/ppermute | solution.py:60
  59.0 0.9 %collective-permute-start.14 = (bf16[88,512]{1,0:T(8,128)(2,1)S(1)}, bf16[88,512]{1,0:T(8,128)(2,1)S(1)}, u32[]{:S(2)}, u32[]{:S(2)}) collective-permute-start(bf16[88,512]{1,0:T(8,128)(2,1)S(1)} %get-tuple-element.71.refs_0_), channel_id=1, source_target_pairs={{0,2},{1,3},{2,0},{3,1},{4,6},{5,7},{6,4},{7,5},{8,10},{9,11},{10,... | collective-permute-start | bytes 270344 | tf_op jit(solution)/shard_map/ppermute | solution.py:60
  60.0 0.5 collective-permute-start.15
  60.5 2.1 %latent_grad.1 = bf16[1,2048,512]{2,1,0:T(8,128)(2,1)} custom-call(bf16[88,512]{1,0:T(8,128)(2,1)S(1)} %get-tuple-element.40.head_ref, bf16[8,88,256]{2,1,0:T(8,128)(2,1)S(1)} %get-tuple-element.70.score_ref), custom_call_target="tpu_custom_call" | custom-call | flops 184549376 | bytes 3145728 | tf_op jit(solution)/shard_map/latent_grad/pallas_call | solution.py:523
  62.5 0.0 collective-permute-done.13.refs_1_
  62.5 1.0 %collective-permute-done.14.refs_2_ = bf16[88,512]{1,0:T(8,128)(2,1)S(1)} collective-permute-done((bf16[88,512]{1,0:T(8,128)(2,1)S(1)}, bf16[88,512]{1,0:T(8,128)(2,1)S(1)}, u32[]{:S(2)}, u32[]{:S(2)}) %collective-permute-start.14) | collective-permute-done | bytes 90144 | tf_op jit(solution)/shard_map/ppermute | solution.py:60
  63.6 0.9 %collective-permute-done.15.refs_3_ = bf16[88,512]{1,0:T(8,128)(2,1)S(1)} collective-permute-done((bf16[88,512]{1,0:T(8,128)(2,1)S(1)}, bf16[88,512]{1,0:T(8,128)(2,1)S(1)}, u32[]{:S(2)}, u32[]{:S(2)}) %collective-permute-start.15) | collective-permute-done | bytes 90144 | tf_op jit(solution)/shard_map/ppermute | solution.py:60
  64.5 0.8 %head_total.1 = f32[83,1,512]{2,1,0:T(1,128)} custom-call(bf16[88,512]{1,0:T(8,128)(2,1)S(1)} %get-tuple-element.71.refs_0_, bf16[88,512]{1,0:T(8,128)(2,1)S(1)} %collective-permute-done.13.refs_1_, bf16[88,512]{1,0:T(8,128)(2,1)S(1)} %collective-permute-done.14.refs_2_, bf16[88,512]{1,0:T(8,128)(2,1)S(1)} %collective-permute-done.15.refs_3_), custom_call_target="tpu_custom_call" | custom-call | flops 180224 | bytes 1048576 | tf_op jit(solution)/shard_map/head_total/pallas_call | solution.py:543
  (5 shorter events, 0.0 us)
Async XLA Ops:
  0.6 21.0 %copy-start = (bf16[2048,512]{1,0:T(8,128)(2,1)S(1)}, bf16[2048,512]{1,0:T(8,128)(2,1)}, u32[]{:S(2)}) copy-start(bf16[2048,512]{1,0:T(8,128)(2,1)} %base_ref.1) | copy-start | bytes 6291460
  2.2 1.8 %collective-permute-start = (bf16[384,512]{1,0:T(8,128)(2,1)S(1)}, bf16[384,512]{1,0:T(8,128)(2,1)S(1)}, u32[]{:S(2)}, u32[]{:S(2)}) collective-permute-start(bf16[384,512]{1,0:T(8,128)(2,1)S(1)} %get-tuple-element.44), channel_id=1, source_target_pairs={{0,4},{4,0},{8,12},{12,8},{16,20},{20,16},{24,28},{28,24},{1,5},{5... | collective-permute-start | bytes 1179656 | tf_op jit(solution)/shard_map/ppermute | solution.py:60
  4.1 20.6 %collective-permute-start.3 = (bf16[256,512]{1,0:T(8,128)(2,1)S(1)}, bf16[256,512]{1,0:T(8,128)(2,1)S(1)}, u32[]{:S(2)}, u32[]{:S(2)}) collective-permute-start(bf16[256,512]{1,0:T(8,128)(2,1)S(1)} %get-tuple-element.49), channel_id=1, source_target_pairs={{0,16},{4,20},{8,24},{12,28},{16,0},{20,4},{24,8},{28,12},{1,17},{... | collective-permute-start | bytes 786440 | tf_op jit(solution)/shard_map/ppermute | solution.py:60
  4.5 21.8 %collective-permute-start.4 = (bf16[256,512]{1,0:T(8,128)(2,1)S(1)}, bf16[256,512]{1,0:T(8,128)(2,1)S(1)}, u32[]{:S(2)}, u32[]{:S(2)}) collective-permute-start(bf16[256,512]{1,0:T(8,128)(2,1)S(1)} %get-tuple-element.51), channel_id=1, source_target_pairs={{0,24},{4,28},{8,16},{12,20},{16,8},{20,12},{24,0},{28,4},{1,25},{... | collective-permute-start | bytes 786440 | tf_op jit(solution)/shard_map/ppermute | solution.py:60
  6.9 12.7 %collective-permute-start.1 = (bf16[128,512]{1,0:T(8,128)(2,1)S(1)}, bf16[128,512]{1,0:T(8,128)(2,1)S(1)}, u32[]{:S(2)}, u32[]{:S(2)}) collective-permute-start(bf16[128,512]{1,0:T(8,128)(2,1)S(1)} %get-tuple-element.45), channel_id=1, source_target_pairs={{0,8},{4,12},{8,0},{12,4},{16,24},{20,28},{24,16},{28,20},{1,9},{5... | collective-permute-start | bytes 393224 | tf_op jit(solution)/shard_map/ppermute | solution.py:60
  7.6 14.0 %collective-permute-start.2 = (bf16[128,512]{1,0:T(8,128)(2,1)S(1)}, bf16[128,512]{1,0:T(8,128)(2,1)S(1)}, u32[]{:S(2)}, u32[]{:S(2)}) collective-permute-start(bf16[128,512]{1,0:T(8,128)(2,1)S(1)} %get-tuple-element.46), channel_id=1, source_target_pairs={{0,12},{4,8},{8,4},{12,0},{16,28},{20,24},{24,20},{28,16},{1,13},{... | collective-permute-start | bytes 393224 | tf_op jit(solution)/shard_map/ppermute | solution.py:60
  26.3 7.7 %copy-start.1 = (bf16[1024,512]{1,0:T(8,128)(2,1)S(1)}, bf16[1024,512]{1,0:T(8,128)(2,1)}, u32[]{:S(2)}) copy-start(bf16[1024,512]{1,0:T(8,128)(2,1)} %w_in_ref.3) | copy-start | bytes 3145732
  26.3 7.7 %copy-start.2 = (bf16[512,512]{1,0:T(8,128)(2,1)S(1)}, bf16[512,512]{1,0:T(8,128)(2,1)}, u32[]{:S(2)}) copy-start(bf16[512,512]{1,0:T(8,128)(2,1)} %w_out_ref.3) | copy-start | bytes 1572868
  26.3 7.6 %copy-start.3 = (f32[512]{0:T(512)S(1)}, f32[512]{0:T(512)}, u32[]{:S(2)}) copy-start(f32[512]{0:T(512)} %param.26) | copy-start | bytes 6148
  27.4 10.8 %collective-permute-start.5 = (bf16[128,512]{1,0:T(8,128)(2,1)S(1)}, bf16[128,512]{1,0:T(8,128)(2,1)S(1)}, u32[]{:S(2)}, u32[]{:S(2)}) collective-permute-start(bf16[128,512]{1,0:T(8,128)(2,1)S(1)} %get-tuple-element.55), channel_id=1, source_target_pairs={{0,4},{4,0},{8,12},{12,8},{16,20},{20,16},{24,28},{28,24},{1,5},{5... | collective-permute-start | bytes 393224 | tf_op jit(solution)/shard_map/ppermute | solution.py:60
  31.3 7.0 %collective-permute-start.6 = (bf16[128,512]{1,0:T(8,128)(2,1)S(1)}, bf16[128,512]{1,0:T(8,128)(2,1)S(1)}, u32[]{:S(2)}, u32[]{:S(2)}) collective-permute-start(bf16[128,512]{1,0:T(8,128)(2,1)S(1)} %get-tuple-element.56), channel_id=1, source_target_pairs={{4,8},{12,16},{20,24},{8,4},{16,12},{24,20},{5,9},{13,17},{21,25},... | collective-permute-start | bytes 393224 | tf_op jit(solution)/shard_map/ppermute | solution.py:594
  40.1 6.0 %collective-permute-start.7 = (bf16[88,512]{1,0:T(8,128)(2,1)S(1)}, bf16[88,512]{1,0:T(8,128)(2,1)S(1)}, u32[]{:S(2)}, u32[]{:S(2)}) collective-permute-start(bf16[88,512]{1,0:T(8,128)(2,1)S(1)} %get-tuple-element.63), channel_id=1, source_target_pairs={{0,3},{1,2},{2,1},{3,0},{4,7},{5,6},{6,5},{7,4},{8,11},{9,10},{10,... | collective-permute-start | bytes 270344 | tf_op jit(solution)/shard_map/ppermute | solution.py:60
  42.6 4.5 %collective-permute-start.8 = (bf16[88,512]{1,0:T(8,128)(2,1)S(1)}, bf16[88,512]{1,0:T(8,128)(2,1)S(1)}, u32[]{:S(2)}, u32[]{:S(2)}) collective-permute-start(bf16[88,512]{1,0:T(8,128)(2,1)S(1)} %get-tuple-element.64), channel_id=1, source_target_pairs={{0,2},{1,3},{2,0},{3,1},{4,6},{5,7},{6,4},{7,5},{8,10},{9,11},{10,... | collective-permute-start | bytes 270344 | tf_op jit(solution)/shard_map/ppermute | solution.py:60
  43.1 4.5 %collective-permute-start.9 = (bf16[88,512]{1,0:T(8,128)(2,1)S(1)}, bf16[88,512]{1,0:T(8,128)(2,1)S(1)}, u32[]{:S(2)}, u32[]{:S(2)}) collective-permute-start(bf16[88,512]{1,0:T(8,128)(2,1)S(1)} %get-tuple-element.65), channel_id=1, source_target_pairs={{0,1},{1,0},{2,3},{3,2},{4,5},{5,4},{6,7},{7,6},{8,9},{9,8},{10,11... | collective-permute-start | bytes 270344 | tf_op jit(solution)/shard_map/ppermute | solution.py:60
  48.3 5.5 %collective-permute-start.10 = (bf16[88,512]{1,0:T(8,128)(2,1)S(1)}, bf16[88,512]{1,0:T(8,128)(2,1)S(1)}, u32[]{:S(2)}, u32[]{:S(2)}) collective-permute-start(bf16[88,512]{1,0:T(8,128)(2,1)S(1)} %get-tuple-element.67), channel_id=1, source_target_pairs={{0,3},{1,2},{2,1},{3,0},{4,7},{5,6},{6,5},{7,4},{8,11},{9,10},{10,... | collective-permute-start | bytes 270344 | tf_op jit(solution)/shard_map/ppermute | solution.py:60
  49.9 4.9 %collective-permute-start.11 = (bf16[88,512]{1,0:T(8,128)(2,1)S(1)}, bf16[88,512]{1,0:T(8,128)(2,1)S(1)}, u32[]{:S(2)}, u32[]{:S(2)}) collective-permute-start(bf16[88,512]{1,0:T(8,128)(2,1)S(1)} %get-tuple-element.68), channel_id=1, source_target_pairs={{0,2},{1,3},{2,0},{3,1},{4,6},{5,7},{6,4},{7,5},{8,10},{9,11},{10,... | collective-permute-start | bytes 270344 | tf_op jit(solution)/shard_map/ppermute | solution.py:60
  50.5 6.0 %collective-permute-start.12 = (bf16[88,512]{1,0:T(8,128)(2,1)S(1)}, bf16[88,512]{1,0:T(8,128)(2,1)S(1)}, u32[]{:S(2)}, u32[]{:S(2)}) collective-permute-start(bf16[88,512]{1,0:T(8,128)(2,1)S(1)} %get-tuple-element.69), channel_id=1, source_target_pairs={{0,1},{1,0},{2,3},{3,2},{4,5},{5,4},{6,7},{7,6},{8,9},{9,8},{10,11... | collective-permute-start | bytes 270344 | tf_op jit(solution)/shard_map/ppermute | solution.py:60
  56.9 5.6 %collective-permute-start.13 = (bf16[88,512]{1,0:T(8,128)(2,1)S(1)}, bf16[88,512]{1,0:T(8,128)(2,1)S(1)}, u32[]{:S(2)}, u32[]{:S(2)}) collective-permute-start(bf16[88,512]{1,0:T(8,128)(2,1)S(1)} %get-tuple-element.71.refs_0_), channel_id=1, source_target_pairs={{0,3},{1,2},{2,1},{3,0},{4,7},{5,6},{6,5},{7,4},{8,11},{9,10},{10,... | collective-permute-start | bytes 270344 | tf_op jit(solution)/shard_map/ppermute | solution.py:60
  59.0 4.5 %collective-permute-start.14 = (bf16[88,512]{1,0:T(8,128)(2,1)S(1)}, bf16[88,512]{1,0:T(8,128)(2,1)S(1)}, u32[]{:S(2)}, u32[]{:S(2)}) collective-permute-start(bf16[88,512]{1,0:T(8,128)(2,1)S(1)} %get-tuple-element.71.refs_0_), channel_id=1, source_target_pairs={{0,2},{1,3},{2,0},{3,1},{4,6},{5,7},{6,4},{7,5},{8,10},{9,11},{10,... | collective-permute-start | bytes 270344 | tf_op jit(solution)/shard_map/ppermute | solution.py:60
  60.0 4.5 %collective-permute-start.15 = (bf16[88,512]{1,0:T(8,128)(2,1)S(1)}, bf16[88,512]{1,0:T(8,128)(2,1)S(1)}, u32[]{:S(2)}, u32[]{:S(2)}) collective-permute-start(bf16[88,512]{1,0:T(8,128)(2,1)S(1)} %get-tuple-element.71.refs_0_), channel_id=1, source_target_pairs={{0,1},{1,0},{2,3},{3,2},{4,5},{5,4},{6,7},{7,6},{8,9},{9,8},{10,11... | collective-permute-start | bytes 270344 | tf_op jit(solution)/shard_map/ppermute | solution.py:60

commit v8 on v7

--- a/solution.py
+++ b/solution.py
@@ -589,7 +589,7 @@
     )
     sums = add_part(first_rows, scale, fine_skip, [own, one, two, three], [slots] * 4, tile, "early")
     sums = add_part(mid_rows, scale, sums, far[:-1], [2 * slots] * (len(far) - 1), tile, "middle")
-    x, inner, outer = late(sums, last_rows, scale, far[-1:], tile)
+    x, inner, outer = late(sums, last_rows, scale, far[-1:], 2 * tile)
     pairs = [(i, i + 1) for i in range(1, dom_count - 1, 2)]
     outer = lax.ppermute(outer, "dom", pairs + [(j, i) for i, j in pairs])
     inner = xor_permute(inner, "dom", 1)
@@ -599,7 +599,7 @@
     preds = trade(preds)
     scores = trade(score(weight, inv_width, target, preds))
     term, by_tile = head_terms(members, mid, end, scores)
-    terms = trade([term] * members)
+    terms = mem_trade([0] + mem_steps(members)[1:2] + sorted(mem_steps(members)[2:]), [term] * members)
     grad_latent = latent_grad(head, by_tile)
     factor = 1.0 / math.sqrt(members * rows)
     return (grad_latent, head_total(terms, num_vars, factor).transpose(1, 2, 0))

time: 65.4 us -> 65.3 us (level)
  transfers between devices with their start and end apart: 16 -> 16, of which waited for: 12 -> 12; matrix products, arithmetic and copies ran while one was open for 0% -> 0% of each run, Pallas kernels for 28% -> 29%
where the time goes in v8:
time: 65.3 us; the launch traced here: 64.7 us
  Pallas kernels  25 us (38%)
  starting transfers between devices  21 us (32%)
  waiting for transfers between devices  17.2 us (26%)
  between operations  1.47 us (2%)
    ppermute x15, starting transfers between devices, xor_permute(): return lax.ppermute(value, axis, [(i, i ^ step) for i in range(count)])  18.4 us
    ppermute x15, waiting for transfers between devices, xor_permute(): return lax.ppermute(value, axis, [(i, i ^ step) for i in range(count)])  17.2 us
    pallas_call x1, Pallas kernels, spread(): pl.pallas_call(functools.partial(spread_kernel, tile, steps), out_shape=[...  7.23 us
    pallas_call x2, Pallas kernels, update_call(): pl.pallas_call(kernel, out_shape=out_shape, in_specs=[pl.BlockSpec(memory...  6.1 us
    pallas_call x2, Pallas kernels, add_part(): pl.pallas_call(functools.partial(part_kernel, tile, lengths), out_shape=j...  4.32 us
    ppermute x1, starting transfers between devices, shards(): outer = lax.ppermute(outer, 'dom', pairs + [(j, i) for i, j in pairs])  2.66 us
    pallas_call x1, Pallas kernels, latent_grad(): pl.pallas_call(latent_kernel, out_shape=jax.ShapeDtypeStruct((1, tiles *...  2.05 us
    pallas_call x1, Pallas kernels, first_pick(): pl.pallas_call(functools.partial(first_pick_kernel, steps), out_shape=[ja...  1.6 us
  transfers between devices with their start and end apart: 16, of which 12 were waited for; matrix products, arithmetic and copies ran while one was open for 0% of the time, Pallas kernels for 29%

profile of v8, /device:TPU:24, one launch (start us, length us, event | category | flops | bytes accessed | tf_op | source)
XLA Modules:
  0.0 64.7 jit_solution(11190385780100731026)
XLA Ops:
  0.6 1.6 %pick_first.1 = (bf16[384,512]{1,0:T(8,128)(2,1)S(1)}, s32[1,8,128]{2,1,0:T(8,128)S(1)}, bf16[1,512,512]{2,1,0:T(8,128)(2,1)S(1)}) custom-call(s32[1,8,128]{2,1,0:T(8,128)} %send_ref.1, bf16[1,512,512]{2,1,0:T(8,128)(2,1)} %coarse_ref.1), custom_call_target="tpu_custom_call" | custom-call | flops 1 | bytes 1 | tf_op jit(solution)/shard_map/pick_first/pallas_call | solution.py:104
  2.2 0.1 collective-permute-start
  2.3 0.6 %pick.1 = (bf16[128,512]{1,0:T(8,128)(2,1)S(1)}, bf16[128,512]{1,0:T(8,128)(2,1)S(1)}, bf16[128,512]{1,0:T(8,128)(2,1)S(1)}, bf16[128,512]{1,0:T(8,128)(2,1)S(1)}, bf16[128,512]{1,0:T(8,128)(2,1)S(1)}) custom-call(s32[1,8,128]{2,1,0:T(8,128)S(1)} %get-tuple-element.37.rows_ref, bf16[1,512,512]{2,1,0:T(8,128)(2,1)S(1)} %get-tuple-element.38.table_ref), custom_call_target="tpu_custom_call" | custom-call | flops 1 | bytes 1 | tf_op jit(solution)/shard_map/pick/pallas_call | solution.py:127
  3.0 1.1 %collective-permute-done.refs_1_.other_ref = bf16[384,512]{1,0:T(8,128)(2,1)S(1)} collective-permute-done((bf16[384,512]{1,0:T(8,128)(2,1)S(1)}, bf16[384,512]{1,0:T(8,128)(2,1)S(1)}, u32[]{:S(2)}, u32[]{:S(2)}) %collective-permute-start) | collective-permute-done | bytes 393248 | tf_op jit(solution)/shard_map/ppermute | solution.py:60
  4.1 0.4 collective-permute-start.3
  4.5 2.5 %collective-permute-start.4 = (bf16[256,512]{1,0:T(8,128)(2,1)S(1)}, bf16[256,512]{1,0:T(8,128)(2,1)S(1)}, u32[]{:S(2)}, u32[]{:S(2)}) collective-permute-start(bf16[256,512]{1,0:T(8,128)(2,1)S(1)} %get-tuple-element.51), channel_id=1, source_target_pairs={{0,24},{4,28},{8,16},{12,20},{16,8},{20,12},{24,0},{28,4},{1,25},{... | collective-permute-start | bytes 786440 | tf_op jit(solution)/shard_map/ppermute | solution.py:60
  6.9 0.7 %collective-permute-start.1 = (bf16[128,512]{1,0:T(8,128)(2,1)S(1)}, bf16[128,512]{1,0:T(8,128)(2,1)S(1)}, u32[]{:S(2)}, u32[]{:S(2)}) collective-permute-start(bf16[128,512]{1,0:T(8,128)(2,1)S(1)} %get-tuple-element.45), channel_id=1, source_target_pairs={{0,8},{4,12},{8,0},{12,4},{16,24},{20,28},{24,16},{28,20},{1,9},{5... | collective-permute-start | bytes 393224 | tf_op jit(solution)/shard_map/ppermute | solution.py:60
  7.6 0.2 collective-permute-start.2
  8.5 7.2 %spread.1 = (bf16[2048,1024]{1,0:T(8,128)(2,1)S(1)}, bf16[2048,512]{1,0:T(8,128)(2,1)S(1)}, bf16[2048,256]{1,0:T(8,128)(2,1)S(1)}, f32[1,2048]{1,0:T(1,128)S(1)}...) custom-call(s32[1]{0:T(128)S(6)} %copy.16.live_ref, ...), custom_call_target="tpu_custom_call" | custom-call | flops 1 | bytes 1 | tf_op jit(solution)/shard_map/spread/pallas_call | solution.py:240
  15.8 3.9 %collective-permute-done.1.refs_2_ = bf16[128,512]{1,0:T(8,128)(2,1)S(1)} collective-permute-done((bf16[128,512]{1,0:T(8,128)(2,1)S(1)}, bf16[128,512]{1,0:T(8,128)(2,1)S(1)}, u32[]{:S(2)}, u32[]{:S(2)}) %collective-permute-start.1) | collective-permute-done | bytes 131104 | tf_op jit(solution)/shard_map/ppermute | solution.py:60
  19.7 2.0 %collective-permute-done.2.refs_3_ = bf16[128,512]{1,0:T(8,128)(2,1)S(1)} collective-permute-done((bf16[128,512]{1,0:T(8,128)(2,1)S(1)}, bf16[128,512]{1,0:T(8,128)(2,1)S(1)}, u32[]{:S(2)}, u32[]{:S(2)}) %collective-permute-start.2) | collective-permute-done | bytes 131104 | tf_op jit(solution)/shard_map/ppermute | solution.py:60
  21.7 2.7 %early.1.base_ref = f32[2048,512]{1,0:T(8,128)S(1)} custom-call(bf16[2048,1024]{1,0:T(8,128)(2,1)S(1)} %get-tuple-element.43.spread_ref, f32[1,2048]{1,0:T(1,128)S(1)} %get-tuple-element.42.scale_ref, bf16[2048,512]{1,0:T(8,128)(2,1)S(1)} %copy-done, bf16[128,512]{1,0:T(8,128)(2,1)S(1)} %get-tuple-element.39.refs_7_.refs_0_, ...), custom_call_target="tpu_custom_call" | custom-call | flops 1 | bytes 1 | tf_op jit(solution)/shard_map/early/pallas_call | solution.py:303
  24.4 0.3 collective-permute-done.3.refs_0_
  24.6 1.6 %middle.1.sum_ref = f32[2048,512]{1,0:T(8,128)S(1)} custom-call(bf16[2048,512]{1,0:T(8,128)(2,1)S(1)} %get-tuple-element.41.spread_ref, f32[1,2048]{1,0:T(1,128)S(1)} %get-tuple-element.42.scale_ref, f32[2048,512]{1,0:T(8,128)S(1)} %early.1.base_ref, bf16[256,512]{1,0:T(8,128)(2,1)S(1)} %collective-permute-done.3.refs_0_), custom_call_target="tpu_custom_call" | custom-call | flops 1 | bytes 1 | tf_op jit(solution)/shard_map/middle/pallas_call | solution.py:303
  26.3 0.0 collective-permute-done.4.refs_0_
  26.3 0.0 copy-start.1
  26.3 0.0 copy-start.2
  26.3 0.0 copy-start.3
  26.3 1.1 %late.1 = (bf16[2048,512]{1,0:T(8,128)(2,1)S(1)}, bf16[128,512]{1,0:T(8,128)(2,1)S(1)}, bf16[128,512]{1,0:T(8,128)(2,1)S(1)}) custom-call(f32[2048,512]{1,0:T(8,128)S(1)} %middle.1.sum_ref, bf16[2048,256]{1,0:T(8,128)(2,1)S(1)} %get-tuple-element.50.spread_ref, f32[1,2048]{1,0:T(1,128)S(1)} %get-tuple-element.42.scale_ref, ...), custom_call_target="tpu_custom_call" | custom-call | flops 536870912 | bytes 8388608 | tf_op jit(solution)/shard_map/late/pallas_call | solution.py:337
  27.4 3.8 %collective-permute-start.5 = (bf16[128,512]{1,0:T(8,128)(2,1)S(1)}, bf16[128,512]{1,0:T(8,128)(2,1)S(1)}, u32[]{:S(2)}, u32[]{:S(2)}) collective-permute-start(bf16[128,512]{1,0:T(8,128)(2,1)S(1)} %get-tuple-element.55), channel_id=1, source_target_pairs={{0,4},{4,0},{8,12},{12,8},{16,20},{20,16},{24,28},{28,24},{1,5},{5... | collective-permute-start | bytes 393224 | tf_op jit(solution)/shard_map/ppermute | solution.py:60
  31.3 2.7 %collective-permute-start.6 = (bf16[128,512]{1,0:T(8,128)(2,1)S(1)}, bf16[128,512]{1,0:T(8,128)(2,1)S(1)}, u32[]{:S(2)}, u32[]{:S(2)}) collective-permute-start(bf16[128,512]{1,0:T(8,128)(2,1)S(1)} %get-tuple-element.56), channel_id=1, source_target_pairs={{4,8},{12,16},{20,24},{8,4},{16,12},{24,20},{5,9},{13,17},{21,25},... | collective-permute-start | bytes 393224 | tf_op jit(solution)/shard_map/ppermute | solution.py:594
  33.9 0.0 copy-done.1
  34.0 4.3 %inner.1 = (bf16[1536,512]{1,0:T(8,128)(2,1)S(1)}, bf16[6,88,256]{2,1,0:T(8,128)(2,1)S(1)}) custom-call(bf16[2048,512]{1,0:T(8,128)(2,1)S(1)} %get-tuple-element.52.x_ref, bf16[8,256,512]{2,1,0:T(8,128)(2,1)S(1)} %get-tuple-element.53.count_ref, bf16[1024,512]{1,0:T(8,128)(2,1)S(1)} %copy-done.1, bf16[512,512]{1,0:T(8,128)(2,1)S(1)} %copy-done.2, ...), custom_call_target="tpu_custom_call" | custom-call | flops 4026531840 | bytes 8388608 | tf_op jit(solution)/shard_map/inner/pallas_call | solution.py:409
  38.3 0.0 collective-permute-done.5.inner_ref
  38.3 0.0 collective-permute-done.6.outer_ref
  38.3 1.8 %outer.1 = (bf16[512,512]{1,0:T(8,128)(2,1)S(1)}, bf16[88,512]{1,0:T(8,128)(2,1)S(1)}, bf16[88,512]{1,0:T(8,128)(2,1)S(1)}, bf16[88,512]{1,0:T(8,128)(2,1)S(1)}, bf16[88,512]{1,0:T(8,128)(2,1)S(1)}) custom-call(bf16[2048,512]{1,0:T(8,128)(2,1)S(1)} %get-tuple-element.52.x_ref, bf16[8,256,512]{2,1,0:T(8,128)(2,1)S(1)} %get-tuple-element.53.count_ref, ...), custom_call_target="tpu_custom_call" | custom-call | flops 1342177280 | bytes 8388608 | tf_op jit(solution)/shard_map/outer/pallas_call | solution.py:409
  40.1 2.5 %collective-permute-start.7 = (bf16[88,512]{1,0:T(8,128)(2,1)S(1)}, bf16[88,512]{1,0:T(8,128)(2,1)S(1)}, u32[]{:S(2)}, u32[]{:S(2)}) collective-permute-start(bf16[88,512]{1,0:T(8,128)(2,1)S(1)} %get-tuple-element.63), channel_id=1, source_target_pairs={{0,3},{1,2},{2,1},{3,0},{4,7},{5,6},{6,5},{7,4},{8,11},{9,10},{10,... | collective-permute-start | bytes 270344 | tf_op jit(solution)/shard_map/ppermute | solution.py:60
  42.6 0.5 collective-permute-start.8
  43.1 0.5 collective-permute-start.9
  43.7 2.4 %collective-permute-done.7.refs_1_ = bf16[88,512]{1,0:T(8,128)(2,1)S(1)} collective-permute-done((bf16[88,512]{1,0:T(8,128)(2,1)S(1)}, bf16[88,512]{1,0:T(8,128)(2,1)S(1)}, u32[]{:S(2)}, u32[]{:S(2)}) %collective-permute-start.7) | collective-permute-done | bytes 90144 | tf_op jit(solution)/shard_map/ppermute | solution.py:60
  46.1 1.1 %collective-permute-done.8.refs_2_ = bf16[88,512]{1,0:T(8,128)(2,1)S(1)} collective-permute-done((bf16[88,512]{1,0:T(8,128)(2,1)S(1)}, bf16[88,512]{1,0:T(8,128)(2,1)S(1)}, u32[]{:S(2)}, u32[]{:S(2)}) %collective-permute-start.8) | collective-permute-done | bytes 90144 | tf_op jit(solution)/shard_map/ppermute | solution.py:60
  47.1 0.5 collective-permute-done.9.refs_3_
  47.6 0.7 %score.1 = (bf16[88,512]{1,0:T(8,128)(2,1)S(1)}, bf16[88,512]{1,0:T(8,128)(2,1)S(1)}, bf16[88,512]{1,0:T(8,128)(2,1)S(1)}, bf16[88,512]{1,0:T(8,128)(2,1)S(1)}) custom-call(f32[1,512]{1,0:T(1,128)S(1)} %get-tuple-element.59.weight_ref, f32[88,1]{1,0:T(8,128)S(1)} %get-tuple-element.60.inv_ref, f32[88,512]{1,0:T(8,128)S(1)} %get-tuple-element.61.target_ref, ...), custom_call_target="tpu_custom_call" | custom-call | flops 7208960 | bytes 1048576 | tf_op jit(solution)/shard_map/score/pallas_call | solution.py:470
  48.3 1.6 %collective-permute-start.10 = (bf16[88,512]{1,0:T(8,128)(2,1)S(1)}, bf16[88,512]{1,0:T(8,128)(2,1)S(1)}, u32[]{:S(2)}, u32[]{:S(2)}) collective-permute-start(bf16[88,512]{1,0:T(8,128)(2,1)S(1)} %get-tuple-element.67), channel_id=1, source_target_pairs={{0,3},{1,2},{2,1},{3,0},{4,7},{5,6},{6,5},{7,4},{8,11},{9,10},{10,... | collective-permute-start | bytes 270344 | tf_op jit(solution)/shard_map/ppermute | solution.py:60
  49.9 0.6 collective-permute-start.11
  50.5 1.4 %collective-permute-start.12 = (bf16[88,512]{1,0:T(8,128)(2,1)S(1)}, bf16[88,512]{1,0:T(8,128)(2,1)S(1)}, u32[]{:S(2)}, u32[]{:S(2)}) collective-permute-start(bf16[88,512]{1,0:T(8,128)(2,1)S(1)} %get-tuple-element.69), channel_id=1, source_target_pairs={{0,1},{1,0},{2,3},{3,2},{4,5},{5,4},{6,7},{7,6},{8,9},{9,8},{10,11... | collective-permute-start | bytes 270344 | tf_op jit(solution)/shard_map/ppermute | solution.py:60
  51.9 2.0 %collective-permute-done.10.refs_1_ = bf16[88,512]{1,0:T(8,128)(2,1)S(1)} collective-permute-done((bf16[88,512]{1,0:T(8,128)(2,1)S(1)}, bf16[88,512]{1,0:T(8,128)(2,1)S(1)}, u32[]{:S(2)}, u32[]{:S(2)}) %collective-permute-start.10) | collective-permute-done | bytes 90144 | tf_op jit(solution)/shard_map/ppermute | solution.py:60
  53.9 0.9 %collective-permute-done.11.refs_2_ = bf16[88,512]{1,0:T(8,128)(2,1)S(1)} collective-permute-done((bf16[88,512]{1,0:T(8,128)(2,1)S(1)}, bf16[88,512]{1,0:T(8,128)(2,1)S(1)}, u32[]{:S(2)}, u32[]{:S(2)}) %collective-permute-start.11) | collective-permute-done | bytes 90144 | tf_op jit(solution)/shard_map/ppermute | solution.py:60
  54.8 1.7 %collective-permute-done.12.refs_3_ = bf16[88,512]{1,0:T(8,128)(2,1)S(1)} collective-permute-done((bf16[88,512]{1,0:T(8,128)(2,1)S(1)}, bf16[88,512]{1,0:T(8,128)(2,1)S(1)}, u32[]{:S(2)}, u32[]{:S(2)}) %collective-permute-start.12) | collective-permute-done | bytes 90144 | tf_op jit(solution)/shard_map/ppermute | solution.py:60
  56.5 0.5 head_terms.1
  56.9 2.2 %collective-permute-start.13 = (bf16[88,512]{1,0:T(8,128)(2,1)S(1)}, bf16[88,512]{1,0:T(8,128)(2,1)S(1)}, u32[]{:S(2)}, u32[]{:S(2)}) collective-permute-start(bf16[88,512]{1,0:T(8,128)(2,1)S(1)} %get-tuple-element.71.refs_0_), channel_id=1, source_target_pairs={{0,3},{1,2},{2,1},{3,0},{4,7},{5,6},{6,5},{7,4},{8,11},{9,10},{10,... | collective-permute-start | bytes 270344 | tf_op jit(solution)/shard_map/ppermute | solution.py:60
  59.1 0.3 collective-permute-start.14
  59.4 1.1 %collective-permute-start.15 = (bf16[88,512]{1,0:T(8,128)(2,1)S(1)}, bf16[88,512]{1,0:T(8,128)(2,1)S(1)}, u32[]{:S(2)}, u32[]{:S(2)}) collective-permute-start(bf16[88,512]{1,0:T(8,128)(2,1)S(1)} %get-tuple-element.71.refs_0_), channel_id=1, source_target_pairs={{0,2},{1,3},{2,0},{3,1},{4,6},{5,7},{6,4},{7,5},{8,10},{9,11},{10,... | collective-permute-start | bytes 270344 | tf_op jit(solution)/shard_map/ppermute | solution.py:60
  60.5 2.1 %latent_grad.1 = bf16[1,2048,512]{2,1,0:T(8,128)(2,1)} custom-call(bf16[88,512]{1,0:T(8,128)(2,1)S(1)} %get-tuple-element.40.head_ref, bf16[8,88,256]{2,1,0:T(8,128)(2,1)S(1)} %get-tuple-element.70.score_ref), custom_call_target="tpu_custom_call" | custom-call | flops 184549376 | bytes 3145728 | tf_op jit(solution)/shard_map/latent_grad/pallas_call | solution.py:523
  62.5 0.0 collective-permute-done.13.refs_1_
  62.5 1.1 %collective-permute-done.14.refs_2_ = bf16[88,512]{1,0:T(8,128)(2,1)S(1)} collective-permute-done((bf16[88,512]{1,0:T(8,128)(2,1)S(1)}, bf16[88,512]{1,0:T(8,128)(2,1)S(1)}, u32[]{:S(2)}, u32[]{:S(2)}) %collective-permute-start.14) | collective-permute-done | bytes 90144 | tf_op jit(solution)/shard_map/ppermute | solution.py:60
  63.7 0.3 collective-permute-done.15.refs_3_
  63.9 0.8 %head_total.1 = f32[83,1,512]{2,1,0:T(1,128)} custom-call(bf16[88,512]{1,0:T(8,128)(2,1)S(1)} %get-tuple-element.71.refs_0_, bf16[88,512]{1,0:T(8,128)(2,1)S(1)} %collective-permute-done.13.refs_1_, bf16[88,512]{1,0:T(8,128)(2,1)S(1)} %collective-permute-done.14.refs_2_, bf16[88,512]{1,0:T(8,128)(2,1)S(1)} %collective-permute-done.15.refs_3_), custom_call_target="tpu_custom_call" | custom-call | flops 180224 | bytes 1048576 | tf_op jit(solution)/shard_map/head_total/pallas_call | solution.py:543
  (5 shorter events, 0.0 us)
Async XLA Ops:
  0.6 21.0 %copy-start = (bf16[2048,512]{1,0:T(8,128)(2,1)S(1)}, bf16[2048,512]{1,0:T(8,128)(2,1)}, u32[]{:S(2)}) copy-start(bf16[2048,512]{1,0:T(8,128)(2,1)} %base_ref.1) | copy-start | bytes 6291460
  2.2 1.8 %collective-permute-start = (bf16[384,512]{1,0:T(8,128)(2,1)S(1)}, bf16[384,512]{1,0:T(8,128)(2,1)S(1)}, u32[]{:S(2)}, u32[]{:S(2)}) collective-permute-start(bf16[384,512]{1,0:T(8,128)(2,1)S(1)} %get-tuple-element.44), channel_id=1, source_target_pairs={{0,4},{4,0},{8,12},{12,8},{16,20},{20,16},{24,28},{28,24},{1,5},{5... | collective-permute-start | bytes 1179656 | tf_op jit(solution)/shard_map/ppermute | solution.py:60
  4.1 20.6 %collective-permute-start.3 = (bf16[256,512]{1,0:T(8,128)(2,1)S(1)}, bf16[256,512]{1,0:T(8,128)(2,1)S(1)}, u32[]{:S(2)}, u32[]{:S(2)}) collective-permute-start(bf16[256,512]{1,0:T(8,128)(2,1)S(1)} %get-tuple-element.49), channel_id=1, source_target_pairs={{0,16},{4,20},{8,24},{12,28},{16,0},{20,4},{24,8},{28,12},{1,17},{... | collective-permute-start | bytes 786440 | tf_op jit(solution)/shard_map/ppermute | solution.py:60
  4.5 21.8 %collective-permute-start.4 = (bf16[256,512]{1,0:T(8,128)(2,1)S(1)}, bf16[256,512]{1,0:T(8,128)(2,1)S(1)}, u32[]{:S(2)}, u32[]{:S(2)}) collective-permute-start(bf16[256,512]{1,0:T(8,128)(2,1)S(1)} %get-tuple-element.51), channel_id=1, source_target_pairs={{0,24},{4,28},{8,16},{12,20},{16,8},{20,12},{24,0},{28,4},{1,25},{... | collective-permute-start | bytes 786440 | tf_op jit(solution)/shard_map/ppermute | solution.py:60
  6.9 12.7 %collective-permute-start.1 = (bf16[128,512]{1,0:T(8,128)(2,1)S(1)}, bf16[128,512]{1,0:T(8,128)(2,1)S(1)}, u32[]{:S(2)}, u32[]{:S(2)}) collective-permute-start(bf16[128,512]{1,0:T(8,128)(2,1)S(1)} %get-tuple-element.45), channel_id=1, source_target_pairs={{0,8},{4,12},{8,0},{12,4},{16,24},{20,28},{24,16},{28,20},{1,9},{5... | collective-permute-start | bytes 393224 | tf_op jit(solution)/shard_map/ppermute | solution.py:60
  7.6 14.0 %collective-permute-start.2 = (bf16[128,512]{1,0:T(8,128)(2,1)S(1)}, bf16[128,512]{1,0:T(8,128)(2,1)S(1)}, u32[]{:S(2)}, u32[]{:S(2)}) collective-permute-start(bf16[128,512]{1,0:T(8,128)(2,1)S(1)} %get-tuple-element.46), channel_id=1, source_target_pairs={{0,12},{4,8},{8,4},{12,0},{16,28},{20,24},{24,20},{28,16},{1,13},{... | collective-permute-start | bytes 393224 | tf_op jit(solution)/shard_map/ppermute | solution.py:60
  26.3 7.7 %copy-start.1 = (bf16[1024,512]{1,0:T(8,128)(2,1)S(1)}, bf16[1024,512]{1,0:T(8,128)(2,1)}, u32[]{:S(2)}) copy-start(bf16[1024,512]{1,0:T(8,128)(2,1)} %w_in_ref.3) | copy-start | bytes 3145732
  26.3 7.7 %copy-start.2 = (bf16[512,512]{1,0:T(8,128)(2,1)S(1)}, bf16[512,512]{1,0:T(8,128)(2,1)}, u32[]{:S(2)}) copy-start(bf16[512,512]{1,0:T(8,128)(2,1)} %w_out_ref.3) | copy-start | bytes 1572868
  26.3 7.6 %copy-start.3 = (f32[512]{0:T(512)S(1)}, f32[512]{0:T(512)}, u32[]{:S(2)}) copy-start(f32[512]{0:T(512)} %param.26) | copy-start | bytes 6148
  27.4 10.8 %collective-permute-start.5 = (bf16[128,512]{1,0:T(8,128)(2,1)S(1)}, bf16[128,512]{1,0:T(8,128)(2,1)S(1)}, u32[]{:S(2)}, u32[]{:S(2)}) collective-permute-start(bf16[128,512]{1,0:T(8,128)(2,1)S(1)} %get-tuple-element.55), channel_id=1, source_target_pairs={{0,4},{4,0},{8,12},{12,8},{16,20},{20,16},{24,28},{28,24},{1,5},{5... | collective-permute-start | bytes 393224 | tf_op jit(solution)/shard_map/ppermute | solution.py:60
  31.3 7.0 %collective-permute-start.6 = (bf16[128,512]{1,0:T(8,128)(2,1)S(1)}, bf16[128,512]{1,0:T(8,128)(2,1)S(1)}, u32[]{:S(2)}, u32[]{:S(2)}) collective-permute-start(bf16[128,512]{1,0:T(8,128)(2,1)S(1)} %get-tuple-element.56), channel_id=1, source_target_pairs={{4,8},{12,16},{20,24},{8,4},{16,12},{24,20},{5,9},{13,17},{21,25},... | collective-permute-start | bytes 393224 | tf_op jit(solution)/shard_map/ppermute | solution.py:594
  40.1 6.0 %collective-permute-start.7 = (bf16[88,512]{1,0:T(8,128)(2,1)S(1)}, bf16[88,512]{1,0:T(8,128)(2,1)S(1)}, u32[]{:S(2)}, u32[]{:S(2)}) collective-permute-start(bf16[88,512]{1,0:T(8,128)(2,1)S(1)} %get-tuple-element.63), channel_id=1, source_target_pairs={{0,3},{1,2},{2,1},{3,0},{4,7},{5,6},{6,5},{7,4},{8,11},{9,10},{10,... | collective-permute-start | bytes 270344 | tf_op jit(solution)/shard_map/ppermute | solution.py:60
  42.6 4.5 %collective-permute-start.8 = (bf16[88,512]{1,0:T(8,128)(2,1)S(1)}, bf16[88,512]{1,0:T(8,128)(2,1)S(1)}, u32[]{:S(2)}, u32[]{:S(2)}) collective-permute-start(bf16[88,512]{1,0:T(8,128)(2,1)S(1)} %get-tuple-element.64), channel_id=1, source_target_pairs={{0,2},{1,3},{2,0},{3,1},{4,6},{5,7},{6,4},{7,5},{8,10},{9,11},{10,... | collective-permute-start | bytes 270344 | tf_op jit(solution)/shard_map/ppermute | solution.py:60
  43.1 4.5 %collective-permute-start.9 = (bf16[88,512]{1,0:T(8,128)(2,1)S(1)}, bf16[88,512]{1,0:T(8,128)(2,1)S(1)}, u32[]{:S(2)}, u32[]{:S(2)}) collective-permute-start(bf16[88,512]{1,0:T(8,128)(2,1)S(1)} %get-tuple-element.65), channel_id=1, source_target_pairs={{0,1},{1,0},{2,3},{3,2},{4,5},{5,4},{6,7},{7,6},{8,9},{9,8},{10,11... | collective-permute-start | bytes 270344 | tf_op jit(solution)/shard_map/ppermute | solution.py:60
  48.3 5.5 %collective-permute-start.10 = (bf16[88,512]{1,0:T(8,128)(2,1)S(1)}, bf16[88,512]{1,0:T(8,128)(2,1)S(1)}, u32[]{:S(2)}, u32[]{:S(2)}) collective-permute-start(bf16[88,512]{1,0:T(8,128)(2,1)S(1)} %get-tuple-element.67), channel_id=1, source_target_pairs={{0,3},{1,2},{2,1},{3,0},{4,7},{5,6},{6,5},{7,4},{8,11},{9,10},{10,... | collective-permute-start | bytes 270344 | tf_op jit(solution)/shard_map/ppermute | solution.py:60
  49.9 4.9 %collective-permute-start.11 = (bf16[88,512]{1,0:T(8,128)(2,1)S(1)}, bf16[88,512]{1,0:T(8,128)(2,1)S(1)}, u32[]{:S(2)}, u32[]{:S(2)}) collective-permute-start(bf16[88,512]{1,0:T(8,128)(2,1)S(1)} %get-tuple-element.68), channel_id=1, source_target_pairs={{0,2},{1,3},{2,0},{3,1},{4,6},{5,7},{6,4},{7,5},{8,10},{9,11},{10,... | collective-permute-start | bytes 270344 | tf_op jit(solution)/shard_map/ppermute | solution.py:60
  50.5 6.0 %collective-permute-start.12 = (bf16[88,512]{1,0:T(8,128)(2,1)S(1)}, bf16[88,512]{1,0:T(8,128)(2,1)S(1)}, u32[]{:S(2)}, u32[]{:S(2)}) collective-permute-start(bf16[88,512]{1,0:T(8,128)(2,1)S(1)} %get-tuple-element.69), channel_id=1, source_target_pairs={{0,1},{1,0},{2,3},{3,2},{4,5},{5,4},{6,7},{7,6},{8,9},{9,8},{10,11... | collective-permute-start | bytes 270344 | tf_op jit(solution)/shard_map/ppermute | solution.py:60
  56.9 5.6 %collective-permute-start.13 = (bf16[88,512]{1,0:T(8,128)(2,1)S(1)}, bf16[88,512]{1,0:T(8,128)(2,1)S(1)}, u32[]{:S(2)}, u32[]{:S(2)}) collective-permute-start(bf16[88,512]{1,0:T(8,128)(2,1)S(1)} %get-tuple-element.71.refs_0_), channel_id=1, source_target_pairs={{0,3},{1,2},{2,1},{3,0},{4,7},{5,6},{6,5},{7,4},{8,11},{9,10},{10,... | collective-permute-start | bytes 270344 | tf_op jit(solution)/shard_map/ppermute | solution.py:60
  59.1 4.5 %collective-permute-start.14 = (bf16[88,512]{1,0:T(8,128)(2,1)S(1)}, bf16[88,512]{1,0:T(8,128)(2,1)S(1)}, u32[]{:S(2)}, u32[]{:S(2)}) collective-permute-start(bf16[88,512]{1,0:T(8,128)(2,1)S(1)} %get-tuple-element.71.refs_0_), channel_id=1, source_target_pairs={{0,1},{1,0},{2,3},{3,2},{4,5},{5,4},{6,7},{7,6},{8,9},{9,8},{10,11... | collective-permute-start | bytes 270344 | tf_op jit(solution)/shard_map/ppermute | solution.py:60
  59.4 4.5 %collective-permute-start.15 = (bf16[88,512]{1,0:T(8,128)(2,1)S(1)}, bf16[88,512]{1,0:T(8,128)(2,1)S(1)}, u32[]{:S(2)}, u32[]{:S(2)}) collective-permute-start(bf16[88,512]{1,0:T(8,128)(2,1)S(1)} %get-tuple-element.71.refs_0_), channel_id=1, source_target_pairs={{0,2},{1,3},{2,0},{3,1},{4,6},{5,7},{6,4},{7,5},{8,10},{9,11},{10,... | collective-permute-start | bytes 270344 | tf_op jit(solution)/shard_map/ppermute | solution.py:60
